TPU v7x, 512 devices: a whole 4x8x8 slice. The times are simulated.
512 devices in a mesh: prow: 32 (over x, z), pcol: 16 (over y, core).
Axes of the slice: x: 4, y: 8, z: 8, core: 2. Of those that a mesh axis runs over, the one named last changes fastest.
Arguments:
- factor: bfloat16 [32, 1, 16, 2, 512, 512], P('prow', None, 'pcol'), may hold values from -0.125 to 0.125
- rhs: float32 [32, 1, 512, 128], P('prow'), may hold values from -6 to 6
- upper_inverse: bfloat16 [32, 1, 512, 512], P('prow')
- lower_inverse: bfloat16 [32, 1, 512, 512], P('prow')
- parents: int32 [32], replicated, may hold values from 16 to 32, as said below
- block_mask: int32 [32, 32], replicated, may hold values 0 or 1
Outputs:
- solution: float32 [32, 1, 512, 128], P('prow')
Inputs may be any that keep to these rules, and one draw needn't show every extreme that they name: `parents`: the parent of a supernode of level l below the top is a supernode of level l + 1; supernodes of the top level have parent 32.
All inputs are finite; a program needn't handle non-finite values.
Results may differ from a plain program's by a relative error of at most 0.0003.
Values sent between devices are 32-bit elements; how exact they have to be, the bound alone decides.
No kernel may reach another device: no remote copies, remote signals or barrier semaphores. Data moves between devices by JAX's collectives and lax.ppermute only.
A program may use at most 64 MiB of HBM per device.

v0:
```python
import jax
import jax.numpy as jnp
from jax import lax
from jax.sharding import PartitionSpec as P

LEVELS = 4


def broadcast(array, axis, root):
    mine = lax.axis_index(axis) == root
    return lax.psum(jnp.where(mine, array, jnp.zeros_like(array)), axis)


def level_ranges(count_blocks):
    spans = []
    for depth_step in range(LEVELS - 1):
        spans.append(
            (
                count_blocks - count_blocks // 2**depth_step,
                count_blocks - count_blocks // 2 ** (depth_step + 1),
            )
        )
    spans.append((count_blocks - count_blocks // 2 ** (LEVELS - 1), count_blocks))
    return spans


def patterns(parents, block_mask):
    count_blocks = parents.shape[0]
    positions = jnp.arange(count_blocks, dtype=jnp.int32)
    step_matrix = (parents[:, None] == positions[None, :]).astype(jnp.float32)
    identity = jnp.eye(count_blocks, dtype=jnp.float32)
    power_now = identity
    ancestry = identity
    for depth_step in range(LEVELS - 1):
        power_now = jnp.dot(power_now, step_matrix, precision=lax.Precision.HIGHEST)
        ancestry = ancestry + power_now
    ancestry = jnp.minimum(ancestry, 1.0)
    weights = block_mask.astype(jnp.float32) * (1.0 - identity)
    return (weights * ancestry, weights * ancestry.T)


def apply_inverse(inverse, residual):
    return jnp.einsum(
        "rbc,rcn->rbn", inverse.astype(jnp.float32), residual, precision=lax.Precision.HIGHEST
    )


def slot_term(blocks, solved, local_use, slot_q):
    scaled = solved * local_use[:, slot_q][:, None, None]
    return jnp.einsum(
        "rab,ran->bn",
        blocks[:, slot_q].astype(jnp.float32),
        scaled,
        precision=lax.Precision.HIGHEST,
    )


def sweep(blocks, base, inverse, local_use, order, row_ids, pcol_count, root_column):
    cols_local = blocks.shape[1]
    solved = jnp.zeros(base.shape, jnp.float32)
    first_level = True
    for lower_end, upper_end in order:
        member = (row_ids >= lower_end) & (row_ids < upper_end)
        if first_level:
            updated = apply_inverse(inverse, base)
        else:
            column_slots = [
                slot_q
                for slot_q in range(cols_local)
                if slot_q * pcol_count < upper_end and slot_q * pcol_count + pcol_count > lower_end
            ]
            partial_terms = []
            for slot_q in column_slots:
                partial_terms.append(slot_term(blocks, solved, local_use, slot_q))
            summed = lax.psum(jnp.stack(partial_terms, 0), "prow")
            chosen_slot = jnp.clip(
                row_ids // pcol_count - column_slots[0], 0, len(column_slots) - 1
            )
            picked = jnp.take(summed, chosen_slot, axis=0)
            residual = base - picked
            updated = broadcast(apply_inverse(inverse, residual), "pcol", root_column)
        solved = jnp.where(member[:, None, None], updated, solved)
        first_level = False
    return solved


def per_device(factor, rhs, upper_inverse, lower_inverse, parents, block_mask):
    prow_count = lax.axis_size("prow")
    pcol_count = lax.axis_size("pcol")
    blocks = factor[0, :, 0]
    rows_local = blocks.shape[0]
    cols_local = blocks.shape[1]
    count_blocks = rows_local * prow_count
    prow_at = lax.axis_index("prow")
    pcol_at = lax.axis_index("pcol")
    row_ids = jnp.arange(rows_local, dtype=jnp.int32) * prow_count + prow_at
    col_ids = jnp.arange(cols_local, dtype=jnp.int32) * pcol_count + pcol_at
    positions = jnp.arange(count_blocks, dtype=jnp.int32)
    pick_rows = (row_ids[:, None] == positions[None, :]).astype(jnp.float32)
    pick_cols = (col_ids[:, None] == positions[None, :]).astype(jnp.float32)
    upper_use, lower_use = patterns(parents, block_mask)
    local_upper = jnp.dot(
        jnp.dot(pick_rows, upper_use, precision=lax.Precision.HIGHEST),
        pick_cols.T,
        precision=lax.Precision.HIGHEST,
    )
    local_lower = jnp.dot(
        jnp.dot(pick_rows, lower_use, precision=lax.Precision.HIGHEST),
        pick_cols.T,
        precision=lax.Precision.HIGHEST,
    )
    root_column = prow_at % pcol_count
    spans = level_ranges(count_blocks)
    forward = sweep(
        blocks, rhs[0], upper_inverse[0], local_upper, spans, row_ids, pcol_count, root_column
    )
    backward = sweep(
        blocks,
        forward,
        lower_inverse[0],
        local_lower,
        spans[::-1],
        row_ids,
        pcol_count,
        root_column,
    )
    return backward[None]


def solution(mesh):
    placed = (
        P("prow", None, "pcol", None, None, None),
        P("prow", None, None, None),
        P("prow", None, None, None),
        P("prow", None, None, None),
        P(),
        P(),
    )
    return jax.shard_map(
        per_device,
        mesh=mesh,
        in_specs=placed,
        out_specs=P("prow", None, None, None),
        check_vma=False,
    )
```

profile of v0, /device:TPU:1, one launch (start us, length us, event | category | flops | bytes accessed | tf_op | source)
XLA Modules:
  0.0 1659.1 jit_solution(25474923758621422)
XLA Ops:
  6.6 0.7 copy-done.6
  8.1 0.8 copy.7
  9.1 0.7 fusion.80
  9.8 0.6 convolution_select_fusion.7
  10.4 2.0 convolution_bitcast_fusion.5
  12.5 156.6 %all-reduce.13.cloned.1.call-done = f32[1,512,128]{2,1,0:T(8,128)} async-done(((f32[1,512,128]{2,1,0:T(8,128)}), f32[1,512,128]{2,1,0:T(8,128)}) %all-reduce.13.cloned.1.call-update) | async-done | bytes 262160 | tf_op jit(solution)/shard_map/psum | solution.py:75
  169.2 2.3 fusion.5
  171.5 114.9 %all-reduce.15.cloned.1.call-done = f32[1,512,128]{2,1,0:T(8,128)} async-done(((f32[1,512,128]{2,1,0:T(8,128)}), f32[1,512,128]{2,1,0:T(8,128)}) %all-reduce.15.cloned.1.call-update) | async-done | bytes 262160 | tf_op jit(solution)/shard_map/psum | solution.py:11
  286.4 2.0 convolution_bitcast_fusion.4
  288.5 153.7 %all-reduce.17.cloned.1.call-done = f32[1,512,128]{2,1,0:T(8,128)} async-done(((f32[1,512,128]{2,1,0:T(8,128)}), f32[1,512,128]{2,1,0:T(8,128)}) %all-reduce.17.cloned.1.call-update) | async-done | bytes 262160 | tf_op jit(solution)/shard_map/psum | solution.py:75
  442.2 2.3 fusion.4
  444.5 114.9 %all-reduce.19.cloned.1.call-done = f32[1,512,128]{2,1,0:T(8,128)} async-done(((f32[1,512,128]{2,1,0:T(8,128)}), f32[1,512,128]{2,1,0:T(8,128)}) %all-reduce.19.cloned.1.call-update) | async-done | bytes 262160 | tf_op jit(solution)/shard_map/psum | solution.py:11
  559.4 2.0 convolution_bitcast_fusion.3
  561.6 153.0 %all-reduce.21.cloned.1.call-done = f32[1,512,128]{2,1,0:T(8,128)} async-done(((f32[1,512,128]{2,1,0:T(8,128)}), f32[1,512,128]{2,1,0:T(8,128)}) %all-reduce.21.cloned.1.call-update) | async-done | bytes 262160 | tf_op jit(solution)/shard_map/psum | solution.py:75
  714.6 2.3 fusion.3
  717.1 0.7 fusion.96
  717.8 114.1 %all-reduce.23.cloned.1.call-done = f32[1,512,128]{2,1,0:T(8,128)} async-done(((f32[1,512,128]{2,1,0:T(8,128)}), f32[1,512,128]{2,1,0:T(8,128)}) %all-reduce.23.cloned.1.call-update) | async-done | bytes 262160 | tf_op jit(solution)/shard_map/psum | solution.py:11
  831.9 1.0 copy-done.2
  832.9 0.6 convolution_select_fusion.3
  833.5 2.1 convolution_bitcast_fusion.2
  835.7 152.0 %all-reduce.25.cloned.1.call-done = f32[1,512,128]{2,1,0:T(8,128)} async-done(((f32[1,512,128]{2,1,0:T(8,128)}), f32[1,512,128]{2,1,0:T(8,128)}) %all-reduce.25.cloned.1.call-update) | async-done | bytes 262160 | tf_op jit(solution)/shard_map/psum | solution.py:75
  987.7 2.3 fusion.2
  990.0 114.9 %all-reduce.27.cloned.1.call-done = f32[1,512,128]{2,1,0:T(8,128)} async-done(((f32[1,512,128]{2,1,0:T(8,128)}), f32[1,512,128]{2,1,0:T(8,128)}) %all-reduce.27.cloned.1.call-update) | async-done | bytes 262160 | tf_op jit(solution)/shard_map/psum | solution.py:11
  1105.0 2.1 convolution_bitcast_fusion.1
  1107.1 153.2 %all-reduce.29.cloned.1.call-done = f32[1,512,128]{2,1,0:T(8,128)} async-done(((f32[1,512,128]{2,1,0:T(8,128)}), f32[1,512,128]{2,1,0:T(8,128)}) %all-reduce.29.cloned.1.call-update) | async-done | bytes 262160 | tf_op jit(solution)/shard_map/psum | solution.py:75
  1260.3 2.3 fusion.1
  1262.7 114.9 %all-reduce.31.cloned.1.call-done = f32[1,512,128]{2,1,0:T(8,128)} async-done(((f32[1,512,128]{2,1,0:T(8,128)}), f32[1,512,128]{2,1,0:T(8,128)}) %all-reduce.31.cloned.1.call-update) | async-done | bytes 262160 | tf_op jit(solution)/shard_map/psum | solution.py:11
  1377.6 2.0 convolution_bitcast_fusion
  1379.7 153.7 %all-reduce.33.cloned.1.call-done = f32[1,512,128]{2,1,0:T(8,128)} async-done(((f32[1,512,128]{2,1,0:T(8,128)}), f32[1,512,128]{2,1,0:T(8,128)}) %all-reduce.33.cloned.1.call-update) | async-done | bytes 262160 | tf_op jit(solution)/shard_map/psum | solution.py:75
  1533.4 2.3 fusion
  1535.7 114.9 %all-reduce.35.cloned.1.call-done = f32[1,512,128]{2,1,0:T(8,128)} async-done(((f32[1,512,128]{2,1,0:T(8,128)}), f32[1,512,128]{2,1,0:T(8,128)}) %all-reduce.35.cloned.1.call-update) | async-done | bytes 262160 | tf_op jit(solution)/shard_map/psum | solution.py:11
  1650.6 1.7 select_bitcast_fusion
  (50 shorter events, 2.1 us)
Async XLA Ops:
  6.5 3.2 copy-start
  6.5 0.7 copy-start.6
  6.5 3.2 copy-start.3
  6.5 3.8 copy-start.1
  6.5 162.6 %all-reduce.13.cloned.1.call-start = ((), (), s32[]{:S(2)}) async-start(), calls=%async_computation | async-start | bytes 524288 | tf_op jit(solution)/shard_map/psum | solution.py:75
  12.5 273.9 %all-reduce.15.cloned.1.call-start = ((), (), s32[]{:S(2)}) async-start(), calls=%async_computation.1 | async-start | bytes 524288 | tf_op jit(solution)/shard_map/psum | solution.py:11
  171.4 270.7 %all-reduce.17.cloned.1.call-start = ((), (), s32[]{:S(2)}) async-start(), calls=%async_computation.2 | async-start | bytes 524288 | tf_op jit(solution)/shard_map/psum | solution.py:75
  288.5 270.9 %all-reduce.19.cloned.1.call-start = ((), (), s32[]{:S(2)}) async-start(), calls=%async_computation.3 | async-start | bytes 524288 | tf_op jit(solution)/shard_map/psum | solution.py:11
  444.5 270.2 %all-reduce.21.cloned.1.call-start = ((), (), s32[]{:S(2)}) async-start(), calls=%async_computation.4 | async-start | bytes 524288 | tf_op jit(solution)/shard_map/psum | solution.py:75
  561.5 270.4 %all-reduce.23.cloned.1.call-start = ((), (), s32[]{:S(2)}) async-start(), calls=%async_computation.5 | async-start | bytes 524288 | tf_op jit(solution)/shard_map/psum | solution.py:11
  716.9 115.0 %copy-start.4 = (f32[1,512,128]{2,1,0:T(8,128)S(1)}, f32[1,512,128]{2,1,0:T(8,128)}, u32[]{:S(2)}) copy-start(f32[1,512,128]{2,1,0:T(8,128)} %all-reduce.19.cloned.1.call-done) | copy-start | bytes 786436
  716.9 270.8 %all-reduce.25.cloned.1.call-start = ((), (), s32[]{:S(2)}) async-start(), calls=%async_computation.6 | async-start | bytes 524288 | tf_op jit(solution)/shard_map/psum | solution.py:75
  831.9 1.0 copy-start.2
  835.6 269.3 %all-reduce.27.cloned.1.call-start = ((), (), s32[]{:S(2)}) async-start(), calls=%async_computation.7 | async-start | bytes 524288 | tf_op jit(solution)/shard_map/psum | solution.py:11
  990.0 270.3 %all-reduce.29.cloned.1.call-start = ((), (), s32[]{:S(2)}) async-start(), calls=%async_computation.8 | async-start | bytes 524288 | tf_op jit(solution)/shard_map/psum | solution.py:75
  1107.1 270.5 %all-reduce.31.cloned.1.call-start = ((), (), s32[]{:S(2)}) async-start(), calls=%async_computation.9 | async-start | bytes 524288 | tf_op jit(solution)/shard_map/psum | solution.py:11
  1262.6 270.7 %all-reduce.33.cloned.1.call-start = ((), (), s32[]{:S(2)}) async-start(), calls=%async_computation.10 | async-start | bytes 524288 | tf_op jit(solution)/shard_map/psum | solution.py:75
  1379.6 271.0 %all-reduce.35.cloned.1.call-start = ((), (), s32[]{:S(2)}) async-start(), calls=%async_computation.11 | async-start | bytes 524288 | tf_op jit(solution)/shard_map/psum | solution.py:11
  1535.6 115.0 %copy-start.5 = (f32[1,512,128]{2,1,0:T(8,128)S(1)}, f32[1,512,128]{2,1,0:T(8,128)}, u32[]{:S(2)}) copy-start(f32[1,512,128]{2,1,0:T(8,128)} %all-reduce.31.cloned.1.call-done) | copy-start | bytes 786436
Sparse Core Ops, SparseCore 0:
  12.6 156.5 all-reduce.12
  171.6 114.7 all-reduce.14
  290.2 151.9 all-reduce.16
  444.6 114.7 all-reduce.18
  562.7 151.8 all-reduce.20
  717.1 114.7 all-reduce.22
  835.7 151.9 all-reduce.24
  990.1 114.7 all-reduce.26
  1108.4 151.8 all-reduce.28
  1262.7 114.7 all-reduce.30
  1381.4 151.9 all-reduce.32
  1535.8 114.7 all-reduce.34
where the time goes:
time: 1660 us
  waiting for transfers between devices  1610 us (97%)
  matrix products  28.8 us (2%)
    psum x6, waiting for transfers between devices, sweep(): summed = lax.psum(jnp.stack(partial_terms, 0), 'prow')  922 us
    psum x6, waiting for transfers between devices, broadcast(): return lax.psum(jnp.where(mine, array, jnp.zeros_like(array)), axis)  689 us
  transfers between devices with their start and end apart: 12, of which 12 were waited for; matrix products, arithmetic and copies ran while one was open for 0% of the time, Pallas kernels for 0%

commit v1 on v0

v1 whole, which is shorter than its diff:
```python
import jax
import jax.numpy as jnp
from jax import lax
from jax.sharding import Mesh, PartitionSpec as P

LEVELS = 4
HALF = ("xl", "z")
ROW = ("xh", "xl", "z")
COL = ("y", "core")


def patterns(parents, block_mask):
    count = parents.shape[0]
    positions = jnp.arange(count, dtype=jnp.int32)
    step = (parents[:, None] == positions[None, :]).astype(jnp.float32)
    identity = jnp.eye(count, dtype=jnp.float32)
    power = identity
    ancestry = identity
    for _ in range(LEVELS - 1):
        power = jnp.dot(power, step, precision=lax.Precision.HIGHEST)
        ancestry = ancestry + power
    ancestry = jnp.minimum(ancestry, 1.0)
    weights = block_mask.astype(jnp.float32) * (1.0 - identity)
    return weights * ancestry, weights * ancestry.T


def mm(matrix, panel):
    return jnp.dot(
        matrix.astype(jnp.float32), panel, precision=lax.Precision.HIGHEST
    )


def weighted(weights, received):
    return jnp.sum(weights[:, None, None] * received, axis=0)


def a2a(array, axes):
    return lax.all_to_all(array, axes, 0, 0, tiled=True)


def spread(piece, ny):
    rows, cols = piece.shape
    copies = jnp.broadcast_to(piece[None], (ny, rows, cols))
    half = a2a(copies, "y").reshape(ny * rows, cols)
    return lax.all_gather(half, "core", tiled=True)


def per_device(factor, rhs, upper_inverse, lower_inverse, parents, block_mask):
    ny, nc, nz = lax.axis_size("y"), lax.axis_size("core"), lax.axis_size("z")
    ncol = ny * nc
    slot0 = factor[0, 0, 0, 0]
    slot1 = factor[0, 0, 0, 1]
    base = rhs[0, 0]
    up = upper_inverse[0, 0]
    low = lower_inverse[0, 0]
    width, nrhs = base.shape
    piece = width // ncol
    count = parents.shape[0]
    top = count // 2
    row = lax.axis_index(ROW)
    col = lax.axis_index(COL)
    high = (lax.axis_index("xh") == 1).astype(jnp.float32)
    last = high * (lax.axis_index("xl") == 1).astype(jnp.float32)
    upper_use, lower_use = patterns(parents, block_mask)
    to_me_u = lax.dynamic_index_in_dim(upper_use, row, 1, keepdims=False)
    to_me_l = lax.dynamic_index_in_dim(lower_use, row, 1, keepdims=False)
    to_col_l = lax.dynamic_index_in_dim(lower_use, col, 1, keepdims=False)
    mine_u = lax.dynamic_index_in_dim(upper_use, row, 0, keepdims=False)
    mine_l = lax.dynamic_index_in_dim(lower_use, row, 0, keepdims=False)
    mine = (mine_u + mine_l)[top:]

    sent = slot1.T.astype(jnp.float32).reshape(nc, ny, piece, width)
    sent = jnp.transpose(sent, (1, 0, 2, 3)).reshape(ncol, piece, width)
    slices = a2a(sent, COL)
    slices = (slices * mine[:, None, None]).astype(jnp.bfloat16).reshape(width, width)

    def updates(panel):
        return mm(slices, panel).reshape(top, piece, nrhs)

    y = mm(up, base)
    out = updates(y)
    got = a2a(jnp.concatenate([jnp.zeros_like(out), out], 0), ROW)
    w = jnp.where(jnp.arange(count) < top, to_me_u, 0.0)
    part = weighted(w, got)
    y = mm(up, base - spread(part, ny))
    got = a2a(updates(y), HALF)
    w = jnp.where(jnp.arange(top) < top // 2, to_me_u[top:], 0.0) * high
    part = part + weighted(w, got)
    y = mm(up, base - spread(part, ny))
    got = a2a(updates(y)[top // 2:], "z")
    w = jnp.where(jnp.arange(nz) < nz // 2, to_me_u[top + top // 2:], 0.0) * last
    part = part + weighted(w, got)
    y = mm(up, base - spread(part, ny))
    x = mm(low, y)
    got = a2a(updates(x)[top // 2:], "z")
    w = to_me_l[top + top // 2:] * last
    x = mm(low, y - spread(weighted(w, got), ny))
    got = a2a(updates(x), HALF)
    w = to_me_l[top:] * high
    known = spread(weighted(w, got), ny)
    x = mm(low, y - known)
    full = lax.dot_general(
        slot0.astype(jnp.float32), x, (((0,), (0,)), ((), ())), precision=lax.Precision.HIGHEST
    )
    small = width // count
    got = a2a(full.reshape(count, small, nrhs), ROW)
    part = weighted(to_col_l, got)
    copies = lax.all_gather(part[None], "core", tiled=True)
    copies = jnp.broadcast_to(copies[None], (ny,) + copies.shape)
    every = a2a(copies, "y").reshape(ncol, small, nrhs)
    got = a2a(jnp.concatenate([every, jnp.zeros_like(every)], 0), ROW).reshape(width, nrhs)
    x = mm(low, y - known - got)
    return x[None, None]


def solution(mesh):
    grid = Mesh(mesh.devices.reshape(2, 2, 8, 8, 2), ("xh", "xl", "z", "y", "core"))
    placed = (
        P(ROW, None, COL, None, None, None),
        P(ROW, None, None, None),
        P(ROW, None, None, None),
        P(ROW, None, None, None),
        P(),
        P(),
    )
    return jax.shard_map(
        per_device,
        mesh=grid,
        in_specs=placed,
        out_specs=P(ROW, None, None, None),
        check_vma=False,
    )
```

time: 1660 us -> 257 us (0.15)
  waiting for transfers between devices: 1610 us -> 84.1 us
  blocking collectives: 0 us -> 109 us
  starting transfers between devices: 0.49 us -> 40.2 us
    psum x12 -> x0, waiting for transfers between devices: 1610 us -> none  [the longest x6 922 us: sweep(): summed = lax.psum(jnp.stack(partial_terms, 0), 'prow')]
    all_to_all x0 -> x7, waiting for transfers between devices: none -> 84.1 us  [a2a(): return lax.all_to_all(array, axes, 0, 0, tiled=True)]
    all_to_all x0 -> x7, blocking collectives: none -> 81.2 us  [a2a(): return lax.all_to_all(array, axes, 0, 0, tiled=True)]
    all_to_all x0 -> x7, starting transfers between devices: none -> 40.2 us  [a2a(): return lax.all_to_all(array, axes, 0, 0, tiled=True)]
    all_gather x0 -> x6, blocking collectives: none -> 28.3 us  [the longest x5 23.1 us: spread(): return lax.all_gather(half, 'core', tiled=True)]
    dot_general x21 -> x16, matrix products: 28.8 us -> 11 us  [the longest x12 10 us: mm(): jnp.dot(matrix.astype(jnp.float32), panel, precision=lax.Precision.HIGHEST)]
  transfers between devices with their start and end apart: 12 -> 7, of which waited for: 12 -> 7; matrix products, arithmetic and copies ran while one was open for 0% -> 1% of each run, Pallas kernels for 0% -> 0%
where the time goes in v1:
time: 257 us; the launch traced here: 254 us
  blocking collectives  109 us (42%)
  waiting for transfers between devices  84.1 us (33%)
  starting transfers between devices  40.2 us (16%)
  matrix products  12.8 us (5%)
  local copies, waits for them, and re-layouts  5.79 us (2%)
    all_to_all x7, waiting for transfers between devices, a2a(): return lax.all_to_all(array, axes, 0, 0, tiled=True)  84.1 us
    all_to_all x7, blocking collectives, a2a(): return lax.all_to_all(array, axes, 0, 0, tiled=True)  81.2 us
    all_to_all x7, starting transfers between devices, a2a(): return lax.all_to_all(array, axes, 0, 0, tiled=True)  40.2 us
    all_gather x5, blocking collectives, spread(): return lax.all_gather(half, 'core', tiled=True)  23.1 us
    dot_general x12, matrix products, mm(): jnp.dot(matrix.astype(jnp.float32), panel, precision=lax.Precision.HIGHEST)  10 us
    all_gather x1, blocking collectives, per_device(): copies = lax.all_gather(part[None], 'core', tiled=True)  5.19 us
  transfers between devices with their start and end apart: 7, of which 7 were waited for; matrix products, arithmetic and copies ran while one was open for 1% of the time, Pallas kernels for 0%

profile of v1, /device:TPU:1, one launch (start us, length us, event | category | flops | bytes accessed | tf_op | source)
XLA Modules:
  0.0 253.9 jit_solution(4898234920565710402)
XLA Ops:
  0.0 1.2 slice-done
  1.5 1.1 copy.28
  2.6 10.5 %all-to-all-start = ((f32[16,32,512]{2,1,0:T(8,128)}), f32[16,32,512]{2,1,0:T(8,128)S(1)}, u32[]{:S(2)}, u32[]{:S(2)}) async-start(f32[16,32,512]{2,1,0:T(8,128)} %bitcast.6), calls=%async_computation | async-start | bytes 2097152 | tf_op jit(solution)/shard_map/all_to_all | solution.py:38
  15.5 25.6 %all-to-all-done = f32[16,32,512]{2,1,0:T(8,128)S(1)} async-done(((f32[16,32,512]{2,1,0:T(8,128)}), f32[16,32,512]{2,1,0:T(8,128)S(1)}, u32[]{:S(2)}, u32[]{:S(2)}) %all-to-all-start) | async-done | bytes 1048608 | tf_op jit(solution)/shard_map/all_to_all | solution.py:38
  41.2 1.8 fusion.39
  43.0 11.1 %all-to-all-start.1 = ((f32[32,32,128]{2,1,0:T(8,128)}), f32[32,32,128]{2,1,0:T(8,128)S(1)}, u32[]{:S(2)}, u32[]{:S(2)}) async-start(f32[32,32,128]{2,1,0:T(8,128)} %fusion.39), calls=%async_computation.1 | async-start | bytes 1048576 | tf_op jit(solution)/shard_map/all_to_all | solution.py:38
  54.1 16.5 %all-to-all-done.1 = f32[32,32,128]{2,1,0:T(8,128)S(1)} async-done(((f32[32,32,128]{2,1,0:T(8,128)}), f32[32,32,128]{2,1,0:T(8,128)S(1)}, u32[]{:S(2)}, u32[]{:S(2)}) %all-to-all-start.1) | async-done | bytes 524320 | tf_op jit(solution)/shard_map/all_to_all | solution.py:38
  70.8 10.3 %all_to_all.70 = f32[8,32,128]{2,1,0:T(8,128)S(1)} all-to-all(f32[8,32,128]{2,1,0:T(8,128)S(1)} %broadcast_in_dim.30), channel_id=1, replica_groups=mesh['xh'=2,'xl'=2,'z'=8,'y'=8,'core'=2] {'y'}, dimensions={0} | all-to-all | bytes 262144 | tf_op jit(solution)/shard_map/all_to_all | solution.py:38
  81.1 4.4 %all_gather.18 = f32[512,128]{1,0:T(8,128)S(1)} all-gather(f32[256,128]{1,0:T(8,128)S(1)} %bitcast.115), channel_id=1, replica_groups=mesh['xh'=2,'xl'=2,'z'=8,'y'=8,'core'=2] {'core'}, dimensions={0}, use_global_device_ids=true | all-gather | bytes 393216 | tf_op jit(solution)/shard_map/all_gather | solution.py:45
  86.2 1.3 fusion.37
  87.6 4.4 %all-to-all-start.3 = ((f32[16,32,128]{2,1,0:T(8,128)}), f32[16,32,128]{2,1,0:T(8,128)S(1)}, u32[]{:S(2)}, u32[]{:S(2)}) async-start(f32[16,32,128]{2,1,0:T(8,128)} %fusion.37), calls=%async_computation.3 | async-start | bytes 524288 | tf_op jit(solution)/shard_map/all_to_all | solution.py:38
  92.1 8.9 %all-to-all-done.3 = f32[16,32,128]{2,1,0:T(8,128)S(1)} async-done(((f32[16,32,128]{2,1,0:T(8,128)}), f32[16,32,128]{2,1,0:T(8,128)S(1)}, u32[]{:S(2)}, u32[]{:S(2)}) %all-to-all-start.3) | async-done | bytes 262176 | tf_op jit(solution)/shard_map/all_to_all | solution.py:38
  101.1 10.4 %all_to_all.71 = f32[8,32,128]{2,1,0:T(8,128)S(1)} all-to-all(f32[8,32,128]{2,1,0:T(8,128)S(1)} %broadcast_in_dim.32), channel_id=1, replica_groups=mesh['xh'=2,'xl'=2,'z'=8,'y'=8,'core'=2] {'y'}, dimensions={0} | all-to-all | bytes 262144 | tf_op jit(solution)/shard_map/all_to_all | solution.py:38
  111.5 4.8 %all_gather.19 = f32[512,128]{1,0:T(8,128)S(1)} all-gather(f32[256,128]{1,0:T(8,128)S(1)} %bitcast.116), channel_id=1, replica_groups=mesh['xh'=2,'xl'=2,'z'=8,'y'=8,'core'=2] {'core'}, dimensions={0}, use_global_device_ids=true | all-gather | bytes 393216 | tf_op jit(solution)/shard_map/all_gather | solution.py:45
  118.1 3.9 %all-to-all-start.5 = ((f32[8,32,128]{2,1,0:T(8,128)}), f32[8,32,128]{2,1,0:T(8,128)S(1)}, u32[]{:S(2)}, u32[]{:S(2)}) async-start(f32[8,32,128]{2,1,0:T(8,128)} %bitcast.18), calls=%async_computation.5 | async-start | bytes 262144 | tf_op jit(solution)/shard_map/all_to_all | solution.py:38
  122.0 7.8 %all-to-all-done.5 = f32[8,32,128]{2,1,0:T(8,128)S(1)} async-done(((f32[8,32,128]{2,1,0:T(8,128)}), f32[8,32,128]{2,1,0:T(8,128)S(1)}, u32[]{:S(2)}, u32[]{:S(2)}) %all-to-all-start.5) | async-done | bytes 131104 | tf_op jit(solution)/shard_map/all_to_all | solution.py:38
  130.6 3.4 %all-to-all-start.6 = ((f32[8,32,128]{2,1,0:T(8,128)}), f32[8,32,128]{2,1,0:T(8,128)S(1)}, u32[]{:S(2)}, u32[]{:S(2)}) async-start(f32[8,32,128]{2,1,0:T(8,128)} %broadcast_in_dim.33), calls=%async_computation.6 | async-start | bytes 262144 | tf_op jit(solution)/shard_map/all_to_all | solution.py:38
  134.0 7.9 %all-to-all-done.6 = f32[8,32,128]{2,1,0:T(8,128)S(1)} async-done(((f32[8,32,128]{2,1,0:T(8,128)}), f32[8,32,128]{2,1,0:T(8,128)S(1)}, u32[]{:S(2)}, u32[]{:S(2)}) %all-to-all-start.6) | async-done | bytes 131104 | tf_op jit(solution)/shard_map/all_to_all | solution.py:38
  142.0 4.8 %all_gather.20 = f32[512,128]{1,0:T(8,128)S(1)} all-gather(f32[256,128]{1,0:T(8,128)S(1)} %bitcast.114), channel_id=1, replica_groups=mesh['xh'=2,'xl'=2,'z'=8,'y'=8,'core'=2] {'core'}, dimensions={0}, use_global_device_ids=true | all-gather | bytes 393216 | tf_op jit(solution)/shard_map/all_gather | solution.py:45
  149.5 3.4 %all-to-all-start.7 = ((f32[8,32,128]{2,1,0:T(8,128)}), f32[8,32,128]{2,1,0:T(8,128)S(1)}, u32[]{:S(2)}, u32[]{:S(2)}) async-start(f32[8,32,128]{2,1,0:T(8,128)} %bitcast.24), calls=%async_computation.7 | async-start | bytes 262144 | tf_op jit(solution)/shard_map/all_to_all | solution.py:38
  153.0 8.2 %all-to-all-done.7 = f32[8,32,128]{2,1,0:T(8,128)S(1)} async-done(((f32[8,32,128]{2,1,0:T(8,128)}), f32[8,32,128]{2,1,0:T(8,128)S(1)}, u32[]{:S(2)}, u32[]{:S(2)}) %all-to-all-start.7) | async-done | bytes 131104 | tf_op jit(solution)/shard_map/all_to_all | solution.py:38
  161.3 10.3 %all_to_all.72 = f32[8,32,128]{2,1,0:T(8,128)S(1)} all-to-all(f32[8,32,128]{2,1,0:T(8,128)S(1)} %broadcast_in_dim.34), channel_id=1, replica_groups=mesh['xh'=2,'xl'=2,'z'=8,'y'=8,'core'=2] {'y'}, dimensions={0} | all-to-all | bytes 262144 | tf_op jit(solution)/shard_map/all_to_all | solution.py:38
  171.7 4.4 %all_gather.21 = f32[512,128]{0,1:T(8,128)S(1)} all-gather(f32[256,128]{0,1:T(8,128)S(1)} %copy.29), channel_id=1, replica_groups=mesh['xh'=2,'xl'=2,'z'=8,'y'=8,'core'=2] {'core'}, dimensions={0}, use_global_device_ids=true | all-gather | bytes 393216 | tf_op jit(solution)/shard_map/all_gather | solution.py:45
  176.8 1.3 fusion.38
  178.1 3.5 %all-to-all-start.9 = ((f32[16,32,128]{2,1,0:T(8,128)}), f32[16,32,128]{2,1,0:T(8,128)S(1)}, u32[]{:S(2)}, u32[]{:S(2)}) async-start(f32[16,32,128]{2,1,0:T(8,128)} %fusion.38), calls=%async_computation.9 | async-start | bytes 524288 | tf_op jit(solution)/shard_map/all_to_all | solution.py:38
  181.7 9.1 %all-to-all-done.9 = f32[16,32,128]{2,1,0:T(8,128)S(1)} async-done(((f32[16,32,128]{2,1,0:T(8,128)}), f32[16,32,128]{2,1,0:T(8,128)S(1)}, u32[]{:S(2)}, u32[]{:S(2)}) %all-to-all-start.9) | async-done | bytes 262176 | tf_op jit(solution)/shard_map/all_to_all | solution.py:38
  190.9 10.3 %all_to_all.73 = f32[8,32,128]{2,1,0:T(8,128)S(1)} all-to-all(f32[8,32,128]{2,1,0:T(8,128)S(1)} %broadcast_in_dim.35), channel_id=1, replica_groups=mesh['xh'=2,'xl'=2,'z'=8,'y'=8,'core'=2] {'y'}, dimensions={0} | all-to-all | bytes 262144 | tf_op jit(solution)/shard_map/all_to_all | solution.py:38
  201.3 4.7 %all_gather.22 = f32[512,128]{0,1:T(8,128)S(1)} all-gather(f32[256,128]{0,1:T(8,128)S(1)} %copy.30), channel_id=1, replica_groups=mesh['xh'=2,'xl'=2,'z'=8,'y'=8,'core'=2] {'core'}, dimensions={0}, use_global_device_ids=true | all-gather | bytes 393216 | tf_op jit(solution)/shard_map/all_gather | solution.py:45
  207.2 15.3 %all_to_all.74 = f32[32,16,128]{2,1,0:T(8,128)S(1)} all-to-all(f32[32,16,128]{2,1,0:T(8,128)S(1)} %bitcast.112), channel_id=1, replica_groups=mesh['xh'=2,'xl'=2,'z'=8,'y'=8,'core'=2] {'xh','xl','z'}, dimensions={0} | all-to-all | bytes 524288 | tf_op jit(solution)/shard_map/all_to_all | solution.py:38
  222.6 5.2 %all-gather = f32[32,128]{1,0:T(8,128)S(1)} all-gather(f32[16,128]{1,0:T(8,128)S(1)} %multiply_reduce_fusion.1), channel_id=2, replica_groups=mesh['xh'=2,'xl'=2,'z'=8,'y'=8,'core'=2] {'core'}, dimensions={0}, use_global_device_ids=true | all-gather | bytes 24576 | tf_op jit(solution)/shard_map/all_gather | solution.py:108
  227.8 10.9 %all_to_all.75 = f32[8,2,16,128]{3,2,1,0:T(8,128)S(1)} all-to-all(f32[8,2,16,128]{3,2,1,0:T(8,128)S(1)} %broadcast_in_dim.37), channel_id=1, replica_groups=mesh['xh'=2,'xl'=2,'z'=8,'y'=8,'core'=2] {'y'}, dimensions={0} | all-to-all | bytes 262144 | tf_op jit(solution)/shard_map/all_to_all | solution.py:38
  238.7 13.6 %all_to_all.76 = f32[32,16,128]{2,1,0:T(8,128)S(1)} all-to-all(f32[32,16,128]{2,1,0:T(8,128)S(1)} %concatenate.7), channel_id=1, replica_groups=mesh['xh'=2,'xl'=2,'z'=8,'y'=8,'core'=2] {'xh','xl','z'}, dimensions={0} | all-to-all | bytes 524288 | tf_op jit(solution)/shard_map/all_to_all | solution.py:38
  (62 shorter events, 13.2 us)
Async XLA Ops:
  0.0 14.9 %copy-start = (bf16[1,1,512,512]{3,2,1,0:T(8,128)(2,1)S(1)}, bf16[1,1,512,512]{3,2,1,0:T(8,128)(2,1)}, u32[]{:S(2)}) copy-start(bf16[1,1,512,512]{3,2,1,0:T(8,128)(2,1)} %param.8) | copy-start | bytes 1572868
  0.0 1.2 slice-start
  2.6 10.5 %copy-start.5 = (s32[32]{0:T(128)S(1)}, s32[32]{0:T(128)}, u32[]{:S(2)}) copy-start(s32[32]{0:T(128)} %param.10) | copy-start | bytes 388
  2.6 38.4 %all-to-all-start = ((f32[16,32,512]{2,1,0:T(8,128)}), f32[16,32,512]{2,1,0:T(8,128)S(1)}, u32[]{:S(2)}, u32[]{:S(2)}) async-start(f32[16,32,512]{2,1,0:T(8,128)} %bitcast.6), calls=%async_computation | async-start | bytes 2097152 | tf_op jit(solution)/shard_map/all_to_all | solution.py:38
  13.1 1.8 copy-start.2
  13.8 0.7 copy-start.4
  43.0 27.7 %all-to-all-start.1 = ((f32[32,32,128]{2,1,0:T(8,128)}), f32[32,32,128]{2,1,0:T(8,128)S(1)}, u32[]{:S(2)}, u32[]{:S(2)}) async-start(f32[32,32,128]{2,1,0:T(8,128)} %fusion.39), calls=%async_computation.1 | async-start | bytes 1048576 | tf_op jit(solution)/shard_map/all_to_all | solution.py:38
  87.6 13.4 %all-to-all-start.3 = ((f32[16,32,128]{2,1,0:T(8,128)}), f32[16,32,128]{2,1,0:T(8,128)S(1)}, u32[]{:S(2)}, u32[]{:S(2)}) async-start(f32[16,32,128]{2,1,0:T(8,128)} %fusion.37), calls=%async_computation.3 | async-start | bytes 524288 | tf_op jit(solution)/shard_map/all_to_all | solution.py:38
  118.1 11.8 %all-to-all-start.5 = ((f32[8,32,128]{2,1,0:T(8,128)}), f32[8,32,128]{2,1,0:T(8,128)S(1)}, u32[]{:S(2)}, u32[]{:S(2)}) async-start(f32[8,32,128]{2,1,0:T(8,128)} %bitcast.18), calls=%async_computation.5 | async-start | bytes 262144 | tf_op jit(solution)/shard_map/all_to_all | solution.py:38
  130.6 11.3 %all-to-all-start.6 = ((f32[8,32,128]{2,1,0:T(8,128)}), f32[8,32,128]{2,1,0:T(8,128)S(1)}, u32[]{:S(2)}, u32[]{:S(2)}) async-start(f32[8,32,128]{2,1,0:T(8,128)} %broadcast_in_dim.33), calls=%async_computation.6 | async-start | bytes 262144 | tf_op jit(solution)/shard_map/all_to_all | solution.py:38
  146.8 1.0 copy-start.1
  149.5 11.7 %all-to-all-start.7 = ((f32[8,32,128]{2,1,0:T(8,128)}), f32[8,32,128]{2,1,0:T(8,128)S(1)}, u32[]{:S(2)}, u32[]{:S(2)}) async-start(f32[8,32,128]{2,1,0:T(8,128)} %bitcast.24), calls=%async_computation.7 | async-start | bytes 262144 | tf_op jit(solution)/shard_map/all_to_all | solution.py:38
  178.1 12.7 %all-to-all-start.9 = ((f32[16,32,128]{2,1,0:T(8,128)}), f32[16,32,128]{2,1,0:T(8,128)S(1)}, u32[]{:S(2)}, u32[]{:S(2)}) async-start(f32[16,32,128]{2,1,0:T(8,128)} %fusion.38), calls=%async_computation.9 | async-start | bytes 524288 | tf_op jit(solution)/shard_map/all_to_all | solution.py:38
  201.2 5.4 %copy-start.3 = (bf16[1,1,1,2,512,512]{5,4,3,2,1,0:T(8,128)(2,1)S(1)}, bf16[1,1,1,2,512,512]{5,4,3,2,1,0:T(8,128)(2,1)}, u32[]{:S(2)}) copy-start(bf16[1,1,1,2,512,512]{5,4,3,2,1,0:T(8,128)(2,1)} %param.6) | copy-start | bytes 3145732

commit v2 on v1

--- a/solution.py
+++ b/solution.py
@@ -64,33 +64,44 @@
     upper_use, lower_use = patterns(parents, block_mask)
     to_me_u = lax.dynamic_index_in_dim(upper_use, row, 1, keepdims=False)
     to_me_l = lax.dynamic_index_in_dim(lower_use, row, 1, keepdims=False)
-    to_col_l = lax.dynamic_index_in_dim(lower_use, col, 1, keepdims=False)
+    to_col_u = lax.dynamic_index_in_dim(upper_use, top + col, 1, keepdims=False)
     mine_u = lax.dynamic_index_in_dim(upper_use, row, 0, keepdims=False)
     mine_l = lax.dynamic_index_in_dim(lower_use, row, 0, keepdims=False)
     mine = (mine_u + mine_l)[top:]
 
-    sent = slot1.T.astype(jnp.float32).reshape(nc, ny, piece, width)
-    sent = jnp.transpose(sent, (1, 0, 2, 3)).reshape(ncol, piece, width)
-    slices = a2a(sent, COL)
-    slices = (slices * mine[:, None, None]).astype(jnp.bfloat16).reshape(width, width)
+    def resliced(block, use):
+        sent = block.T.astype(jnp.float32).reshape(nc, ny, piece, width)
+        sent = jnp.transpose(sent, (1, 0, 2, 3)).reshape(ncol, piece, width)
+        got = a2a(sent, COL) * use[:, None, None]
+        return got.astype(jnp.bfloat16).reshape(width, width)
+
+    slices = resliced(slot1, (mine_u + mine_l)[top:])
+    slices0 = resliced(slot0, mine_l[:top])
 
     def updates(panel):
         return mm(slices, panel).reshape(top, piece, nrhs)
 
     y = mm(up, base)
-    out = updates(y)
-    got = a2a(jnp.concatenate([jnp.zeros_like(out), out], 0), ROW)
-    w = jnp.where(jnp.arange(count) < top, to_me_u, 0.0)
+    full = lax.dot_general(
+        slot1.astype(jnp.float32), y, (((0,), (0,)), ((), ())), precision=lax.Precision.HIGHEST
+    )
+    small = width // count
+    got = a2a(full.reshape(count, small, nrhs), ROW)
+    w = jnp.where(jnp.arange(count) < top, to_col_u, 0.0)
     part = weighted(w, got)
-    y = mm(up, base - spread(part, ny))
+    copies = lax.all_gather(part[None], "core", tiled=True)
+    copies = jnp.broadcast_to(copies[None], (ny,) + copies.shape)
+    every = a2a(copies, "y").reshape(ncol, small, nrhs)
+    known = a2a(jnp.concatenate([jnp.zeros_like(every), every], 0), ROW).reshape(width, nrhs)
+    y = mm(up, base - known)
     got = a2a(updates(y), HALF)
     w = jnp.where(jnp.arange(top) < top // 2, to_me_u[top:], 0.0) * high
-    part = part + weighted(w, got)
-    y = mm(up, base - spread(part, ny))
+    part = weighted(w, got)
+    y = mm(up, base - known - spread(part, ny))
     got = a2a(updates(y)[top // 2:], "z")
     w = jnp.where(jnp.arange(nz) < nz // 2, to_me_u[top + top // 2:], 0.0) * last
     part = part + weighted(w, got)
-    y = mm(up, base - spread(part, ny))
+    y = mm(up, base - known - spread(part, ny))
     x = mm(low, y)
     got = a2a(updates(x)[top // 2:], "z")
     w = to_me_l[top + top // 2:] * last
@@ -99,17 +110,10 @@
     w = to_me_l[top:] * high
     known = spread(weighted(w, got), ny)
     x = mm(low, y - known)
-    full = lax.dot_general(
-        slot0.astype(jnp.float32), x, (((0,), (0,)), ((), ())), precision=lax.Precision.HIGHEST
-    )
-    small = width // count
-    got = a2a(full.reshape(count, small, nrhs), ROW)
-    part = weighted(to_col_l, got)
-    copies = lax.all_gather(part[None], "core", tiled=True)
-    copies = jnp.broadcast_to(copies[None], (ny,) + copies.shape)
-    every = a2a(copies, "y").reshape(ncol, small, nrhs)
-    got = a2a(jnp.concatenate([every, jnp.zeros_like(every)], 0), ROW).reshape(width, nrhs)
-    x = mm(low, y - known - got)
+    out = mm(slices0, x).reshape(top, piece, nrhs)
+    got = a2a(jnp.concatenate([out, jnp.zeros_like(out)], 0), ROW)
+    rest = spread(weighted(to_me_l, got) * (1.0 - high), ny)
+    x = mm(low, y - known - rest)
     return x[None, None]
 
 

time: 257 us -> 289 us (1.12)
  waiting for transfers between devices: 84.1 us -> 133 us
  blocking collectives: 109 us -> 70.5 us
  starting transfers between devices: 40.2 us -> 58.5 us
  local copies, waits for them, and re-layouts: 5.79 us -> 10.7 us
    all_to_all x7 -> x11, waiting for transfers between devices: 84.1 us -> 133 us  [a2a(): return lax.all_to_all(array, axes, 0, 0, tiled=True)]
    all_to_all x7 -> x4, blocking collectives: 81.2 us -> 45.6 us  [a2a(): return lax.all_to_all(array, axes, 0, 0, tiled=True)]
    all_to_all x7 -> x11, starting transfers between devices: 40.2 us -> 58.5 us  [a2a(): return lax.all_to_all(array, axes, 0, 0, tiled=True)]
    all_gather x5, blocking collectives: 23.1 us -> 19.6 us  [spread(): return lax.all_gather(half, 'core', tiled=True)]
    dot_general x12 -> x13, matrix products: 10 us -> 11.5 us  [mm(): jnp.dot(matrix.astype(jnp.float32), panel, precision=lax.Precision.HIGHEST)]
  transfers between devices with their start and end apart: 7 -> 11, of which waited for: 7 -> 11; matrix products, arithmetic and copies ran while one was open for 1% -> 2% of each run, Pallas kernels for 0% -> 0%
where the time goes in v2:
time: 289 us; the launch traced here: 287 us
  waiting for transfers between devices  133 us (46%)
  blocking collectives  70.5 us (24%)
  starting transfers between devices  58.5 us (20%)
  matrix products  12.8 us (4%)
  local copies, waits for them, and re-layouts  10.7 us (4%)
    all_to_all x11, waiting for transfers between devices, a2a(): return lax.all_to_all(array, axes, 0, 0, tiled=True)  133 us
    all_to_all x11, starting transfers between devices, a2a(): return lax.all_to_all(array, axes, 0, 0, tiled=True)  58.5 us
    all_to_all x4, blocking collectives, a2a(): return lax.all_to_all(array, axes, 0, 0, tiled=True)  45.6 us
    all_gather x5, blocking collectives, spread(): return lax.all_gather(half, 'core', tiled=True)  19.6 us
    dot_general x13, matrix products, mm(): jnp.dot(matrix.astype(jnp.float32), panel, precision=lax.Precision.HIGHEST)  11.5 us
  transfers between devices with their start and end apart: 11, of which 11 were waited for; matrix products, arithmetic and copies ran while one was open for 2% of the time, Pallas kernels for 0%

profile of v2, /device:TPU:1, one launch (start us, length us, event | category | flops | bytes accessed | tf_op | source)
XLA Modules:
  0.0 287.2 jit_solution(18119243703465430428)
XLA Ops:
  3.9 13.8 %all-to-all-start = ((f32[32,16,128]{2,1,0:T(8,128)}), f32[32,16,128]{2,1,0:T(8,128)S(1)}, u32[]{:S(2)}, u32[]{:S(2)}) async-start(f32[32,16,128]{2,1,0:T(8,128)} %bitcast.4), calls=%async_computation | async-start | bytes 524288 | tf_op jit(solution)/shard_map/all_to_all | solution.py:38
  19.7 7.7 %all-to-all-done = f32[32,16,128]{2,1,0:T(8,128)S(1)} async-done(((f32[32,16,128]{2,1,0:T(8,128)}), f32[32,16,128]{2,1,0:T(8,128)S(1)}, u32[]{:S(2)}, u32[]{:S(2)}) %all-to-all-start) | async-done | bytes 262176 | tf_op jit(solution)/shard_map/all_to_all | solution.py:38
  27.6 5.2 %all-gather = f32[32,128]{1,0:T(8,128)S(1)} all-gather(f32[16,128]{1,0:T(8,128)S(1)} %multiply_reduce_fusion.3), channel_id=2, replica_groups=mesh['xh'=2,'xl'=2,'z'=8,'y'=8,'core'=2] {'core'}, dimensions={0}, use_global_device_ids=true | all-gather | bytes 24576 | tf_op jit(solution)/shard_map/all_gather | solution.py:92
  32.8 14.6 %all_to_all.75 = f32[8,2,16,128]{3,2,1,0:T(8,128)S(1)} all-to-all(f32[8,2,16,128]{3,2,1,0:T(8,128)S(1)} %broadcast_in_dim.30), channel_id=1, replica_groups=mesh['xh'=2,'xl'=2,'z'=8,'y'=8,'core'=2] {'y'}, dimensions={0} | all-to-all | bytes 262144 | tf_op jit(solution)/shard_map/all_to_all | solution.py:38
  48.1 4.1 %all-to-all-start.2 = ((f32[32,16,128]{2,1,0:T(8,128)}), f32[32,16,128]{2,1,0:T(8,128)S(1)}, u32[]{:S(2)}, u32[]{:S(2)}) async-start(f32[32,16,128]{2,1,0:T(8,128)} %concatenate.6), calls=%async_computation.2 | async-start | bytes 524288 | tf_op jit(solution)/shard_map/all_to_all | solution.py:38
  53.7 8.1 %all-to-all-done.2 = f32[32,16,128]{2,1,0:T(8,128)S(1)} async-done(((f32[32,16,128]{2,1,0:T(8,128)}), f32[32,16,128]{2,1,0:T(8,128)S(1)}, u32[]{:S(2)}, u32[]{:S(2)}) %all-to-all-start.2) | async-done | bytes 262176 | tf_op jit(solution)/shard_map/all_to_all | solution.py:38
  61.9 7.6 %all-to-all-start.3 = ((f32[16,32,512]{2,1,0:T(8,128)}), f32[16,32,512]{2,1,0:T(8,128)S(1)}, u32[]{:S(2)}, u32[]{:S(2)}) async-start(f32[16,32,512]{2,1,0:T(8,128)} %bitcast.11), calls=%async_computation.3 | async-start | bytes 2097152 | tf_op jit(solution)/shard_map/all_to_all | solution.py:38
  70.3 27.2 %all-to-all-done.3 = f32[16,32,512]{2,1,0:T(8,128)S(1)} async-done(((f32[16,32,512]{2,1,0:T(8,128)}), f32[16,32,512]{2,1,0:T(8,128)S(1)}, u32[]{:S(2)}, u32[]{:S(2)}) %all-to-all-start.3) | async-done | bytes 1048608 | tf_op jit(solution)/shard_map/all_to_all | solution.py:38
  98.9 3.5 %all-to-all-start.4 = ((f32[16,32,128]{2,1,0:T(8,128)}), f32[16,32,128]{2,1,0:T(8,128)S(1)}, u32[]{:S(2)}, u32[]{:S(2)}) async-start(f32[16,32,128]{2,1,0:T(8,128)} %fusion.45), calls=%async_computation.4 | async-start | bytes 524288 | tf_op jit(solution)/shard_map/all_to_all | solution.py:38
  102.6 9.3 %all-to-all-done.4 = f32[16,32,128]{2,1,0:T(8,128)S(1)} async-done(((f32[16,32,128]{2,1,0:T(8,128)}), f32[16,32,128]{2,1,0:T(8,128)S(1)}, u32[]{:S(2)}, u32[]{:S(2)}) %all-to-all-start.4) | async-done | bytes 262176 | tf_op jit(solution)/shard_map/all_to_all | solution.py:38
  112.7 3.4 %all-to-all-start.5 = ((f32[8,32,128]{2,1,0:T(8,128)}), f32[8,32,128]{2,1,0:T(8,128)S(1)}, u32[]{:S(2)}, u32[]{:S(2)}) async-start(f32[8,32,128]{2,1,0:T(8,128)} %broadcast_in_dim.33), calls=%async_computation.5 | async-start | bytes 262144 | tf_op jit(solution)/shard_map/all_to_all | solution.py:38
  116.1 7.8 %all-to-all-done.5 = f32[8,32,128]{2,1,0:T(8,128)S(1)} async-done(((f32[8,32,128]{2,1,0:T(8,128)}), f32[8,32,128]{2,1,0:T(8,128)S(1)}, u32[]{:S(2)}, u32[]{:S(2)}) %all-to-all-start.5) | async-done | bytes 131104 | tf_op jit(solution)/shard_map/all_to_all | solution.py:38
  124.0 4.0 %all_gather.19 = f32[512,128]{1,0:T(8,128)S(1)} all-gather(f32[256,128]{1,0:T(8,128)S(1)} %bitcast.113), channel_id=1, replica_groups=mesh['xh'=2,'xl'=2,'z'=8,'y'=8,'core'=2] {'core'}, dimensions={0}, use_global_device_ids=true | all-gather | bytes 393216 | tf_op jit(solution)/shard_map/all_gather | solution.py:45
  129.7 4.0 %all-to-all-start.6 = ((f32[8,32,128]{2,1,0:T(8,128)}), f32[8,32,128]{2,1,0:T(8,128)S(1)}, u32[]{:S(2)}, u32[]{:S(2)}) async-start(f32[8,32,128]{2,1,0:T(8,128)} %bitcast.21), calls=%async_computation.6 | async-start | bytes 262144 | tf_op jit(solution)/shard_map/all_to_all | solution.py:38
  133.9 7.7 %all-to-all-done.6 = f32[8,32,128]{2,1,0:T(8,128)S(1)} async-done(((f32[8,32,128]{2,1,0:T(8,128)}), f32[8,32,128]{2,1,0:T(8,128)S(1)}, u32[]{:S(2)}, u32[]{:S(2)}) %all-to-all-start.6) | async-done | bytes 131104 | tf_op jit(solution)/shard_map/all_to_all | solution.py:38
  141.7 10.4 %all_to_all.76 = f32[8,32,128]{2,1,0:T(8,128)S(1)} all-to-all(f32[8,32,128]{2,1,0:T(8,128)S(1)} %broadcast_in_dim.34), channel_id=1, replica_groups=mesh['xh'=2,'xl'=2,'z'=8,'y'=8,'core'=2] {'y'}, dimensions={0} | all-to-all | bytes 262144 | tf_op jit(solution)/shard_map/all_to_all | solution.py:38
  152.1 4.8 %all_gather.20 = f32[512,128]{1,0:T(8,128)S(1)} all-gather(f32[256,128]{1,0:T(8,128)S(1)} %bitcast.114), channel_id=1, replica_groups=mesh['xh'=2,'xl'=2,'z'=8,'y'=8,'core'=2] {'core'}, dimensions={0}, use_global_device_ids=true | all-gather | bytes 393216 | tf_op jit(solution)/shard_map/all_gather | solution.py:45
  159.7 3.4 %all-to-all-start.8 = ((f32[8,32,128]{2,1,0:T(8,128)}), f32[8,32,128]{2,1,0:T(8,128)S(1)}, u32[]{:S(2)}, u32[]{:S(2)}) async-start(f32[8,32,128]{2,1,0:T(8,128)} %bitcast.25), calls=%async_computation.8 | async-start | bytes 262144 | tf_op jit(solution)/shard_map/all_to_all | solution.py:38
  163.2 8.1 %all-to-all-done.8 = f32[8,32,128]{2,1,0:T(8,128)S(1)} async-done(((f32[8,32,128]{2,1,0:T(8,128)}), f32[8,32,128]{2,1,0:T(8,128)S(1)}, u32[]{:S(2)}, u32[]{:S(2)}) %all-to-all-start.8) | async-done | bytes 131104 | tf_op jit(solution)/shard_map/all_to_all | solution.py:38
  171.5 10.3 %all_to_all.77 = f32[8,32,128]{2,1,0:T(8,128)S(1)} all-to-all(f32[8,32,128]{2,1,0:T(8,128)S(1)} %broadcast_in_dim.35), channel_id=1, replica_groups=mesh['xh'=2,'xl'=2,'z'=8,'y'=8,'core'=2] {'y'}, dimensions={0} | all-to-all | bytes 262144 | tf_op jit(solution)/shard_map/all_to_all | solution.py:38
  181.9 4.4 %all_gather.21 = f32[512,128]{0,1:T(8,128)S(1)} all-gather(f32[256,128]{0,1:T(8,128)S(1)} %copy.29), channel_id=1, replica_groups=mesh['xh'=2,'xl'=2,'z'=8,'y'=8,'core'=2] {'core'}, dimensions={0}, use_global_device_ids=true | all-gather | bytes 393216 | tf_op jit(solution)/shard_map/all_gather | solution.py:45
  188.2 3.5 %all-to-all-start.10 = ((f32[16,32,128]{2,1,0:T(8,128)}), f32[16,32,128]{2,1,0:T(8,128)S(1)}, u32[]{:S(2)}, u32[]{:S(2)}) async-start(f32[16,32,128]{2,1,0:T(8,128)} %fusion.46), calls=%async_computation.10 | async-start | bytes 524288 | tf_op jit(solution)/shard_map/all_to_all | solution.py:38
  192.2 8.8 %all-to-all-done.10 = f32[16,32,128]{2,1,0:T(8,128)S(1)} async-done(((f32[16,32,128]{2,1,0:T(8,128)}), f32[16,32,128]{2,1,0:T(8,128)S(1)}, u32[]{:S(2)}, u32[]{:S(2)}) %all-to-all-start.10) | async-done | bytes 262176 | tf_op jit(solution)/shard_map/all_to_all | solution.py:38
  201.7 3.4 %all-to-all-start.11 = ((f32[8,32,128]{2,1,0:T(8,128)}), f32[8,32,128]{2,1,0:T(8,128)S(1)}, u32[]{:S(2)}, u32[]{:S(2)}) async-start(f32[8,32,128]{2,1,0:T(8,128)} %broadcast_in_dim.36), calls=%async_computation.11 | async-start | bytes 262144 | tf_op jit(solution)/shard_map/all_to_all | solution.py:38
  206.3 6.6 %all-to-all-done.11 = f32[8,32,128]{2,1,0:T(8,128)S(1)} async-done(((f32[8,32,128]{2,1,0:T(8,128)}), f32[8,32,128]{2,1,0:T(8,128)S(1)}, u32[]{:S(2)}, u32[]{:S(2)}) %all-to-all-start.11) | async-done | bytes 131104 | tf_op jit(solution)/shard_map/all_to_all | solution.py:38
  213.0 6.3 %all-to-all-start.12 = ((f32[16,32,512]{2,1,0:T(8,128)}), f32[16,32,512]{2,1,0:T(8,128)S(1)}, u32[]{:S(2)}, u32[]{:S(2)}) async-start(f32[16,32,512]{2,1,0:T(8,128)} %bitcast.33), calls=%async_computation.12 | async-start | bytes 2097152 | tf_op jit(solution)/shard_map/all_to_all | solution.py:38
  219.4 2.0 all_gather.22
  222.1 25.2 %all-to-all-done.12 = f32[16,32,512]{2,1,0:T(8,128)S(1)} async-done(((f32[16,32,512]{2,1,0:T(8,128)}), f32[16,32,512]{2,1,0:T(8,128)S(1)}, u32[]{:S(2)}, u32[]{:S(2)}) %all-to-all-start.12) | async-done | bytes 1048608 | tf_op jit(solution)/shard_map/all_to_all | solution.py:38
  248.8 5.5 %all-to-all-start.13 = ((f32[32,32,128]{2,1,0:T(8,128)}), f32[32,32,128]{2,1,0:T(8,128)S(1)}, u32[]{:S(2)}, u32[]{:S(2)}) async-start(f32[32,32,128]{2,1,0:T(8,128)} %concatenate.7), calls=%async_computation.13 | async-start | bytes 1048576 | tf_op jit(solution)/shard_map/all_to_all | solution.py:38
  254.4 16.3 %all-to-all-done.13 = f32[32,32,128]{2,1,0:T(8,128)S(1)} async-done(((f32[32,32,128]{2,1,0:T(8,128)}), f32[32,32,128]{2,1,0:T(8,128)S(1)}, u32[]{:S(2)}, u32[]{:S(2)}) %all-to-all-start.13) | async-done | bytes 524320 | tf_op jit(solution)/shard_map/all_to_all | solution.py:38
  270.9 10.3 %all_to_all.78 = f32[8,32,128]{2,1,0:T(8,128)S(1)} all-to-all(f32[8,32,128]{2,1,0:T(8,128)S(1)} %broadcast_in_dim.37), channel_id=1, replica_groups=mesh['xh'=2,'xl'=2,'z'=8,'y'=8,'core'=2] {'y'}, dimensions={0} | all-to-all | bytes 262144 | tf_op jit(solution)/shard_map/all_to_all | solution.py:38
  281.3 4.5 %all_gather.23 = f32[512,128]{0,1:T(8,128)S(1)} all-gather(f32[256,128]{0,1:T(8,128)S(1)} %copy.33), channel_id=1, replica_groups=mesh['xh'=2,'xl'=2,'z'=8,'y'=8,'core'=2] {'core'}, dimensions={0}, use_global_device_ids=true | all-gather | bytes 393216 | tf_op jit(solution)/shard_map/all_gather | solution.py:45
  (75 shorter events, 24.9 us)
Async XLA Ops:
  0.0 1.0 copy-start
  0.0 2.6 copy-start.3
  3.9 13.9 %copy-start.5 = (s32[32]{0:T(128)S(1)}, s32[32]{0:T(128)}, u32[]{:S(2)}) copy-start(s32[32]{0:T(128)} %param.10) | copy-start | bytes 388
  3.9 23.5 %all-to-all-start = ((f32[32,16,128]{2,1,0:T(8,128)}), f32[32,16,128]{2,1,0:T(8,128)S(1)}, u32[]{:S(2)}, u32[]{:S(2)}) async-start(f32[32,16,128]{2,1,0:T(8,128)} %bitcast.4), calls=%async_computation | async-start | bytes 524288 | tf_op jit(solution)/shard_map/all_to_all | solution.py:38
  18.8 0.7 copy-start.4
  48.1 13.8 %all-to-all-start.2 = ((f32[32,16,128]{2,1,0:T(8,128)}), f32[32,16,128]{2,1,0:T(8,128)S(1)}, u32[]{:S(2)}, u32[]{:S(2)}) async-start(f32[32,16,128]{2,1,0:T(8,128)} %concatenate.6), calls=%async_computation.2 | async-start | bytes 524288 | tf_op jit(solution)/shard_map/all_to_all | solution.py:38
  61.9 7.7 %copy-start.2 = (f32[1,1,512,128]{3,2,1,0:T(8,128)S(1)}, f32[1,1,512,128]{3,2,1,0:T(8,128)}, u32[]{:S(2)}) copy-start(f32[1,1,512,128]{3,2,1,0:T(8,128)} %param.7) | copy-start | bytes 786436
  61.9 35.5 %all-to-all-start.3 = ((f32[16,32,512]{2,1,0:T(8,128)}), f32[16,32,512]{2,1,0:T(8,128)S(1)}, u32[]{:S(2)}, u32[]{:S(2)}) async-start(f32[16,32,512]{2,1,0:T(8,128)} %bitcast.11), calls=%async_computation.3 | async-start | bytes 2097152 | tf_op jit(solution)/shard_map/all_to_all | solution.py:38
  98.9 13.1 %all-to-all-start.4 = ((f32[16,32,128]{2,1,0:T(8,128)}), f32[16,32,128]{2,1,0:T(8,128)S(1)}, u32[]{:S(2)}, u32[]{:S(2)}) async-start(f32[16,32,128]{2,1,0:T(8,128)} %fusion.45), calls=%async_computation.4 | async-start | bytes 524288 | tf_op jit(solution)/shard_map/all_to_all | solution.py:38
  112.7 11.2 %all-to-all-start.5 = ((f32[8,32,128]{2,1,0:T(8,128)}), f32[8,32,128]{2,1,0:T(8,128)S(1)}, u32[]{:S(2)}, u32[]{:S(2)}) async-start(f32[8,32,128]{2,1,0:T(8,128)} %broadcast_in_dim.33), calls=%async_computation.5 | async-start | bytes 262144 | tf_op jit(solution)/shard_map/all_to_all | solution.py:38
  129.7 11.9 %all-to-all-start.6 = ((f32[8,32,128]{2,1,0:T(8,128)}), f32[8,32,128]{2,1,0:T(8,128)S(1)}, u32[]{:S(2)}, u32[]{:S(2)}) async-start(f32[8,32,128]{2,1,0:T(8,128)} %bitcast.21), calls=%async_computation.6 | async-start | bytes 262144 | tf_op jit(solution)/shard_map/all_to_all | solution.py:38
  156.9 1.0 copy-start.1
  159.7 11.7 %all-to-all-start.8 = ((f32[8,32,128]{2,1,0:T(8,128)}), f32[8,32,128]{2,1,0:T(8,128)S(1)}, u32[]{:S(2)}, u32[]{:S(2)}) async-start(f32[8,32,128]{2,1,0:T(8,128)} %bitcast.25), calls=%async_computation.8 | async-start | bytes 262144 | tf_op jit(solution)/shard_map/all_to_all | solution.py:38
  188.2 12.7 %all-to-all-start.10 = ((f32[16,32,128]{2,1,0:T(8,128)}), f32[16,32,128]{2,1,0:T(8,128)S(1)}, u32[]{:S(2)}, u32[]{:S(2)}) async-start(f32[16,32,128]{2,1,0:T(8,128)} %fusion.46), calls=%async_computation.10 | async-start | bytes 524288 | tf_op jit(solution)/shard_map/all_to_all | solution.py:38
  201.7 11.2 %all-to-all-start.11 = ((f32[8,32,128]{2,1,0:T(8,128)}), f32[8,32,128]{2,1,0:T(8,128)S(1)}, u32[]{:S(2)}, u32[]{:S(2)}) async-start(f32[8,32,128]{2,1,0:T(8,128)} %broadcast_in_dim.36), calls=%async_computation.11 | async-start | bytes 262144 | tf_op jit(solution)/shard_map/all_to_all | solution.py:38
  213.0 34.3 %all-to-all-start.12 = ((f32[16,32,512]{2,1,0:T(8,128)}), f32[16,32,512]{2,1,0:T(8,128)S(1)}, u32[]{:S(2)}, u32[]{:S(2)}) async-start(f32[16,32,512]{2,1,0:T(8,128)} %bitcast.33), calls=%async_computation.12 | async-start | bytes 2097152 | tf_op jit(solution)/shard_map/all_to_all | solution.py:38
  248.8 22.0 %all-to-all-start.13 = ((f32[32,32,128]{2,1,0:T(8,128)}), f32[32,32,128]{2,1,0:T(8,128)S(1)}, u32[]{:S(2)}, u32[]{:S(2)}) async-start(f32[32,32,128]{2,1,0:T(8,128)} %concatenate.7), calls=%async_computation.13 | async-start | bytes 1048576 | tf_op jit(solution)/shard_map/all_to_all | solution.py:38

commit v3 on v1

--- a/solution.py
+++ b/solution.py
@@ -35,7 +35,8 @@
 
 
 def a2a(array, axes):
-    return lax.all_to_all(array, axes, 0, 0, tiled=True)
+    array = lax.optimization_barrier(array)
+    return lax.optimization_barrier(lax.all_to_all(array, axes, 0, 0, tiled=True))
 
 
 def spread(piece, ny):
@@ -69,35 +70,41 @@
     mine_l = lax.dynamic_index_in_dim(lower_use, row, 0, keepdims=False)
     mine = (mine_u + mine_l)[top:]
 
+    ranks = jnp.arange(count)
+    w_all = jnp.where(ranks < top, to_me_u, 0.0)
+    w_one = jnp.where(ranks[:top] < top // 2, to_me_u[top:], 0.0) * high
+    w_two = jnp.where(ranks[:nz] < nz // 2, to_me_u[top + top // 2:], 0.0) * last
+    w_three = to_me_l[top + top // 2:] * last
+    w_down = to_me_l[top:] * high
+    y = mm(up, base)
+
     sent = slot1.T.astype(jnp.float32).reshape(nc, ny, piece, width)
     sent = jnp.transpose(sent, (1, 0, 2, 3)).reshape(ncol, piece, width)
+    first = (sent, y, mine, w_all, w_one, w_two, w_three, w_down, to_col_l, base, up, low)
+    sent, y, mine, w_all, w_one, w_two, w_three, w_down, to_col_l, base, up, low = (
+        lax.optimization_barrier(first)
+    )
     slices = a2a(sent, COL)
     slices = (slices * mine[:, None, None]).astype(jnp.bfloat16).reshape(width, width)
 
     def updates(panel):
         return mm(slices, panel).reshape(top, piece, nrhs)
 
-    y = mm(up, base)
     out = updates(y)
     got = a2a(jnp.concatenate([jnp.zeros_like(out), out], 0), ROW)
-    w = jnp.where(jnp.arange(count) < top, to_me_u, 0.0)
-    part = weighted(w, got)
+    part = weighted(w_all, got)
     y = mm(up, base - spread(part, ny))
     got = a2a(updates(y), HALF)
-    w = jnp.where(jnp.arange(top) < top // 2, to_me_u[top:], 0.0) * high
-    part = part + weighted(w, got)
+    part = part + weighted(w_one, got)
     y = mm(up, base - spread(part, ny))
     got = a2a(updates(y)[top // 2:], "z")
-    w = jnp.where(jnp.arange(nz) < nz // 2, to_me_u[top + top // 2:], 0.0) * last
-    part = part + weighted(w, got)
+    part = part + weighted(w_two, got)
     y = mm(up, base - spread(part, ny))
     x = mm(low, y)
     got = a2a(updates(x)[top // 2:], "z")
-    w = to_me_l[top + top // 2:] * last
-    x = mm(low, y - spread(weighted(w, got), ny))
+    x = mm(low, y - spread(weighted(w_three, got), ny))
     got = a2a(updates(x), HALF)
-    w = to_me_l[top:] * high
-    known = spread(weighted(w, got), ny)
+    known = spread(weighted(w_down, got), ny)
     x = mm(low, y - known)
     full = lax.dot_general(
         slot0.astype(jnp.float32), x, (((0,), (0,)), ((), ())), precision=lax.Precision.HIGHEST

time: 257 us -> 251 us (0.977)
  blocking collectives: 109 us -> 233 us
  waiting for transfers between devices: 84.1 us -> 0 us
  starting transfers between devices: 40.2 us -> 0 us
  matrix products: 12.8 us -> 9.55 us
    all_to_all x7 -> x14, blocking collectives: 81.2 us -> 205 us  [a2a(): lax.all_to_all(array, axes, 0, 0, tiled=True)]
    all_to_all x7 -> x0, waiting for transfers between devices: 84.1 us -> none  [a2a(): return lax.all_to_all(array, axes, 0, 0, tiled=True)]
    all_to_all x7 -> x0, starting transfers between devices: 40.2 us -> none  [a2a(): return lax.all_to_all(array, axes, 0, 0, tiled=True)]
  transfers between devices with their start and end apart: 7 -> 0, of which waited for: 7 -> 0; matrix products, arithmetic and copies ran while one was open for 1% -> 0% of each run, Pallas kernels for 0% -> 0%
where the time goes in v3:
time: 251 us; the launch traced here: 248 us
  blocking collectives  233 us (93%)
  matrix products  9.55 us (4%)
  local copies, waits for them, and re-layouts  4.51 us (2%)
    all_to_all x14, blocking collectives, a2a(): lax.all_to_all(array, axes, 0, 0, tiled=True)  205 us
    all_gather x5, blocking collectives, spread(): return lax.all_gather(half, 'core', tiled=True)  22.6 us
    dot_general x12, matrix products, mm(): jnp.dot(matrix.astype(jnp.float32), panel, precision=lax.Precision.HIGHEST)  7.51 us
    all_gather x1, blocking collectives, per_device(): copies = lax.all_gather(part[None], 'core', tiled=True)  5.19 us

profile of v3, /device:TPU:1, one launch (start us, length us, event | category | flops | bytes accessed | tf_op | source)
XLA Modules:
  0.0 248.5 jit_solution(1383902474912780864)
XLA Ops:
  0.0 0.7 copy-done.5
  1.6 0.7 copy-done.4
  2.8 1.0 slice-done
  4.4 0.8 copy-done.2
  5.8 37.9 %all_to_all.70 = f32[16,32,512]{2,1,0:T(8,128)S(1)} all-to-all(f32[16,32,512]{2,1,0:T(8,128)S(1)} %bitcast.101), channel_id=1, replica_groups=mesh['xh'=2,'xl'=2,'z'=8,'y'=8,'core'=2] {'y','core'}, dimensions={0} | all-to-all | bytes 2097152 | tf_op jit(solution)/shard_map/all_to_all | solution.py:39
  43.8 1.0 fusion.2
  44.8 28.3 %all_to_all.71 = f32[32,32,128]{2,1,0:T(8,128)S(1)} all-to-all(f32[32,32,128]{2,1,0:T(8,128)S(1)} %fusion.2), channel_id=1, replica_groups=mesh['xh'=2,'xl'=2,'z'=8,'y'=8,'core'=2] {'xh','xl','z'}, dimensions={0} | all-to-all | bytes 1048576 | tf_op jit(solution)/shard_map/all_to_all | solution.py:39
  73.2 10.1 %all_to_all.72 = f32[8,32,128]{2,1,0:T(8,128)S(1)} all-to-all(f32[8,32,128]{2,1,0:T(8,128)S(1)} %broadcast_in_dim.31), channel_id=1, replica_groups=mesh['xh'=2,'xl'=2,'z'=8,'y'=8,'core'=2] {'y'}, dimensions={0} | all-to-all | bytes 262144 | tf_op jit(solution)/shard_map/all_to_all | solution.py:39
  83.4 4.0 %all_gather.18 = f32[512,128]{1,0:T(8,128)S(1)} all-gather(f32[256,128]{1,0:T(8,128)S(1)} %bitcast.104), channel_id=1, replica_groups=mesh['xh'=2,'xl'=2,'z'=8,'y'=8,'core'=2] {'core'}, dimensions={0}, use_global_device_ids=true | all-gather | bytes 393216 | tf_op jit(solution)/shard_map/all_gather | solution.py:46
  87.4 0.6 convolution_bitcast_fusion.3
  88.0 0.6 fusion.34
  88.6 13.2 %all_to_all.73 = f32[16,32,128]{2,1,0:T(8,128)S(1)} all-to-all(f32[16,32,128]{2,1,0:T(8,128)S(1)} %fusion.34), channel_id=1, replica_groups=mesh['xh'=2,'xl'=2,'z'=8,'y'=8,'core'=2] {'xl','z'}, dimensions={0} | all-to-all | bytes 524288 | tf_op jit(solution)/shard_map/all_to_all | solution.py:39
  101.9 10.4 %all_to_all.74 = f32[8,32,128]{2,1,0:T(8,128)S(1)} all-to-all(f32[8,32,128]{2,1,0:T(8,128)S(1)} %broadcast_in_dim.32), channel_id=1, replica_groups=mesh['xh'=2,'xl'=2,'z'=8,'y'=8,'core'=2] {'y'}, dimensions={0} | all-to-all | bytes 262144 | tf_op jit(solution)/shard_map/all_to_all | solution.py:39
  112.3 4.8 %all_gather.19 = f32[512,128]{1,0:T(8,128)S(1)} all-gather(f32[256,128]{1,0:T(8,128)S(1)} %bitcast.105), channel_id=1, replica_groups=mesh['xh'=2,'xl'=2,'z'=8,'y'=8,'core'=2] {'core'}, dimensions={0}, use_global_device_ids=true | all-gather | bytes 393216 | tf_op jit(solution)/shard_map/all_gather | solution.py:46
  117.1 0.6 fusion.7
  118.1 11.6 %all_to_all.75 = f32[8,32,128]{2,1,0:T(8,128)S(1)} all-to-all(f32[8,32,128]{2,1,0:T(8,128)S(1)} %bitcast.106), channel_id=1, replica_groups=mesh['xh'=2,'xl'=2,'z'=8,'y'=8,'core'=2] {'z'}, dimensions={0} | all-to-all | bytes 262144 | tf_op jit(solution)/shard_map/all_to_all | solution.py:39
  129.9 10.4 %all_to_all.76 = f32[8,32,128]{2,1,0:T(8,128)S(1)} all-to-all(f32[8,32,128]{2,1,0:T(8,128)S(1)} %broadcast_in_dim.33), channel_id=1, replica_groups=mesh['xh'=2,'xl'=2,'z'=8,'y'=8,'core'=2] {'y'}, dimensions={0} | all-to-all | bytes 262144 | tf_op jit(solution)/shard_map/all_to_all | solution.py:39
  140.3 4.8 %all_gather.20 = f32[512,128]{1,0:T(8,128)S(1)} all-gather(f32[256,128]{1,0:T(8,128)S(1)} %bitcast.107), channel_id=1, replica_groups=mesh['xh'=2,'xl'=2,'z'=8,'y'=8,'core'=2] {'core'}, dimensions={0}, use_global_device_ids=true | all-gather | bytes 393216 | tf_op jit(solution)/shard_map/all_gather | solution.py:46
  145.1 0.6 fusion.5
  147.1 10.8 %all_to_all.77 = f32[8,32,128]{2,1,0:T(8,128)S(1)} all-to-all(f32[8,32,128]{2,1,0:T(8,128)S(1)} %bitcast.108), channel_id=1, replica_groups=mesh['xh'=2,'xl'=2,'z'=8,'y'=8,'core'=2] {'z'}, dimensions={0} | all-to-all | bytes 262144 | tf_op jit(solution)/shard_map/all_to_all | solution.py:39
  158.0 10.3 %all_to_all.78 = f32[8,32,128]{2,1,0:T(8,128)S(1)} all-to-all(f32[8,32,128]{2,1,0:T(8,128)S(1)} %broadcast_in_dim.34), channel_id=1, replica_groups=mesh['xh'=2,'xl'=2,'z'=8,'y'=8,'core'=2] {'y'}, dimensions={0} | all-to-all | bytes 262144 | tf_op jit(solution)/shard_map/all_to_all | solution.py:39
  168.4 4.3 %all_gather.21 = f32[512,128]{1,0:T(8,128)S(1)} all-gather(f32[256,128]{1,0:T(8,128)S(1)} %bitcast.109), channel_id=1, replica_groups=mesh['xh'=2,'xl'=2,'z'=8,'y'=8,'core'=2] {'core'}, dimensions={0}, use_global_device_ids=true | all-gather | bytes 393216 | tf_op jit(solution)/shard_map/all_gather | solution.py:46
  172.7 0.6 convolution_bitcast_fusion.2
  173.3 0.6 fusion.36
  173.9 11.8 %all_to_all.79 = f32[16,32,128]{2,1,0:T(8,128)S(1)} all-to-all(f32[16,32,128]{2,1,0:T(8,128)S(1)} %fusion.36), channel_id=1, replica_groups=mesh['xh'=2,'xl'=2,'z'=8,'y'=8,'core'=2] {'xl','z'}, dimensions={0} | all-to-all | bytes 524288 | tf_op jit(solution)/shard_map/all_to_all | solution.py:39
  185.9 10.3 %all_to_all.80 = f32[8,32,128]{2,1,0:T(8,128)S(1)} all-to-all(f32[8,32,128]{2,1,0:T(8,128)S(1)} %broadcast_in_dim.35), channel_id=1, replica_groups=mesh['xh'=2,'xl'=2,'z'=8,'y'=8,'core'=2] {'y'}, dimensions={0} | all-to-all | bytes 262144 | tf_op jit(solution)/shard_map/all_to_all | solution.py:39
  196.2 4.7 %all_gather.22 = f32[512,128]{1,0:T(8,128)S(1)} all-gather(f32[256,128]{1,0:T(8,128)S(1)} %bitcast.110), channel_id=1, replica_groups=mesh['xh'=2,'xl'=2,'z'=8,'y'=8,'core'=2] {'core'}, dimensions={0}, use_global_device_ids=true | all-gather | bytes 393216 | tf_op jit(solution)/shard_map/all_gather | solution.py:46
  202.1 15.3 %all_to_all.81 = f32[32,16,128]{2,1,0:T(8,128)S(1)} all-to-all(f32[32,16,128]{2,1,0:T(8,128)S(1)} %bitcast.103), channel_id=1, replica_groups=mesh['xh'=2,'xl'=2,'z'=8,'y'=8,'core'=2] {'xh','xl','z'}, dimensions={0} | all-to-all | bytes 524288 | tf_op jit(solution)/shard_map/all_to_all | solution.py:39
  217.5 5.2 %all-gather = f32[32,128]{1,0:T(8,128)S(1)} all-gather(f32[16,128]{1,0:T(8,128)S(1)} %multiply_reduce_fusion.1), channel_id=2, replica_groups=mesh['xh'=2,'xl'=2,'z'=8,'y'=8,'core'=2] {'core'}, dimensions={0}, use_global_device_ids=true | all-gather | bytes 24576 | tf_op jit(solution)/shard_map/all_gather | solution.py:115
  222.7 10.9 %all_to_all.82 = f32[8,2,16,128]{3,2,1,0:T(8,128)S(1)} all-to-all(f32[8,2,16,128]{3,2,1,0:T(8,128)S(1)} %broadcast_in_dim.37), channel_id=1, replica_groups=mesh['xh'=2,'xl'=2,'z'=8,'y'=8,'core'=2] {'y'}, dimensions={0} | all-to-all | bytes 262144 | tf_op jit(solution)/shard_map/all_to_all | solution.py:39
  233.5 13.6 %all_to_all.83 = f32[32,16,128]{2,1,0:T(8,128)S(1)} all-to-all(f32[32,16,128]{2,1,0:T(8,128)S(1)} %concatenate.7), channel_id=1, replica_groups=mesh['xh'=2,'xl'=2,'z'=8,'y'=8,'core'=2] {'xh','xl','z'}, dimensions={0} | all-to-all | bytes 524288 | tf_op jit(solution)/shard_map/all_to_all | solution.py:39
  247.2 1.3 convolution_bitcast_fusion
  (55 shorter events, 6.2 us)
Async XLA Ops:
  0.0 4.3 %copy-start = (bf16[1,1,512,512]{3,2,1,0:T(8,128)(2,1)S(1)}, bf16[1,1,512,512]{3,2,1,0:T(8,128)(2,1)}, u32[]{:S(2)}) copy-start(bf16[1,1,512,512]{3,2,1,0:T(8,128)(2,1)} %param.8) | copy-start | bytes 1572868
  0.0 0.7 copy-start.5
  1.5 0.7 copy-start.4
  2.8 1.0 slice-start
  4.2 1.0 copy-start.2
  145.1 1.0 copy-start.1
  196.2 5.3 %copy-start.3 = (bf16[1,1,1,2,512,512]{5,4,3,2,1,0:T(8,128)(2,1)S(1)}, bf16[1,1,1,2,512,512]{5,4,3,2,1,0:T(8,128)(2,1)}, u32[]{:S(2)}) copy-start(bf16[1,1,1,2,512,512]{5,4,3,2,1,0:T(8,128)(2,1)} %param.6) | copy-start | bytes 3145732

commit v4 on v3

v4 whole, which is shorter than its diff:
```python
import jax
import jax.numpy as jnp
import numpy as np
from jax import lax
from jax.sharding import Mesh, PartitionSpec as P

LEVELS = 4
HALF = ("xl", "z")
ROW = ("xh", "xl", "z")
COL = ("y", "core")
HIGHEST = lax.Precision.HIGHEST


def patterns(parents, block_mask):
    count = parents.shape[0]
    positions = jnp.arange(count, dtype=jnp.int32)
    step = (parents[:, None] == positions[None, :]).astype(jnp.float32)
    identity = jnp.eye(count, dtype=jnp.float32)
    power = identity
    ancestry = identity
    for _ in range(LEVELS - 1):
        power = jnp.dot(power, step, precision=HIGHEST)
        ancestry = ancestry + power
    ancestry = jnp.minimum(ancestry, 1.0)
    weights = block_mask.astype(jnp.float32) * (1.0 - identity)
    return weights * ancestry, weights * ancestry.T, ancestry


def mm(matrix, panel):
    return jnp.dot(matrix.astype(jnp.float32), panel, precision=HIGHEST)


def mt(panel, matrix):
    return lax.dot_general(
        panel, matrix.astype(jnp.float32), (((1,), (1,)), ((), ())), precision=HIGHEST
    )


def weighted(weights, received):
    return jnp.sum(weights[:, None, None] * received, axis=0)


def a2a(array, axes):
    array = lax.optimization_barrier(array)
    return lax.optimization_barrier(lax.all_to_all(array, axes, 0, 0, tiled=True))


def copies(array, times):
    return jnp.broadcast_to(array[None], (times,) + array.shape)


def over_columns(array, ny):
    both = lax.all_gather(array[None], "core", tiled=True)
    return a2a(copies(both, ny), "y")


def per_device(factor, rhs, upper_inverse, lower_inverse, parents, block_mask):
    ny, nc, nz = lax.axis_size("y"), lax.axis_size("core"), lax.axis_size("z")
    ncol = ny * nc
    slot0 = factor[0, 0, 0, 0]
    slot1 = factor[0, 0, 0, 1]
    base = rhs[0, 0]
    up = upper_inverse[0, 0]
    low = lower_inverse[0, 0]
    width, nrhs = base.shape
    piece = width // ncol
    mine_rhs = nrhs // ncol
    count = parents.shape[0]
    top = count // 2
    small = width // count
    row = lax.axis_index(ROW)
    col = lax.axis_index(COL)
    zat = lax.axis_index("z")
    is_high = lax.axis_index("xh") == 1
    high = is_high.astype(jnp.float32)
    last = high * (lax.axis_index("xl") == 1).astype(jnp.float32)
    levels_np = np.zeros(count, np.int32)
    for level in range(1, LEVELS):
        levels_np[count - count // 2**level:] = level
    level_of = jnp.asarray(levels_np)
    my_level = level_of[row]
    is_one = high * (my_level == 1)
    upper_use, lower_use, ancestry = patterns(parents, block_mask)

    def column(table, at):
        return lax.dynamic_index_in_dim(table, at, 1, keepdims=False)

    def line(table, at):
        return lax.dynamic_index_in_dim(table, at, 0, keepdims=False)

    w_all = jnp.where(level_of == 0, column(upper_use, row), 0.0)
    to_col_l = column(lower_use, col)
    above_u = line(upper_use, row)[top:]
    used = (line(upper_use, row) + line(lower_use, row))[top:]
    above_l = column(lower_use, row)[top:]
    above = line(ancestry, row)[top:] * high
    lev_top = level_of[top:]
    pick_u = [jnp.where(lev_top == level, above_u, 0.0) for level in (2, 3)]
    pick_l = [jnp.where(lev_top == level, above_l, 0.0) for level in (2, 3)]
    send_to = [jnp.where(lev_top == level, above, 0.0) * is_one for level in (2, 3)]
    take = [jnp.where(lev_top == level, above, 0.0) for level in (2, 3)]
    roots = jnp.where(level_of == 3, jnp.arange(count, dtype=jnp.int32), parents)[count - nz:]
    family = (roots == roots[zat]).astype(jnp.float32) * last

    y0 = mm(up, base)
    base_t = lax.dynamic_slice_in_dim(base.T, col * mine_rhs, mine_rhs, 0)
    both = jnp.dot(low, up, preferred_element_type=jnp.float32)
    sent = slot1.T.astype(jnp.float32).reshape(ncol, piece, width)
    (sent, y0, base_t, both, up, low, used, w_all, to_col_l, pick_u, pick_l, send_to, take, family) = (
        lax.optimization_barrier(
            (sent, y0, base_t, both, up, low, used, w_all, to_col_l, pick_u, pick_l, send_to, take, family)
        )
    )

    slices = a2a(sent, COL)

    def gathered(weights, pieces):
        local = jnp.concatenate([weighted(w, pieces) for w in weights], 0)
        return lax.all_gather(local, COL, tiled=True)

    def apart(product):
        split = product.reshape(mine_rhs, ncol, 2, piece)
        return jnp.transpose(split, (2, 0, 1, 3)).reshape(2, mine_rhs, width)

    blocks_u = gathered(pick_u, slices)
    half = top // 2
    quarter = top // 4
    roots_part = slices[half:half + quarter].reshape(quarter * piece, width)
    roots_part = mm(roots_part, both).reshape(quarter, piece, width)
    middle = jnp.where(my_level == 3, roots_part, slices[half:half + quarter])
    down = jnp.concatenate([slices[:half], middle, slices[half + quarter:]], 0)
    blocks_l = gathered(pick_l, a2a(down, HALF))

    own = (slices * used[:, None, None]).astype(jnp.bfloat16).reshape(width, width)
    out = mm(own, y0).reshape(top, piece, nrhs)
    got = a2a(jnp.concatenate([jnp.zeros_like(out), out], 0), ROW)
    part = weighted(w_all, got).T.reshape(ncol, mine_rhs, piece)
    part = jnp.transpose(a2a(part, COL), (1, 0, 2)).reshape(mine_rhs, width)
    rest = base_t - part * high
    y = mt(rest, up)
    parts = apart(mt(y, blocks_u))
    out = send_to[0][:, None, None] * parts[0] + send_to[1][:, None, None] * parts[1]
    rest = rest - jnp.sum(a2a(out, HALF), 0) * high
    y = mt(rest, up)
    out = jnp.where(my_level == 3, rest, -apart(mt(y, blocks_u))[1])
    root = weighted(family, a2a(copies(out, nz), "z"))
    y_root = mt(root, up)
    down_root = apart(mt(root, blocks_l))[1]
    x = mt(jnp.where(my_level == 3, y_root, y - down_root), low)
    got = a2a(copies(x, top), HALF)
    two = jnp.concatenate([weighted(take[0], got), weighted(take[1], got)], 0)
    prod = lax.dot_general(
        two, blocks_l, (((1,), (1,)), ((), ())), precision=HIGHEST
    ).reshape(2, mine_rhs, ncol, 2, piece)
    update = (prod[0, :, :, 0] + prod[1, :, :, 1]).reshape(mine_rhs, width)
    x = jnp.where(my_level == 1, mt(y - update, low), x)
    x = over_columns(x, ny).reshape(nrhs, width)
    full = lax.dot_general(
        slot0.astype(jnp.float32), x, (((0,), (1,)), ((), ())), precision=HIGHEST
    )
    got = a2a(full.reshape(count, small, nrhs), ROW)
    every = over_columns(weighted(to_col_l, got), ny).reshape(ncol, small, nrhs)
    got = a2a(jnp.concatenate([every, jnp.zeros_like(every)], 0), ROW).reshape(width, nrhs)
    result = jnp.where(is_high, x.T, mm(low, y0 - got))
    return result[None, None]


def solution(mesh):
    grid = Mesh(mesh.devices.reshape(2, 2, 8, 8, 2), ("xh", "xl", "z", "y", "core"))
    placed = (
        P(ROW, None, COL, None, None, None),
        P(ROW, None, None, None),
        P(ROW, None, None, None),
        P(ROW, None, None, None),
        P(),
        P(),
    )
    return jax.shard_map(
        per_device,
        mesh=grid,
        in_specs=placed,
        out_specs=P(ROW, None, None, None),
        check_vma=False,
    )
```

time: 251 us -> 272 us (1.084)
  blocking collectives: 233 us -> 139 us
  waiting for transfers between devices: 0 us -> 48.6 us
  starting transfers between devices: 0 us -> 20 us
  matrix products: 9.55 us -> 25.2 us
  between operations: 0.29 us -> 15.1 us
  local copies, waits for them, and re-layouts: 4.51 us -> 12.7 us
  other arithmetic: 1.36 us -> 9.18 us
    all_to_all x14 -> x8, blocking collectives: 205 us -> 128 us  [a2a(): lax.all_to_all(array, axes, 0, 0, tiled=True)]
    all_to_all x0 -> x3, waiting for transfers between devices: none -> 48.5 us  [a2a(): lax.all_to_all(array, axes, 0, 0, tiled=True)]
    all_to_all x0 -> x3, starting transfers between devices: none -> 19.9 us  [a2a(): lax.all_to_all(array, axes, 0, 0, tiled=True)]
    all_gather x6 -> x2, blocking collectives: 27.8 us -> 11 us  [over_columns(): both = lax.all_gather(array[None], 'core', tiled=True)]
    dot_general x16 -> x17, matrix products: 8.55 us -> 23.4 us  [the longest x8 14.5 us: mt(): lax.dot_general(panel, matrix.astype(jnp.float32), (((1,), (1,)), ((), ()...]
  transfers between devices with their start and end apart: 0 -> 5, of which waited for: 0 -> 3; matrix products, arithmetic and copies ran while one was open for 0% -> 7% of each run, Pallas kernels for 0% -> 0%
where the time goes in v4:
time: 272 us; the launch traced here: 270 us
  blocking collectives  139 us (51%)
  waiting for transfers between devices  48.6 us (18%)
  matrix products  25.2 us (9%)
  starting transfers between devices  20 us (7%)
  between operations  15.1 us (6%)
  local copies, waits for them, and re-layouts  12.7 us (5%)
  other arithmetic  9.18 us (3%)
    all_to_all x8, blocking collectives, a2a(): lax.all_to_all(array, axes, 0, 0, tiled=True)  128 us
    all_to_all x3, waiting for transfers between devices, a2a(): lax.all_to_all(array, axes, 0, 0, tiled=True)  48.5 us
    all_to_all x3, starting transfers between devices, a2a(): lax.all_to_all(array, axes, 0, 0, tiled=True)  19.9 us
    dot_general x8, matrix products, mt(): lax.dot_general(panel, matrix.astype(jnp.float32), (((1,), (1,)), ((), ()...  14.5 us
    all_gather x2, blocking collectives, over_columns(): both = lax.all_gather(array[None], 'core', tiled=True)  11 us
  transfers between devices with their start and end apart: 5, of which 3 were waited for; matrix products, arithmetic and copies ran while one was open for 7% of the time, Pallas kernels for 0%

profile of v4, /device:TPU:1, one launch (start us, length us, event | category | flops | bytes accessed | tf_op | source)
XLA Modules:
  0.0 269.7 jit_solution(7768904584808392175)
XLA Ops:
  6.5 1.0 fusion.23
  9.4 1.3 dynamic_slice.30
  12.9 1.1 constant_dynamic-slice_fusion.3
  14.1 1.6 fusion.7
  15.9 1.3 copy.46
  18.2 1.2 compare_select_fusion
  21.0 38.9 %all_to_all.55 = f32[16,32,512]{2,1,0:T(8,128)S(1)} all-to-all(f32[16,32,512]{2,1,0:T(8,128)} %bitcast.120), channel_id=1, replica_groups=mesh['xh'=2,'xl'=2,'z'=8,'y'=8,'core'=2] {'y','core'}, dimensions={0} | all-to-all | bytes 2097152 | tf_op jit(solution)/shard_map/all_to_all | solution.py:45
  62.2 1.1 pad_maximum_fusion
  63.3 9.3 %all-to-all-start.5 = ((f32[16,32,512]{2,1,0:T(8,128)}), f32[16,32,512]{2,1,0:T(8,128)S(1)}, u32[]{:S(2)}, u32[]{:S(2)}) async-start(f32[16,32,512]{2,1,0:T(8,128)} %pad_maximum_fusion), calls=%async_computation.5 | async-start | bytes 2097152 | tf_op jit(solution)/shard_map/all_to_all | solution.py:45
  72.6 1.8 fusion.2
  74.4 25.3 %all-to-all-done.5 = f32[16,32,512]{2,1,0:T(8,128)S(1)} async-done(((f32[16,32,512]{2,1,0:T(8,128)}), f32[16,32,512]{2,1,0:T(8,128)S(1)}, u32[]{:S(2)}, u32[]{:S(2)}) %all-to-all-start.5) | async-done | bytes 1048608 | tf_op jit(solution)/shard_map/all_to_all | solution.py:45
  99.7 6.4 %all-to-all-start.1 = ((f32[32,32,128]{2,1,0:T(8,128)}), f32[32,32,128]{2,1,0:T(8,128)S(1)}, u32[]{:S(2)}, u32[]{:S(2)}) async-start(f32[32,32,128]{2,1,0:T(8,128)} %fusion.2), calls=%async_computation.1 | async-start | bytes 1048576 | tf_op jit(solution)/shard_map/all_to_all | solution.py:45
  107.1 13.7 %all-to-all-done.1 = f32[32,32,128]{2,1,0:T(8,128)S(1)} async-done(((f32[32,32,128]{2,1,0:T(8,128)}), f32[32,32,128]{2,1,0:T(8,128)S(1)}, u32[]{:S(2)}, u32[]{:S(2)}) %all-to-all-start.1) | async-done | bytes 524320 | tf_op jit(solution)/shard_map/all_to_all | solution.py:45
  121.1 12.9 %all_to_all.56 = f32[16,1,256]{2,1,0:T(1,128)S(1)} all-to-all(f32[16,1,256]{2,1,0:T(1,128)S(1)} %reshape.151), channel_id=1, replica_groups=mesh['xh'=2,'xl'=2,'z'=8,'y'=8,'core'=2] {'y','core'}, dimensions={0} | all-to-all | bytes 32768 | tf_op jit(solution)/shard_map/all_to_all | solution.py:45
  135.9 4.2 %fusion.41 = f32[8,1024]{1,0:T(8,128)} fusion(f32[8,512]{1,0:T(8,128)S(1)} %fusion.40, f32[1024,512]{1,0:T(8,128)} %all-gather.5.cloned.1.call-done), kind=kOutput, calls=%fused_computation.93 | convolution fusion | flops 50331648 | bytes 2146304 | tf_op jit(solution)/shard_map/dot_general | solution.py:34
  141.1 1.0 slice_reduce_fusion.1
  143.0 0.9 mul.214
  144.7 13.1 %all_to_all.57 = f32[16,8,512]{2,1,0:T(8,128)} all-to-all(f32[16,8,512]{2,1,0:T(8,128)S(1)} %multiply_add_fusion), channel_id=1, replica_groups=mesh['xh'=2,'xl'=2,'z'=8,'y'=8,'core'=2] {'xl','z'}, dimensions={0} | all-to-all | bytes 524288 | tf_op jit(solution)/shard_map/all_to_all | solution.py:45
  157.8 1.0 reduce_sum.93
  159.2 1.8 fusion.42
  161.4 12.3 %all_to_all.58 = f32[8,8,512]{2,1,0:T(8,128)S(1)} all-to-all(f32[8,8,512]{2,1,0:T(8,128)S(1)} %broadcast_in_dim.31), channel_id=1, replica_groups=mesh['xh'=2,'xl'=2,'z'=8,'y'=8,'core'=2] {'z'}, dimensions={0} | all-to-all | bytes 262144 | tf_op jit(solution)/shard_map/all_to_all | solution.py:45
  174.4 5.9 %convolution_bitcast_fusion.1 = f32[2,8,16,32]{3,1,0,2:T(8,128)S(1)} fusion(f32[16,2,32,512]{3,2,1,0:T(8,128)} %bitcast.116, f32[8,512]{1,0:T(8,128)S(1)} %multiply_reduce_fusion.8), kind=kOutput, calls=%fused_computation.4 | convolution fusion | flops 50331648 | bytes 2146304 | tf_op jit(solution)/shard_map/dot_general | solution.py:34
  181.5 10.4 %all_to_all.59 = f32[16,8,512]{2,1,0:T(8,128)S(1)} all-to-all(f32[16,8,512]{2,1,0:T(8,128)S(1)} %broadcast_in_dim.32), channel_id=1, replica_groups=mesh['xh'=2,'xl'=2,'z'=8,'y'=8,'core'=2] {'xl','z'}, dimensions={0} | all-to-all | bytes 524288 | tf_op jit(solution)/shard_map/all_to_all | solution.py:45
  192.0 1.8 fusion.9
  194.8 5.8 %all-gather = f32[16,512]{1,0:T(8,128)S(1)} all-gather(f32[8,512]{1,0:T(8,128)S(1)} %convolution_select_fusion.2), channel_id=2, replica_groups=mesh['xh'=2,'xl'=2,'z'=8,'y'=8,'core'=2] {'core'}, dimensions={0}, use_global_device_ids=true | all-gather | bytes 49152 | tf_op jit(solution)/shard_map/all_gather | solution.py:53
  200.6 14.8 %all_to_all.60 = f32[8,2,8,512]{3,2,1,0:T(8,128)S(1)} all-to-all(f32[8,2,8,512]{3,2,1,0:T(8,128)S(1)} %broadcast_in_dim.34), channel_id=1, replica_groups=mesh['xh'=2,'xl'=2,'z'=8,'y'=8,'core'=2] {'y'}, dimensions={0} | all-to-all | bytes 524288 | tf_op jit(solution)/shard_map/all_to_all | solution.py:45
  215.9 14.9 %all_to_all.61 = f32[32,16,128]{2,1,0:T(8,128)S(1)} all-to-all(f32[32,16,128]{2,1,0:T(8,128)S(1)} %bitcast.123), channel_id=1, replica_groups=mesh['xh'=2,'xl'=2,'z'=8,'y'=8,'core'=2] {'xh','xl','z'}, dimensions={0} | all-to-all | bytes 524288 | tf_op jit(solution)/shard_map/all_to_all | solution.py:45
  230.9 5.2 %all-gather.1 = f32[32,128]{1,0:T(8,128)S(1)} all-gather(f32[16,128]{1,0:T(8,128)S(1)} %multiply_reduce_fusion.5), channel_id=3, replica_groups=mesh['xh'=2,'xl'=2,'z'=8,'y'=8,'core'=2] {'core'}, dimensions={0}, use_global_device_ids=true | all-gather | bytes 24576 | tf_op jit(solution)/shard_map/all_gather | solution.py:53
  236.1 10.9 %all_to_all.62 = f32[8,2,16,128]{3,2,1,0:T(8,128)S(1)} all-to-all(f32[8,2,16,128]{3,2,1,0:T(8,128)S(1)} %broadcast_in_dim.36), channel_id=1, replica_groups=mesh['xh'=2,'xl'=2,'z'=8,'y'=8,'core'=2] {'y'}, dimensions={0} | all-to-all | bytes 262144 | tf_op jit(solution)/shard_map/all_to_all | solution.py:45
  247.7 4.2 %all-to-all-start.10 = ((f32[32,16,128]{2,1,0:T(8,128)}), f32[32,16,128]{2,1,0:T(8,128)S(1)}, u32[]{:S(2)}, u32[]{:S(2)}) async-start(f32[32,16,128]{2,1,0:T(8,128)} %concatenate.23), calls=%async_computation.10 | async-start | bytes 524288 | tf_op jit(solution)/shard_map/all_to_all | solution.py:45
  252.0 9.5 %all-to-all-done.10 = f32[32,16,128]{2,1,0:T(8,128)S(1)} async-done(((f32[32,16,128]{2,1,0:T(8,128)}), f32[32,16,128]{2,1,0:T(8,128)S(1)}, u32[]{:S(2)}, u32[]{:S(2)}) %all-to-all-start.10) | async-done | bytes 262176 | tf_op jit(solution)/shard_map/all_to_all | solution.py:45
  261.6 1.3 fusion
  (105 shorter events, 18.9 us)
Async XLA Ops:
  6.5 7.5 %copy-start = (bf16[1,1,512,512]{3,2,1,0:T(8,128)(2,1)S(1)}, bf16[1,1,512,512]{3,2,1,0:T(8,128)(2,1)}, u32[]{:S(2)}) copy-start(bf16[1,1,512,512]{3,2,1,0:T(8,128)(2,1)} %param.9) | copy-start | bytes 1572868
  6.5 9.1 %copy-start.4 = (bf16[1,1,1,2,512,512]{5,4,3,2,1,0:T(8,128)(2,1)S(1)}, bf16[1,1,1,2,512,512]{5,4,3,2,1,0:T(8,128)(2,1)}, u32[]{:S(2)}) copy-start(bf16[1,1,1,2,512,512]{5,4,3,2,1,0:T(8,128)(2,1)} %param.7) | copy-start | bytes 3145732
  6.5 129.4 %all-gather.5.cloned.1.call-start = ((), (), s32[]{:S(2)}) async-start(), calls=%async_computation.11 | async-start | bytes 2228224 | tf_op jit(solution)/shard_map/all_gather | solution.py:119
  15.6 1.5 copy-start.3
  15.8 3.6 %copy-start.15 = (pred[32,1]{0,1:T(4,128)(4,1)S(1)}, pred[32,1]{0,1:T(4,128)(4,1)}, u32[]{:S(2)}) copy-start(pred[32,1]{0,1:T(4,128)(4,1)} %constant.87) | copy-start | bytes 100
  15.8 4.3 %copy-start.13 = (pred[16,1]{0,1:T(4,128)(4,1)S(1)}, pred[16,1]{0,1:T(4,128)(4,1)}, u32[]{:S(2)}) copy-start(pred[16,1]{0,1:T(4,128)(4,1)} %constant.91) | copy-start | bytes 52
  15.8 4.2 %copy-start.14 = (pred[16,1]{0,1:T(4,128)(4,1)S(1)}, pred[16,1]{0,1:T(4,128)(4,1)}, u32[]{:S(2)}) copy-start(pred[16,1]{0,1:T(4,128)(4,1)} %constant.90) | copy-start | bytes 52
  15.8 4.3 %copy-start.11 = (pred[1,16]{0,1:T(8,128)(4,1)S(1)}, pred[1,16]{0,1:T(8,128)(4,1)}, u32[]{:S(2)}) copy-start(pred[1,16]{0,1:T(8,128)(4,1)} %constant.89) | copy-start | bytes 52
  15.8 4.3 %copy-start.12 = (pred[1,16]{0,1:T(8,128)(4,1)S(1)}, pred[1,16]{0,1:T(8,128)(4,1)}, u32[]{:S(2)}) copy-start(pred[1,16]{0,1:T(8,128)(4,1)} %constant.88) | copy-start | bytes 52
  20.4 0.6 copy-start.6
  20.4 0.6 copy-start.8
  63.3 36.4 %all-to-all-start.5 = ((f32[16,32,512]{2,1,0:T(8,128)}), f32[16,32,512]{2,1,0:T(8,128)S(1)}, u32[]{:S(2)}, u32[]{:S(2)}) async-start(f32[16,32,512]{2,1,0:T(8,128)} %pad_maximum_fusion), calls=%async_computation.5 | async-start | bytes 2097152 | tf_op jit(solution)/shard_map/all_to_all | solution.py:45
  99.7 21.1 %all-to-all-start.1 = ((f32[32,32,128]{2,1,0:T(8,128)}), f32[32,32,128]{2,1,0:T(8,128)S(1)}, u32[]{:S(2)}, u32[]{:S(2)}) async-start(f32[32,32,128]{2,1,0:T(8,128)} %fusion.2), calls=%async_computation.1 | async-start | bytes 1048576 | tf_op jit(solution)/shard_map/all_to_all | solution.py:45
  106.1 68.2 %all-gather.7.cloned.1.call-start = ((), (), s32[]{:S(2)}) async-start(), calls=%async_computation.12 | async-start | bytes 2228224 | tf_op jit(solution)/shard_map/all_gather | solution.py:119
  135.9 23.3 %copy-start.1 = (f32[1024,512]{1,0:T(8,128)S(1)}, f32[1024,512]{1,0:T(8,128)}, u32[]{:S(2)}) copy-start(f32[1024,512]{1,0:T(8,128)} %all-gather.5.cloned.1.call-done) | copy-start | bytes 6291460
  174.4 17.5 %copy-start.7 = (f32[16]{0:T(128)S(1)}, f32[16]{0:T(128)}, u32[]{:S(2)}) copy-start(f32[16]{0:T(128)} %copy-done.6) | copy-start | bytes 196
  174.4 17.5 %copy-start.9 = (f32[16]{0:T(128)S(1)}, f32[16]{0:T(128)}, u32[]{:S(2)}) copy-start(f32[16]{0:T(128)} %copy-done.8) | copy-start | bytes 196
  174.4 17.6 %copy-start.2 = (f32[1024,512]{1,0:T(8,128)S(1)}, f32[1024,512]{1,0:T(8,128)}, u32[]{:S(2)}) copy-start(f32[1024,512]{1,0:T(8,128)} %all-gather.7.cloned.1.call-done) | copy-start | bytes 6291460
  193.8 21.6 %copy-start.5 = (bf16[1,1,1,2,512,512]{5,4,3,2,1,0:T(8,128)(2,1)S(1)}, bf16[1,1,1,2,512,512]{5,4,3,2,1,0:T(8,128)(2,1)}, u32[]{:S(2)}) copy-start(bf16[1,1,1,2,512,512]{5,4,3,2,1,0:T(8,128)(2,1)} %param.7) | copy-start | bytes 3145732
  194.1 36.8 %copy-start.10 = (f32[32]{0:T(128)S(1)}, f32[32]{0:T(128)}, u32[]{:S(2)}) copy-start(f32[32]{0:T(128)} %get-tuple-element.40) | copy-start | bytes 388
  247.7 13.8 %all-to-all-start.10 = ((f32[32,16,128]{2,1,0:T(8,128)}), f32[32,16,128]{2,1,0:T(8,128)S(1)}, u32[]{:S(2)}, u32[]{:S(2)}) async-start(f32[32,16,128]{2,1,0:T(8,128)} %concatenate.23), calls=%async_computation.10 | async-start | bytes 524288 | tf_op jit(solution)/shard_map/all_to_all | solution.py:45
Sparse Core Ops, SparseCore 0:
  60.9 40.3 all-gather.4
  109.1 38.8 all-gather.6

commit v5 on v3

v5 whole, which is shorter than its diff:
```python
import functools

import jax
import jax.numpy as jnp
from jax import lax
from jax.experimental import pallas as pl
from jax.experimental.pallas import tpu as pltpu
from jax.sharding import Mesh, PartitionSpec as P

LEVELS = 4
HALF = ("xl", "z")
ROW = ("xh", "xl", "z")
COL = ("y", "core")
HIGHEST = lax.Precision.HIGHEST
F32 = jnp.float32
BF16 = jnp.bfloat16
ROOMY = pltpu.CompilerParams(vmem_limit_bytes=40 * 1024 * 1024)

FROM_LEAF, FROM_LOW, PICK_TWO, PICK_THREE, BELOW, SEND_TWO, SEND_THREE, SEND_ROOT, FLAGS = range(9)


def call(body, shape, specs, *args, scratch=()):
    many = isinstance(shape, tuple)
    out = [pl.BlockSpec(memory_space=pltpu.VMEM)] * len(shape) if many else pl.BlockSpec(
        memory_space=pltpu.VMEM
    )
    return pl.pallas_call(
        body,
        out_shape=shape,
        in_specs=specs,
        out_specs=out,
        scratch_shapes=list(scratch),
        compiler_params=ROOMY,
    )(*args)


VM = pl.BlockSpec(memory_space=pltpu.VMEM)
SM = pl.BlockSpec(memory_space=pltpu.SMEM)
HB = pl.BlockSpec(memory_space=pl.ANY)


def fetch(blocks, held, arrived, start):
    copy = pltpu.make_async_copy(blocks.at[:, pl.ds(start, held.shape[1])], held, arrived)
    copy.start()
    return copy


def room(blocks, slots):
    shape = (blocks.shape[0], slots) + blocks.shape[2:]
    return [pltpu.VMEM(shape, F32), pltpu.SemaphoreType.DMA]


def shape_of(*dims, kind=F32):
    return jax.ShapeDtypeStruct(dims, kind)


def three(panel):
    high = panel.astype(BF16).astype(F32)
    rest = panel - high
    mid = rest.astype(BF16).astype(F32)
    return high, mid, rest - mid


def mt(panel, matrix):
    rows = panel.shape[0]
    parts = jnp.concatenate(three(panel), 0).astype(BF16)
    product = lax.dot_general(
        parts, matrix, (((1,), (1,)), ((), ())), preferred_element_type=F32
    )
    return product[:rows] + product[rows:2 * rows] + product[2 * rows:]


def table_kernel(at, parents_row, parents_col, mask, mask_t, out):
    count = mask.shape[0]
    top = count // 2
    row, col = at[0], at[1]
    down = lax.broadcasted_iota(jnp.int32, (count, count), 0)
    across = lax.broadcasted_iota(jnp.int32, (count, count), 1)
    step = (parents_col[...] == across).astype(F32)
    step_t = (parents_row[...] == down).astype(F32)
    identity = (down == across).astype(F32)
    anc = power = anc_t = power_t = identity
    for _ in range(LEVELS - 1):
        power = jnp.dot(power, step, preferred_element_type=F32)
        power_t = jnp.dot(step_t, power_t, preferred_element_type=F32)
        anc = anc + power
        anc_t = anc_t + power_t
    anc = jnp.minimum(anc, 1.0)
    anc_t = jnp.minimum(anc_t, 1.0)
    weights = mask[...].astype(F32) * (1.0 - identity)
    weights_t = mask_t[...].astype(F32) * (1.0 - identity)

    def line(matrix, index):
        return jnp.sum(jnp.where(down == index, matrix, 0.0), axis=0, keepdims=True)

    def level(ids):
        total = jnp.zeros_like(ids)
        for depth in range(1, LEVELS):
            total = total + (ids >= count - count // 2**depth).astype(jnp.int32)
        return total

    levels = level(lax.broadcasted_iota(jnp.int32, (1, count), 1))
    mine = level(jnp.full((1, count), row, jnp.int32))
    two = (levels == 2).astype(F32)
    three_ = (levels == 3).astype(F32)
    one_mine = (mine == 1).astype(F32)
    two_mine = (mine == 2).astype(F32)
    late = (mine >= 2).astype(F32)
    use_row = line(weights * anc, row)
    above = line(anc, row)
    rows = [
        line(weights_t * anc_t, row) * (levels == 0).astype(F32),
        line(weights_t * anc, col),
        use_row * two * one_mine,
        use_row * three_ * (one_mine + two_mine),
        line(weights * anc_t, row) * late,
        above * two * one_mine,
        above * three_ * one_mine,
        above * three_ * two_mine,
        jnp.where(
            lax.broadcasted_iota(jnp.int32, (1, count), 1) == 0,
            (mine >= 1).astype(F32),
            (mine == 3).astype(F32),
        ),
    ]
    rows = rows + [jnp.zeros((1, count), F32)] * (out.shape[0] - len(rows))
    out[...] = jnp.concatenate(rows, 0)


def first_kernel(table, slices, y0, out, local_a, local_b):
    top, piece, width = slices.shape
    nrhs = y0.shape[1]
    half, quarter = top // 2, top // 4
    is_root = table[FLAGS, 1]
    own = slices[...].reshape(top * piece, width).astype(BF16)
    parts = jnp.concatenate(three(y0[...]), 1).astype(BF16)
    product = jnp.dot(own, parts, preferred_element_type=F32)
    product = product[:, :nrhs] + product[:, nrhs:2 * nrhs] + product[:, 2 * nrhs:]
    out[:top] = jnp.zeros((top, piece, nrhs), F32)
    out[top:] = product.reshape(top, piece, nrhs)
    for slot in range(quarter):
        total = (table[BELOW, top + half + slot] * is_root) * slices[half + slot]
        if slot < 2:
            line = (PICK_TWO, PICK_THREE)[slot]
            start = half + slot * quarter
            for k in range(start, start + quarter):
                total = total + table[line, top + k] * slices[k]
        local_a[0, slot] = total
    for k in range(half):
        local_b[0, k] = table[BELOW, top + k] * slices[k]


def leaf_kernel(table, got, out):
    total = table[FROM_LEAF, 0] * got[0]
    for k in range(1, got.shape[0] // 2):
        total = total + table[FROM_LEAF, k] * got[k]
    out[...] = total.T


def level_one_kernel(table, got, base_t, up, blocks, rest_out, y_out, out, held, arrived):
    copy = fetch(blocks, held, arrived, 0)
    pieces, rhs, piece = got.shape
    top = out.shape[0]
    width = base_t.shape[1]
    part = jnp.concatenate([got[k] for k in range(pieces)], 1)
    rest = base_t[...] - part * table[FLAGS, 0]
    y = mt(rest, up[...])
    rest_out[...] = rest
    y_out[...] = y
    copy.wait()
    a = mt(y, held[:, 0].reshape(width, width).astype(BF16))
    b = mt(y, held[:, 1].reshape(width, width).astype(BF16))
    for k in range(top):
        out[k] = table[SEND_TWO, top + k] * a + table[SEND_THREE, top + k] * b


def level_two_kernel(table, got, rest_in, up, blocks, rest_out, y_out, out, held, arrived):
    copy = fetch(blocks, held, arrived, 1)
    width = rest_in.shape[1]
    nz = out.shape[0]
    count = table.shape[1]
    rest = rest_in[...] - jnp.sum(got[...], 0)
    y = mt(rest, up[...])
    rest_out[...] = rest
    y_out[...] = y
    copy.wait()
    b = mt(y, held[:, 0].reshape(width, width).astype(BF16))
    for k in range(nz):
        out[k] = table[SEND_ROOT, count - nz + k] * b


def level_three_kernel(table, got, rest_in, up, low, blocks, y_out, out, held, arrived):
    copy = fetch(blocks, held, arrived, 0)
    width = rest_in.shape[1]
    nz = out.shape[0]
    slots = blocks.shape[1]
    rest = rest_in[...] - jnp.sum(got[...], 0)
    y = mt(rest, up[...])
    y_out[...] = y
    x = mt(y, low[...]) * table[FLAGS, 1]
    copy.wait()
    for k in range(slots):
        out[k] = mt(x, held[:, k].reshape(width, width).astype(BF16))
    for k in range(slots, nz):
        out[k] = jnp.zeros_like(x)


def down_kernel(slots, got, y_in, low, blocks, rest_out, out, x_now):
    step = pl.program_id(0)
    width = y_in.shape[1]

    @pl.when(step == 0)
    def _():
        rest = y_in[...] - jnp.sum(got[...], 0)
        rest_out[...] = rest
        x_now[...] = mt(rest, low[...])

    @pl.when(step < slots)
    def _():
        out[0] = mt(x_now[...], blocks[...].reshape(width, width).astype(BF16))

    @pl.when(step >= slots)
    def _():
        out[0] = jnp.zeros_like(x_now)


def last_kernel(got, rest_in, low, out):
    out[0] = mt(rest_in[...] - jnp.sum(got[...], 0), low[...])


def a2a(array, axes):
    array = lax.optimization_barrier(array)
    return lax.optimization_barrier(lax.all_to_all(array, axes, 0, 0, tiled=True))


def copies(array, times):
    return jnp.broadcast_to(array[None], (times,) + array.shape)


def over_columns(array, ny):
    both = lax.all_gather(array, "core", tiled=True)
    return a2a(copies(both, ny), "y")


def per_device(factor, rhs, upper_inverse, lower_inverse, parents, block_mask):
    ny, nc, nz = lax.axis_size("y"), lax.axis_size("core"), lax.axis_size("z")
    ncol = ny * nc
    slot0 = factor[0, 0, 0, 0]
    slot1 = factor[0, 0, 0, 1]
    base = rhs[0, 0]
    up = upper_inverse[0, 0]
    low = lower_inverse[0, 0]
    width, nrhs = base.shape
    piece = width // ncol
    mine = nrhs // ncol
    count = parents.shape[0]
    top = count // 2
    half, quarter = top // 2, top // 4
    small = width // count
    row = lax.axis_index(ROW)
    col = lax.axis_index(COL)
    is_high = lax.axis_index("xh") == 1

    sent = slot1.T.astype(F32).reshape(ncol, piece, width)
    table = call(
        table_kernel, shape_of(16, count), [SM, VM, VM, VM, VM],
        jnp.stack([row, col]).astype(jnp.int32), parents[None, :], parents[:, None],
        block_mask, block_mask.T,
    )
    y0 = jnp.dot(up.astype(F32), base, precision=HIGHEST)
    base_t = lax.dynamic_slice_in_dim(base.T, col * mine, mine, 0)

    slices = lax.all_to_all(sent, COL, 0, 0, tiled=True)
    table, y0, base_t, slices = lax.optimization_barrier((table, y0, base_t, slices))
    out, local_a, local_b = call(
        first_kernel,
        (
            shape_of(count, piece, nrhs),
            shape_of(1, quarter, piece, width),
            shape_of(1, half, piece, width),
        ),
        [SM, VM, VM], table, slices, y0,
    )
    blocks_a = lax.all_gather(local_a, COL, tiled=True)
    blocks_b = lax.all_gather(local_b, COL, tiled=True)

    part = call(leaf_kernel, shape_of(nrhs, piece), [SM, VM], table, a2a(out, ROW))
    got = a2a(part.reshape(ncol, mine, piece), COL)
    panel = shape_of(mine, width)
    rest, y, out = call(
        level_one_kernel, (panel, panel, shape_of(top, mine, width)), [SM, VM, VM, VM, HB],
        table, got, base_t, up, blocks_a, scratch=room(blocks_a, 2),
    )
    rest, y, out = call(
        level_two_kernel, (panel, panel, shape_of(nz, mine, width)), [SM, VM, VM, VM, HB],
        table, a2a(out, HALF), rest, up, blocks_a, scratch=room(blocks_a, 1),
    )
    y, out = call(
        level_three_kernel, (panel, shape_of(nz, mine, width)), [SM, VM, VM, VM, VM, HB],
        table, a2a(out, "z"), rest, up, low, blocks_a, scratch=room(blocks_a, quarter),
    )
    got = a2a(out, "z")
    whole = lambda array: pl.BlockSpec(array.shape, lambda k: (0,) * array.ndim)
    rest, out = pl.pallas_call(
        functools.partial(down_kernel, half),
        out_shape=(panel, shape_of(top, mine, width)),
        grid=(top,),
        in_specs=[
            whole(got), whole(y), whole(low),
            pl.BlockSpec((ncol, 1, piece, width), lambda k: (0, jnp.minimum(k, half - 1), 0, 0)),
        ],
        out_specs=(
            pl.BlockSpec((mine, width), lambda k: (0, 0)),
            pl.BlockSpec((1, mine, width), lambda k: (k, 0, 0)),
        ),
        scratch_shapes=[pltpu.VMEM((mine, width), F32)],
        compiler_params=ROOMY,
    )(got, y, low, blocks_b)
    x = call(last_kernel, shape_of(1, mine, width), [VM, VM, VM], a2a(out, HALF), rest, low)
    x = over_columns(x, ny).reshape(nrhs, width)
    full = lax.dot_general(
        slot0.astype(F32), x, (((0,), (1,)), ((), ())), precision=HIGHEST
    )
    got = a2a(full.reshape(count, small, nrhs), ROW)
    part = jnp.sum(table[FROM_LOW][:, None, None] * got, axis=0)
    every = over_columns(part[None], ny).reshape(ncol, small, nrhs)
    got = a2a(jnp.concatenate([every, jnp.zeros_like(every)], 0), ROW).reshape(width, nrhs)
    below = jnp.dot(low.astype(F32), y0 - got, precision=HIGHEST)
    return jnp.where(is_high, x.T, below)[None, None]


def solution(mesh):
    grid = Mesh(mesh.devices.reshape(2, 2, 8, 8, 2), ("xh", "xl", "z", "y", "core"))
    placed = (
        P(ROW, None, COL, None, None, None),
        P(ROW, None, None, None),
        P(ROW, None, None, None),
        P(ROW, None, None, None),
        P(),
        P(),
    )
    return jax.shard_map(
        per_device,
        mesh=grid,
        in_specs=placed,
        out_specs=P(ROW, None, None, None),
        check_vma=False,
    )
```

time: 251 us -> 254 us (1.012)
  blocking collectives: 233 us -> 130 us
  waiting for transfers between devices: 0 us -> 54.2 us
  starting transfers between devices: 0 us -> 21.1 us
  between operations: 0.29 us -> 13.6 us
  Pallas kernels: 0 us -> 12.7 us
  local copies, waits for them, and re-layouts: 4.51 us -> 15.5 us
  matrix products: 9.55 us -> 2.71 us
    all_to_all x14 -> x8, blocking collectives: 205 us -> 121 us  [a2a(): lax.all_to_all(array, axes, 0, 0, tiled=True)]
    all_to_all x0 -> x3, waiting for transfers between devices: none -> 41.4 us  [the longest x1 22.1 us: per_device(): slices = lax.all_to_all(sent, COL, 0, 0, tiled=True)]
    all_to_all x0 -> x3, starting transfers between devices: none -> 21 us  [the longest x2 10.7 us: a2a(): lax.all_to_all(array, axes, 0, 0, tiled=True)]
    all_gather x6 -> x2, blocking collectives: 27.8 us -> 8.74 us  [over_columns(): both = lax.all_gather(array, 'core', tiled=True)]
    pallas_call x0 -> x8, Pallas kernels: none -> 12.7 us  [the longest x7 9.48 us: call(): pl.pallas_call(body, out_shape=shape, in_specs=specs, out_specs=out, scra...]
    all_gather x0 -> x2, waiting for transfers between devices: none -> 12.1 us  [the longest x1 9.92 us: per_device(): blocks_b = lax.all_gather(local_b, COL, tiled=True)]
    unnamed x14 -> x21, local copies, waits for them, and re-layouts: 2.93 us -> 10.2 us
    dot_general x16 -> x3, matrix products: 8.55 us -> 2.71 us  [the longest x1 1.64 us: per_device(): y0 = jnp.dot(up.astype(F32), base, precision=HIGHEST)]
  transfers between devices with their start and end apart: 0 -> 5, of which waited for: 0 -> 5; matrix products, arithmetic and copies ran while one was open for 0% -> 2% of each run, Pallas kernels for 0% -> 3%
where the time goes in v5:
time: 254 us; the launch traced here: 252 us
  blocking collectives  130 us (51%)
  waiting for transfers between devices  54.2 us (21%)
  starting transfers between devices  21.1 us (8%)
  local copies, waits for them, and re-layouts  15.5 us (6%)
  between operations  13.6 us (5%)
  Pallas kernels  12.7 us (5%)
  matrix products  2.71 us (1%)
    all_to_all x8, blocking collectives, a2a(): lax.all_to_all(array, axes, 0, 0, tiled=True)  121 us
    all_to_all x1, waiting for transfers between devices, per_device(): slices = lax.all_to_all(sent, COL, 0, 0, tiled=True)  22.1 us
    all_to_all x2, waiting for transfers between devices, a2a(): lax.all_to_all(array, axes, 0, 0, tiled=True)  19.3 us
    all_to_all x2, starting transfers between devices, a2a(): lax.all_to_all(array, axes, 0, 0, tiled=True)  10.7 us
    all_to_all x1, starting transfers between devices, per_device(): slices = lax.all_to_all(sent, COL, 0, 0, tiled=True)  10.3 us
    unnamed x21, local copies, waits for them, and re-layouts  10.2 us
    all_gather x1, waiting for transfers between devices, per_device(): blocks_b = lax.all_gather(local_b, COL, tiled=True)  9.92 us
    pallas_call x7, Pallas kernels, call(): pl.pallas_call(body, out_shape=shape, in_specs=specs, out_specs=out, scra...  9.48 us
  transfers between devices with their start and end apart: 5, of which 5 were waited for; matrix products, arithmetic and copies ran while one was open for 2% of the time, Pallas kernels for 3%

profile of v5, /device:TPU:1, one launch (start us, length us, event | category | flops | bytes accessed | tf_op | source)
XLA Modules:
  0.0 251.7 jit_solution(7470963766963142791)
XLA Ops:
  6.5 1.2 convert_bitcast_fusion
  7.8 1.3 copy.21
  9.1 10.3 %all-to-all-start = ((f32[16,32,512]{2,1,0:T(8,128)}), f32[16,32,512]{2,1,0:T(8,128)S(1)}, u32[]{:S(2)}, u32[]{:S(2)}) async-start(f32[16,32,512]{2,1,0:T(8,128)} %bitcast.11), calls=%async_computation | async-start | bytes 2097152 | tf_op jit(solution)/shard_map/all_to_all | solution.py:273
  22.7 1.0 shard_map.64.table
  23.7 1.6 fusion.3.y0
  25.4 22.1 %all-to-all-done.slices = f32[16,32,512]{2,1,0:T(8,128)S(1)} async-done(((f32[16,32,512]{2,1,0:T(8,128)}), f32[16,32,512]{2,1,0:T(8,128)S(1)}, u32[]{:S(2)}, u32[]{:S(2)}) %all-to-all-start) | async-done | bytes 1048608 | tf_op jit(solution)/shard_map/all_to_all | solution.py:273
  47.4 2.0 shard_map.65
  50.2 27.5 %all_to_all.55.got = f32[32,32,128]{2,1,0:T(8,128)S(1)} all-to-all(f32[32,32,128]{2,1,0:T(8,128)S(1)} %get-tuple-element.23), channel_id=1, replica_groups=mesh['xh'=2,'xl'=2,'z'=8,'y'=8,'core'=2] {'xh','xl','z'}, dimensions={0} | all-to-all | bytes 1048576 | tf_op jit(solution)/shard_map/all_to_all | solution.py:233
  78.6 11.4 %all_to_all.56 = f32[16,1,256]{2,1,0:T(1,128)S(1)} all-to-all(f32[16,1,256]{2,1,0:T(1,128)S(1)} %reshape.43), channel_id=1, replica_groups=mesh['xh'=2,'xl'=2,'z'=8,'y'=8,'core'=2] {'y','core'}, dimensions={0} | all-to-all | bytes 32768 | tf_op jit(solution)/shard_map/all_to_all | solution.py:233
  91.4 2.2 all-gather.4.cloned.1.call-done.blocks
  93.5 2.2 copy-done.1
  95.7 1.7 shard_map.67
  97.4 16.7 %all_to_all.57.got = f32[16,8,512]{2,1,0:T(8,128)S(1)} all-to-all(f32[16,8,512]{2,1,0:T(8,128)S(1)} %get-tuple-element.26), channel_id=1, replica_groups=mesh['xh'=2,'xl'=2,'z'=8,'y'=8,'core'=2] {'xl','z'}, dimensions={0} | all-to-all | bytes 524288 | tf_op jit(solution)/shard_map/all_to_all | solution.py:233
  114.1 2.3 copy-done.2
  116.4 1.6 shard_map.68
  118.0 12.1 %all_to_all.58.got = f32[8,8,512]{2,1,0:T(8,128)S(1)} all-to-all(f32[8,8,512]{2,1,0:T(8,128)S(1)} %get-tuple-element.28), channel_id=1, replica_groups=mesh['xh'=2,'xl'=2,'z'=8,'y'=8,'core'=2] {'z'}, dimensions={0} | all-to-all | bytes 262144 | tf_op jit(solution)/shard_map/all_to_all | solution.py:233
  130.2 2.2 shard_map.69
  132.3 10.4 %all_to_all.59.got = f32[8,8,512]{2,1,0:T(8,128)S(1)} all-to-all(f32[8,8,512]{2,1,0:T(8,128)S(1)} %get-tuple-element.30), channel_id=1, replica_groups=mesh['xh'=2,'xl'=2,'z'=8,'y'=8,'core'=2] {'z'}, dimensions={0} | all-to-all | bytes 262144 | tf_op jit(solution)/shard_map/all_to_all | solution.py:233
  142.7 9.9 %all-gather.6.cloned.1.call-done.blocks = f32[16,8,32,512]{3,2,1,0:T(8,128)} async-done(((f32[1,8,32,512]{3,2,1,0:T(8,128)}), f32[16,8,32,512]{3,2,1,0:T(8,128)}) %all-gather.6.cloned.1.call-update) | async-done | bytes 8388624 | tf_op jit(solution)/shard_map/all_gather | solution.py:285
  152.7 3.4 %copy-done.3 = f32[16,8,32,512]{3,2,1,0:T(8,128)S(1)} copy-done((f32[16,8,32,512]{3,2,1,0:T(8,128)S(1)}, f32[16,8,32,512]{3,2,1,0:T(8,128)}, u32[]{:S(2)}) %copy-start.3) | copy-done | bytes 8388632
  156.0 3.2 %shard_map.70 = (f32[8,512]{1,0:T(8,128)S(1)}, f32[16,8,512]{2,1,0:T(8,128)S(1)}) custom-call(f32[8,8,512]{2,1,0:T(8,128)S(1)} %all_to_all.59.got, f32[8,512]{1,0:T(8,128)S(1)} %get-tuple-element.31.y_in, bf16[512,512]{1,0:T(8,128)(2,1)S(1)} %bitcast.47, f32[16,8,32,512]{3,2,1,0:T(8,128)S(1)} %copy-done.3), custom_call_target="tpu_custom_call" | custom-call | tf_op jit(solution)/shard_map/pallas_call | solution.py:304
  159.3 16.9 %all_to_all.60.got = f32[16,8,512]{2,1,0:T(8,128)S(1)} all-to-all(f32[16,8,512]{2,1,0:T(8,128)S(1)} %get-tuple-element.33), channel_id=1, replica_groups=mesh['xh'=2,'xl'=2,'z'=8,'y'=8,'core'=2] {'xl','z'}, dimensions={0} | all-to-all | bytes 524288 | tf_op jit(solution)/shard_map/all_to_all | solution.py:233
  176.4 3.6 %all_gather.14 = f32[2,8,512]{2,1,0:T(8,128)S(1)} all-gather(f32[1,8,512]{2,1,0:T(8,128)S(1)} %shard_map.71), channel_id=1, replica_groups=mesh['xh'=2,'xl'=2,'z'=8,'y'=8,'core'=2] {'core'}, dimensions={0}, use_global_device_ids=true | all-gather | bytes 49152 | tf_op jit(solution)/shard_map/all_gather | solution.py:241
  180.1 15.2 %all_to_all.61 = f32[8,2,8,512]{3,2,1,0:T(8,128)S(1)} all-to-all(f32[8,2,8,512]{3,2,1,0:T(8,128)S(1)} %broadcast_in_dim.27), channel_id=1, replica_groups=mesh['xh'=2,'xl'=2,'z'=8,'y'=8,'core'=2] {'y'}, dimensions={0} | all-to-all | bytes 524288 | tf_op jit(solution)/shard_map/all_to_all | solution.py:233
  195.7 0.8 copy.22
  196.5 6.4 %all-to-all-start.8 = ((f32[32,16,128]{2,1,0:T(8,128)}), f32[32,16,128]{2,1,0:T(8,128)S(1)}, u32[]{:S(2)}, u32[]{:S(2)}) async-start(f32[32,16,128]{2,1,0:T(8,128)} %bitcast.18), calls=%async_computation.8 | async-start | bytes 524288 | tf_op jit(solution)/shard_map/all_to_all | solution.py:233
  202.9 9.6 %all-to-all-done.8 = f32[32,16,128]{2,1,0:T(8,128)S(1)} async-done(((f32[32,16,128]{2,1,0:T(8,128)}), f32[32,16,128]{2,1,0:T(8,128)S(1)}, u32[]{:S(2)}, u32[]{:S(2)}) %all-to-all-start.8) | async-done | bytes 262176 | tf_op jit(solution)/shard_map/all_to_all | solution.py:233
  212.7 5.1 %all-gather = f32[32,128]{1,0:T(8,128)S(1)} all-gather(f32[16,128]{1,0:T(8,128)S(1)} %multiply_reduce_fusion), channel_id=2, replica_groups=mesh['xh'=2,'xl'=2,'z'=8,'y'=8,'core'=2] {'core'}, dimensions={0}, use_global_device_ids=true | all-gather | bytes 24576 | tf_op jit(solution)/shard_map/all_gather | solution.py:241
  217.8 10.9 %all_to_all.62 = f32[8,2,16,128]{3,2,1,0:T(8,128)S(1)} all-to-all(f32[8,2,16,128]{3,2,1,0:T(8,128)S(1)} %broadcast_in_dim.29), channel_id=1, replica_groups=mesh['xh'=2,'xl'=2,'z'=8,'y'=8,'core'=2] {'y'}, dimensions={0} | all-to-all | bytes 262144 | tf_op jit(solution)/shard_map/all_to_all | solution.py:233
  229.4 4.2 %all-to-all-start.10 = ((f32[32,16,128]{2,1,0:T(8,128)}), f32[32,16,128]{2,1,0:T(8,128)S(1)}, u32[]{:S(2)}, u32[]{:S(2)}) async-start(f32[32,16,128]{2,1,0:T(8,128)} %concatenate.3), calls=%async_computation.10 | async-start | bytes 524288 | tf_op jit(solution)/shard_map/all_to_all | solution.py:233
  233.7 9.7 %all-to-all-done.10 = f32[32,16,128]{2,1,0:T(8,128)S(1)} async-done(((f32[32,16,128]{2,1,0:T(8,128)}), f32[32,16,128]{2,1,0:T(8,128)S(1)}, u32[]{:S(2)}, u32[]{:S(2)}) %all-to-all-start.10) | async-done | bytes 262176 | tf_op jit(solution)/shard_map/all_to_all | solution.py:233
  244.1 0.8 copy.23
  (38 shorter events, 8.4 us)
Async XLA Ops:
  6.5 13.0 %copy-start = (f32[1,1,512,128]{3,2,1,0:T(8,128)S(1)}, f32[1,1,512,128]{3,2,1,0:T(8,128)}, u32[]{:S(2)}) copy-start(f32[1,1,512,128]{3,2,1,0:T(8,128)} %param.7) | copy-start | bytes 786436
  6.5 87.0 %copy-start.4 = (bf16[1,1,512,512]{3,2,1,0:T(8,128)(2,1)S(1)}, bf16[1,1,512,512]{3,2,1,0:T(8,128)(2,1)}, u32[]{:S(2)}) copy-start(bf16[1,1,512,512]{3,2,1,0:T(8,128)(2,1)} %param.8) | copy-start | bytes 1572868
  9.1 38.3 %all-to-all-start = ((f32[16,32,512]{2,1,0:T(8,128)}), f32[16,32,512]{2,1,0:T(8,128)S(1)}, u32[]{:S(2)}, u32[]{:S(2)}) async-start(f32[16,32,512]{2,1,0:T(8,128)} %bitcast.11), calls=%async_computation | async-start | bytes 2097152 | tf_op jit(solution)/shard_map/all_to_all | solution.py:273
  19.4 110.7 %copy-start.5 = (bf16[1,1,512,512]{3,2,1,0:T(8,128)(2,1)S(1)}, bf16[1,1,512,512]{3,2,1,0:T(8,128)(2,1)}, u32[]{:S(2)}) copy-start(bf16[1,1,512,512]{3,2,1,0:T(8,128)(2,1)} %param.9) | copy-start | bytes 1572868
  19.4 74.1 %all-gather.4.cloned.1.call-start = ((), (), s32[]{:S(2)}) async-start(), calls=%async_computation.11 | async-start | bytes 4456448 | tf_op jit(solution)/shard_map/all_gather | solution.py:284
  21.4 0.7 copy-start.6
  22.1 0.7 copy-start.7
  49.5 103.2 %all-gather.6.cloned.1.call-start = ((), (), s32[]{:S(2)}) async-start(), calls=%async_computation.12 | async-start | bytes 8912896 | tf_op jit(solution)/shard_map/all_gather | solution.py:285
  93.5 2.2 copy-start.1
  114.1 2.3 copy-start.2
  130.2 65.1 %copy-start.8 = (bf16[1,1,1,2,512,512]{5,4,3,2,1,0:T(8,128)(2,1)S(1)}, bf16[1,1,1,2,512,512]{5,4,3,2,1,0:T(8,128)(2,1)}, u32[]{:S(2)}) copy-start(bf16[1,1,1,2,512,512]{5,4,3,2,1,0:T(8,128)(2,1)} %param.6) | copy-start | bytes 3145732
  152.7 3.4 %copy-start.3 = (f32[16,8,32,512]{3,2,1,0:T(8,128)S(1)}, f32[16,8,32,512]{3,2,1,0:T(8,128)}, u32[]{:S(2)}) copy-start(f32[16,8,32,512]{3,2,1,0:T(8,128)} %all-gather.6.cloned.1.call-done.blocks) | copy-start | bytes 25165828
  196.5 16.1 %all-to-all-start.8 = ((f32[32,16,128]{2,1,0:T(8,128)}), f32[32,16,128]{2,1,0:T(8,128)S(1)}, u32[]{:S(2)}, u32[]{:S(2)}) async-start(f32[32,16,128]{2,1,0:T(8,128)} %bitcast.18), calls=%async_computation.8 | async-start | bytes 524288 | tf_op jit(solution)/shard_map/all_to_all | solution.py:233
  229.4 13.9 %all-to-all-start.10 = ((f32[32,16,128]{2,1,0:T(8,128)}), f32[32,16,128]{2,1,0:T(8,128)S(1)}, u32[]{:S(2)}, u32[]{:S(2)}) async-start(f32[32,16,128]{2,1,0:T(8,128)} %concatenate.3), calls=%async_computation.10 | async-start | bytes 524288 | tf_op jit(solution)/shard_map/all_to_all | solution.py:233
Sparse Core Ops, SparseCore 0:
  49.6 43.8 all-gather.3
  95.6 56.9 all-gather.5

commit v6 on v5

--- a/solution.py
+++ b/solution.py
@@ -1,5 +1,3 @@
-import functools
-
 import jax
 import jax.numpy as jnp
 from jax import lax
@@ -16,7 +14,7 @@
 BF16 = jnp.bfloat16
 ROOMY = pltpu.CompilerParams(vmem_limit_bytes=40 * 1024 * 1024)
 
-FROM_LEAF, FROM_LOW, PICK_TWO, PICK_THREE, BELOW, SEND_TWO, SEND_THREE, SEND_ROOT, FLAGS = range(9)
+FROM_LEAF, FROM_LOW, PICK_TWO, PICK_THREE, BELOW, SEND_TWO, SEND_THREE, SEND_ROOT, FLAGS, ABOVE = range(10)
 
 
 def call(body, shape, specs, *args, scratch=()):
@@ -36,7 +34,7 @@
 
 VM = pl.BlockSpec(memory_space=pltpu.VMEM)
 SM = pl.BlockSpec(memory_space=pltpu.SMEM)
-HB = pl.BlockSpec(memory_space=pl.ANY)
+HB = pl.BlockSpec(memory_space=pltpu.HBM)
 
 
 def fetch(blocks, held, arrived, start):
@@ -122,12 +120,17 @@
             (mine >= 1).astype(F32),
             (mine == 3).astype(F32),
         ),
+        line(weights_t * anc, row) * one_mine,
     ]
     rows = rows + [jnp.zeros((1, count), F32)] * (out.shape[0] - len(rows))
     out[...] = jnp.concatenate(rows, 0)
 
 
-def first_kernel(table, slices, y0, out, local_a, local_b):
+def turn_kernel(block, out):
+    out[...] = block[0, 0, 0, 0].astype(F32).T
+
+
+def first_kernel(table, slices, y0, out, local_a, own_out):
     top, piece, width = slices.shape
     nrhs = y0.shape[1]
     half, quarter = top // 2, top // 4
@@ -146,8 +149,7 @@
             for k in range(start, start + quarter):
                 total = total + table[line, top + k] * slices[k]
         local_a[0, slot] = total
-    for k in range(half):
-        local_b[0, k] = table[BELOW, top + k] * slices[k]
+    own_out[...] = own[:half * piece]
 
 
 def leaf_kernel(table, got, out):
@@ -205,27 +207,35 @@
         out[k] = jnp.zeros_like(x)
 
 
-def down_kernel(slots, got, y_in, low, blocks, rest_out, out, x_now):
-    step = pl.program_id(0)
-    width = y_in.shape[1]
-
-    @pl.when(step == 0)
-    def _():
-        rest = y_in[...] - jnp.sum(got[...], 0)
-        rest_out[...] = rest
-        x_now[...] = mt(rest, low[...])
-
-    @pl.when(step < slots)
-    def _():
-        out[0] = mt(x_now[...], blocks[...].reshape(width, width).astype(BF16))
-
-    @pl.when(step >= slots)
-    def _():
-        out[0] = jnp.zeros_like(x_now)
-
-
-def last_kernel(got, rest_in, low, out):
-    out[0] = mt(rest_in[...] - jnp.sum(got[...], 0), low[...])
+def level_two_back_kernel(got, y_in, low, out):
+    out[0] = mt(y_in[...] - jnp.sum(got[...], 0), low[...])
+
+
+def down_kernel(own, x, out):
+    half, piece, nrhs = out.shape[0] // 2, out.shape[1], out.shape[2]
+    parts = jnp.concatenate(three(x[...]), 0).astype(BF16)
+    product = lax.dot_general(
+        own[...], parts, (((1,), (1,)), ((), ())), preferred_element_type=F32
+    )
+    product = product[:, :nrhs] + product[:, nrhs:2 * nrhs] + product[:, 2 * nrhs:]
+    out[:half] = product.reshape(half, piece, nrhs)
+    out[half:] = jnp.zeros((half, piece, nrhs), F32)
+
+
+def sum_kernel(table, got, out):
+    top = got.shape[0]
+    total = table[ABOVE, top + top // 2] * got[top // 2]
+    for k in range(top // 2 + 1, top):
+        total = total + table[ABOVE, top + k] * got[k]
+    out[0] = total
+
+
+def level_one_back_kernel(x, update, low, out):
+    nrhs = update.shape[1]
+    parts = jnp.concatenate(three(update[...]), 1).astype(BF16)
+    product = jnp.dot(low[...], parts, preferred_element_type=F32)
+    product = product[:, :nrhs] + product[:, nrhs:2 * nrhs] + product[:, 2 * nrhs:]
+    out[...] = x[...].T - product
 
 
 def a2a(array, axes):
@@ -246,7 +256,6 @@
     ny, nc, nz = lax.axis_size("y"), lax.axis_size("core"), lax.axis_size("z")
     ncol = ny * nc
     slot0 = factor[0, 0, 0, 0]
-    slot1 = factor[0, 0, 0, 1]
     base = rhs[0, 0]
     up = upper_inverse[0, 0]
     low = lower_inverse[0, 0]
@@ -261,7 +270,14 @@
     col = lax.axis_index(COL)
     is_high = lax.axis_index("xh") == 1
 
-    sent = slot1.T.astype(F32).reshape(ncol, piece, width)
+    sent = pl.pallas_call(
+        turn_kernel,
+        out_shape=shape_of(width, width),
+        grid=(1,),
+        in_specs=[pl.BlockSpec((1, 1, 1, 1, width, width), lambda k: (0, 0, 0, 1, 0, 0))],
+        out_specs=pl.BlockSpec((width, width), lambda k: (0, 0)),
+        compiler_params=ROOMY,
+    )(factor).reshape(ncol, piece, width)
     table = call(
         table_kernel, shape_of(16, count), [SM, VM, VM, VM, VM],
         jnp.stack([row, col]).astype(jnp.int32), parents[None, :], parents[:, None],
@@ -272,17 +288,16 @@
 
     slices = lax.all_to_all(sent, COL, 0, 0, tiled=True)
     table, y0, base_t, slices = lax.optimization_barrier((table, y0, base_t, slices))
-    out, local_a, local_b = call(
+    out, local_a, own = call(
         first_kernel,
         (
             shape_of(count, piece, nrhs),
             shape_of(1, quarter, piece, width),
-            shape_of(1, half, piece, width),
+            shape_of(half * piece, width, kind=BF16),
         ),
         [SM, VM, VM], table, slices, y0,
     )
     blocks_a = lax.all_gather(local_a, COL, tiled=True)
-    blocks_b = lax.all_gather(local_b, COL, tiled=True)
 
     part = call(leaf_kernel, shape_of(nrhs, piece), [SM, VM], table, a2a(out, ROW))
     got = a2a(part.reshape(ncol, mine, piece), COL)
@@ -299,34 +314,21 @@
         level_three_kernel, (panel, shape_of(nz, mine, width)), [SM, VM, VM, VM, VM, HB],
         table, a2a(out, "z"), rest, up, low, blocks_a, scratch=room(blocks_a, quarter),
     )
-    got = a2a(out, "z")
-    whole = lambda array: pl.BlockSpec(array.shape, lambda k: (0,) * array.ndim)
-    rest, out = pl.pallas_call(
-        functools.partial(down_kernel, half),
-        out_shape=(panel, shape_of(top, mine, width)),
-        grid=(top,),
-        in_specs=[
-            whole(got), whole(y), whole(low),
-            pl.BlockSpec((ncol, 1, piece, width), lambda k: (0, jnp.minimum(k, half - 1), 0, 0)),
-        ],
-        out_specs=(
-            pl.BlockSpec((mine, width), lambda k: (0, 0)),
-            pl.BlockSpec((1, mine, width), lambda k: (k, 0, 0)),
-        ),
-        scratch_shapes=[pltpu.VMEM((mine, width), F32)],
-        compiler_params=ROOMY,
-    )(got, y, low, blocks_b)
-    x = call(last_kernel, shape_of(1, mine, width), [VM, VM, VM], a2a(out, HALF), rest, low)
+    x = call(level_two_back_kernel, shape_of(1, mine, width), [VM, VM, VM], a2a(out, "z"), y, low)
     x = over_columns(x, ny).reshape(nrhs, width)
+    out = call(down_kernel, shape_of(top, piece, nrhs), [VM, VM], own, x)
+    part = call(sum_kernel, shape_of(1, piece, nrhs), [SM, VM], table, a2a(out, HALF))
+    update = over_columns(part, ny).reshape(width, nrhs)
+    x = call(level_one_back_kernel, shape_of(width, nrhs), [VM, VM, VM], x, update, low)
     full = lax.dot_general(
-        slot0.astype(F32), x, (((0,), (1,)), ((), ())), precision=HIGHEST
+        slot0.astype(F32), x, (((0,), (0,)), ((), ())), precision=HIGHEST
     )
     got = a2a(full.reshape(count, small, nrhs), ROW)
     part = jnp.sum(table[FROM_LOW][:, None, None] * got, axis=0)
     every = over_columns(part[None], ny).reshape(ncol, small, nrhs)
     got = a2a(jnp.concatenate([every, jnp.zeros_like(every)], 0), ROW).reshape(width, nrhs)
     below = jnp.dot(low.astype(F32), y0 - got, precision=HIGHEST)
-    return jnp.where(is_high, x.T, below)[None, None]
+    return jnp.where(is_high, x, below)[None, None]
 
 
 def solution(mesh):

time: 254 us -> 251 us (0.988)
  blocking collectives: 130 us -> 145 us
  local copies, waits for them, and re-layouts: 15.5 us -> 6.26 us
  waiting for transfers between devices: 54.2 us -> 48 us
    all_gather x1 -> x0, waiting for transfers between devices: 9.92 us -> none  [per_device(): blocks_b = lax.all_gather(local_b, COL, tiled=True)]
    all_to_all x8 -> x9, blocking collectives: 121 us -> 129 us  [a2a(): lax.all_to_all(array, axes, 0, 0, tiled=True)]
    all_gather x2 -> x3, blocking collectives: 8.74 us -> 15.6 us  [over_columns(): both = lax.all_gather(array, 'core', tiled=True)]
    unnamed x21, local copies, waits for them, and re-layouts: 10.2 us -> 3.75 us
    all_to_all x1, waiting for transfers between devices: 22.1 us -> 25.8 us  [per_device(): slices = lax.all_to_all(sent, COL, 0, 0, tiled=True)]
    pallas_call x7 -> x10, Pallas kernels: 9.48 us -> 10.7 us  [call(): pl.pallas_call(body, out_shape=shape, in_specs=specs, out_specs=out, scra...]
  transfers between devices with their start and end apart: 5 -> 4, of which waited for: 5 -> 4; matrix products, arithmetic and copies ran while one was open for 2% -> 1% of each run, Pallas kernels for 3% -> 1%
where the time goes in v6:
time: 251 us; the launch traced here: 249 us
  blocking collectives  145 us (58%)
  waiting for transfers between devices  48 us (19%)
  starting transfers between devices  21 us (8%)
  between operations  13.6 us (5%)
  Pallas kernels  11.9 us (5%)
  local copies, waits for them, and re-layouts  6.26 us (2%)
    all_to_all x9, blocking collectives, a2a(): lax.all_to_all(array, axes, 0, 0, tiled=True)  129 us
    all_to_all x1, waiting for transfers between devices, per_device(): slices = lax.all_to_all(sent, COL, 0, 0, tiled=True)  25.8 us
    all_to_all x2, waiting for transfers between devices, a2a(): lax.all_to_all(array, axes, 0, 0, tiled=True)  19.3 us
    all_gather x3, blocking collectives, over_columns(): both = lax.all_gather(array, 'core', tiled=True)  15.6 us
    pallas_call x10, Pallas kernels, call(): pl.pallas_call(body, out_shape=shape, in_specs=specs, out_specs=out, scra...  10.7 us
    all_to_all x2, starting transfers between devices, a2a(): lax.all_to_all(array, axes, 0, 0, tiled=True)  10.6 us
    all_to_all x1, starting transfers between devices, per_device(): slices = lax.all_to_all(sent, COL, 0, 0, tiled=True)  10.3 us
  transfers between devices with their start and end apart: 4, of which 4 were waited for; matrix products, arithmetic and copies ran while one was open for 1% of the time, Pallas kernels for 1%

profile of v6, /device:TPU:1, one launch (start us, length us, event | category | flops | bytes accessed | tf_op | source)
XLA Modules:
  0.0 249.1 jit_solution(78749956504091183)
XLA Ops:
  6.5 1.3 copy-done.5
  7.8 1.2 shard_map.65
  9.0 10.3 %all-to-all-start = ((f32[16,32,512]{2,1,0:T(8,128)}), f32[16,32,512]{2,1,0:T(8,128)S(1)}, u32[]{:S(2)}, u32[]{:S(2)}) async-start(f32[16,32,512]{2,1,0:T(8,128)} %bitcast.9), calls=%async_computation | async-start | bytes 2097152 | tf_op jit(solution)/shard_map/all_to_all | solution.py:289
  19.9 1.0 shard_map.64.table
  21.5 25.8 %all-to-all-done.slices = f32[16,32,512]{2,1,0:T(8,128)S(1)} async-done(((f32[16,32,512]{2,1,0:T(8,128)}), f32[16,32,512]{2,1,0:T(8,128)S(1)}, u32[]{:S(2)}, u32[]{:S(2)}) %all-to-all-start) | async-done | bytes 1048608 | tf_op jit(solution)/shard_map/all_to_all | solution.py:289
  47.3 1.8 shard_map.66
  49.2 27.5 %all_to_all.60.got = f32[32,32,128]{2,1,0:T(8,128)S(1)} all-to-all(f32[32,32,128]{2,1,0:T(8,128)S(1)} %get-tuple-element.21), channel_id=1, replica_groups=mesh['xh'=2,'xl'=2,'z'=8,'y'=8,'core'=2] {'xh','xl','z'}, dimensions={0} | all-to-all | bytes 1048576 | tf_op jit(solution)/shard_map/all_to_all | solution.py:243
  76.6 0.8 shard_map.67
  77.5 11.4 %all_to_all.61 = f32[16,1,256]{2,1,0:T(1,128)S(1)} all-to-all(f32[16,1,256]{2,1,0:T(1,128)S(1)} %reshape.37), channel_id=1, replica_groups=mesh['xh'=2,'xl'=2,'z'=8,'y'=8,'core'=2] {'y','core'}, dimensions={0} | all-to-all | bytes 32768 | tf_op jit(solution)/shard_map/all_to_all | solution.py:243
  89.5 0.7 reduce
  90.4 2.9 %all-gather.3.cloned.1.call-done.blocks = f32[16,4,32,512]{3,2,1,0:T(8,128)} async-done(((f32[1,4,32,512]{3,2,1,0:T(8,128)}), f32[16,4,32,512]{3,2,1,0:T(8,128)}) %all-gather.3.cloned.1.call-update) | async-done | bytes 4194320 | tf_op jit(solution)/shard_map/all_gather | solution.py:300
  93.2 2.2 copy-done.1
  95.4 1.7 shard_map.68
  97.1 16.8 %all_to_all.62.got = f32[16,8,512]{2,1,0:T(8,128)S(1)} all-to-all(f32[16,8,512]{2,1,0:T(8,128)S(1)} %get-tuple-element.24), channel_id=1, replica_groups=mesh['xh'=2,'xl'=2,'z'=8,'y'=8,'core'=2] {'xl','z'}, dimensions={0} | all-to-all | bytes 524288 | tf_op jit(solution)/shard_map/all_to_all | solution.py:243
  113.9 1.6 shard_map.69
  115.5 12.1 %all_to_all.63.got = f32[8,8,512]{2,1,0:T(8,128)S(1)} all-to-all(f32[8,8,512]{2,1,0:T(8,128)S(1)} %get-tuple-element.26), channel_id=1, replica_groups=mesh['xh'=2,'xl'=2,'z'=8,'y'=8,'core'=2] {'z'}, dimensions={0} | all-to-all | bytes 262144 | tf_op jit(solution)/shard_map/all_to_all | solution.py:243
  127.7 2.2 shard_map.70
  129.8 10.4 %all_to_all.64.got = f32[8,8,512]{2,1,0:T(8,128)S(1)} all-to-all(f32[8,8,512]{2,1,0:T(8,128)S(1)} %get-tuple-element.28), channel_id=1, replica_groups=mesh['xh'=2,'xl'=2,'z'=8,'y'=8,'core'=2] {'z'}, dimensions={0} | all-to-all | bytes 262144 | tf_op jit(solution)/shard_map/all_to_all | solution.py:243
  140.4 5.6 %all_gather.13 = f32[2,8,512]{2,1,0:T(8,128)S(1)} all-gather(f32[1,8,512]{2,1,0:T(8,128)S(1)} %shard_map.71), channel_id=1, replica_groups=mesh['xh'=2,'xl'=2,'z'=8,'y'=8,'core'=2] {'core'}, dimensions={0}, use_global_device_ids=true | all-gather | bytes 49152 | tf_op jit(solution)/shard_map/all_gather | solution.py:251
  146.1 15.2 %all_to_all.65 = f32[8,2,8,512]{3,2,1,0:T(8,128)S(1)} all-to-all(f32[8,2,8,512]{3,2,1,0:T(8,128)S(1)} %broadcast_in_dim.16), channel_id=1, replica_groups=mesh['xh'=2,'xl'=2,'z'=8,'y'=8,'core'=2] {'y'}, dimensions={0} | all-to-all | bytes 524288 | tf_op jit(solution)/shard_map/all_to_all | solution.py:243
  161.6 10.4 %all_to_all.66.got = f32[16,32,128]{2,1,0:T(8,128)S(1)} all-to-all(f32[16,32,128]{2,1,0:T(8,128)S(1)} %shard_map.72), channel_id=1, replica_groups=mesh['xh'=2,'xl'=2,'z'=8,'y'=8,'core'=2] {'xl','z'}, dimensions={0} | all-to-all | bytes 524288 | tf_op jit(solution)/shard_map/all_to_all | solution.py:243
  172.7 4.8 %all_gather.14 = f32[2,32,128]{2,1,0:T(8,128)S(1)} all-gather(f32[1,32,128]{2,1,0:T(8,128)S(1)} %shard_map.73), channel_id=1, replica_groups=mesh['xh'=2,'xl'=2,'z'=8,'y'=8,'core'=2] {'core'}, dimensions={0}, use_global_device_ids=true | all-gather | bytes 49152 | tf_op jit(solution)/shard_map/all_gather | solution.py:251
  177.5 14.8 %all_to_all.67 = f32[8,2,32,128]{3,2,1,0:T(8,128)S(1)} all-to-all(f32[8,2,32,128]{3,2,1,0:T(8,128)S(1)} %broadcast_in_dim.34), channel_id=1, replica_groups=mesh['xh'=2,'xl'=2,'z'=8,'y'=8,'core'=2] {'y'}, dimensions={0} | all-to-all | bytes 524288 | tf_op jit(solution)/shard_map/all_to_all | solution.py:243
  193.2 0.8 copy.19
  194.0 6.5 %all-to-all-start.9 = ((f32[32,16,128]{2,1,0:T(8,128)}), f32[32,16,128]{2,1,0:T(8,128)S(1)}, u32[]{:S(2)}, u32[]{:S(2)}) async-start(f32[32,16,128]{2,1,0:T(8,128)} %bitcast.17), calls=%async_computation.9 | async-start | bytes 524288 | tf_op jit(solution)/shard_map/all_to_all | solution.py:243
  200.5 9.7 %all-to-all-done.9 = f32[32,16,128]{2,1,0:T(8,128)S(1)} async-done(((f32[32,16,128]{2,1,0:T(8,128)}), f32[32,16,128]{2,1,0:T(8,128)S(1)}, u32[]{:S(2)}, u32[]{:S(2)}) %all-to-all-start.9) | async-done | bytes 262176 | tf_op jit(solution)/shard_map/all_to_all | solution.py:243
  210.3 5.2 %all-gather = f32[32,128]{1,0:T(8,128)S(1)} all-gather(f32[16,128]{1,0:T(8,128)S(1)} %multiply_reduce_fusion), channel_id=2, replica_groups=mesh['xh'=2,'xl'=2,'z'=8,'y'=8,'core'=2] {'core'}, dimensions={0}, use_global_device_ids=true | all-gather | bytes 24576 | tf_op jit(solution)/shard_map/all_gather | solution.py:251
  215.5 10.9 %all_to_all.68 = f32[8,2,16,128]{3,2,1,0:T(8,128)S(1)} all-to-all(f32[8,2,16,128]{3,2,1,0:T(8,128)S(1)} %broadcast_in_dim.36), channel_id=1, replica_groups=mesh['xh'=2,'xl'=2,'z'=8,'y'=8,'core'=2] {'y'}, dimensions={0} | all-to-all | bytes 262144 | tf_op jit(solution)/shard_map/all_to_all | solution.py:243
  226.3 0.7 concatenate.3
  227.1 4.2 %all-to-all-start.11 = ((f32[32,16,128]{2,1,0:T(8,128)}), f32[32,16,128]{2,1,0:T(8,128)S(1)}, u32[]{:S(2)}, u32[]{:S(2)}) async-start(f32[32,16,128]{2,1,0:T(8,128)} %concatenate.3), calls=%async_computation.11 | async-start | bytes 524288 | tf_op jit(solution)/shard_map/all_to_all | solution.py:243
  231.2 9.7 %all-to-all-done.11 = f32[32,16,128]{2,1,0:T(8,128)S(1)} async-done(((f32[32,16,128]{2,1,0:T(8,128)}), f32[32,16,128]{2,1,0:T(8,128)S(1)}, u32[]{:S(2)}, u32[]{:S(2)}) %all-to-all-start.11) | async-done | bytes 262176 | tf_op jit(solution)/shard_map/all_to_all | solution.py:243
  240.9 1.3 fusion.1
  (38 shorter events, 4.2 us)
Async XLA Ops:
  6.5 12.9 %copy-start = (f32[1,1,512,128]{3,2,1,0:T(8,128)S(1)}, f32[1,1,512,128]{3,2,1,0:T(8,128)}, u32[]{:S(2)}) copy-start(f32[1,1,512,128]{3,2,1,0:T(8,128)} %param.7) | copy-start | bytes 786436
  6.5 14.4 %copy-start.3 = (bf16[1,1,512,512]{3,2,1,0:T(8,128)(2,1)S(1)}, bf16[1,1,512,512]{3,2,1,0:T(8,128)(2,1)}, u32[]{:S(2)}) copy-start(bf16[1,1,512,512]{3,2,1,0:T(8,128)(2,1)} %param.8) | copy-start | bytes 1572868
  6.5 1.3 copy-start.5
  7.8 11.8 %copy-start.7 = (s32[32,32]{1,0:T(8,128)S(1)}, s32[32,32]{1,0:T(8,128)}, u32[]{:S(2)}) copy-start(s32[32,32]{1,0:T(8,128)} %mask.1) | copy-start | bytes 12292
  7.8 11.9 %copy-start.8 = (s32[32]{0:T(128)S(1)}, s32[32]{0:T(128)}, u32[]{:S(2)}) copy-start(s32[32]{0:T(128)} %param.10) | copy-start | bytes 388
  9.0 38.3 %all-to-all-start = ((f32[16,32,512]{2,1,0:T(8,128)}), f32[16,32,512]{2,1,0:T(8,128)S(1)}, u32[]{:S(2)}, u32[]{:S(2)}) async-start(f32[16,32,512]{2,1,0:T(8,128)} %bitcast.9), calls=%async_computation | async-start | bytes 2097152 | tf_op jit(solution)/shard_map/all_to_all | solution.py:289
  19.4 73.9 %all-gather.3.cloned.1.call-start = ((), (), s32[]{:S(2)}) async-start(), calls=%async_computation.12 | async-start | bytes 4456448 | tf_op jit(solution)/shard_map/all_gather | solution.py:300
  93.2 2.2 copy-start.1
  95.4 18.5 %copy-start.2 = (f32[16,4,32,512]{3,2,1,0:T(8,128)S(1)}, f32[16,4,32,512]{3,2,1,0:T(8,128)}, u32[]{:S(2)}) copy-start(f32[16,4,32,512]{3,2,1,0:T(8,128)} %all-gather.3.cloned.1.call-done.blocks) | copy-start | bytes 12582916
  95.4 32.3 %copy-start.4 = (bf16[1,1,512,512]{3,2,1,0:T(8,128)(2,1)S(1)}, bf16[1,1,512,512]{3,2,1,0:T(8,128)(2,1)}, u32[]{:S(2)}) copy-start(bf16[1,1,512,512]{3,2,1,0:T(8,128)(2,1)} %param.9) | copy-start | bytes 1572868
  127.7 65.1 %copy-start.6 = (bf16[1,1,1,2,512,512]{5,4,3,2,1,0:T(8,128)(2,1)S(1)}, bf16[1,1,1,2,512,512]{5,4,3,2,1,0:T(8,128)(2,1)}, u32[]{:S(2)}) copy-start(bf16[1,1,1,2,512,512]{5,4,3,2,1,0:T(8,128)(2,1)} %block.1) | copy-start | bytes 3145732
  194.0 16.2 %all-to-all-start.9 = ((f32[32,16,128]{2,1,0:T(8,128)}), f32[32,16,128]{2,1,0:T(8,128)S(1)}, u32[]{:S(2)}, u32[]{:S(2)}) async-start(f32[32,16,128]{2,1,0:T(8,128)} %bitcast.17), calls=%async_computation.9 | async-start | bytes 524288 | tf_op jit(solution)/shard_map/all_to_all | solution.py:243
  227.1 13.8 %all-to-all-start.11 = ((f32[32,16,128]{2,1,0:T(8,128)}), f32[32,16,128]{2,1,0:T(8,128)S(1)}, u32[]{:S(2)}, u32[]{:S(2)}) async-start(f32[32,16,128]{2,1,0:T(8,128)} %concatenate.3), calls=%async_computation.11 | async-start | bytes 524288 | tf_op jit(solution)/shard_map/all_to_all | solution.py:243
Sparse Core Ops, SparseCore 0:
  49.3 43.8 all-gather.2

commit v7 on v3

v7 whole, which is shorter than its diff:
```python
import functools

import jax
import jax.numpy as jnp
from jax import lax
from jax.experimental import pallas as pl
from jax.experimental.pallas import tpu as pltpu
from jax.sharding import Mesh, PartitionSpec as P

LEVELS = 4
HALF = ("xl", "z")
ROW = ("xh", "xl", "z")
COL = ("y", "core")
ACROSS = ("xh", "y")
F32 = jnp.float32
BF16 = jnp.bfloat16
ROOMY = pltpu.CompilerParams(vmem_limit_bytes=40 * 1024 * 1024)
VM = pl.BlockSpec(memory_space=pltpu.VMEM)
SM = pl.BlockSpec(memory_space=pltpu.SMEM)

FROM_LEAF, FROM_ONE, FROM_TWO, FROM_THREE, FROM_ABOVE, TO_COLUMN, FLAGS = range(7)


def shape_of(*dims, kind=F32):
    return jax.ShapeDtypeStruct(dims, kind)


def call(body, shape, *args, scalars=0):
    out = [VM] * len(shape) if isinstance(shape, tuple) else VM
    return pl.pallas_call(
        body,
        out_shape=shape,
        in_specs=[SM] * scalars + [VM] * (len(args) - scalars),
        out_specs=out,
        compiler_params=ROOMY,
    )(*args)


def product(matrix, panel):
    cols = panel.shape[1]
    high = panel.astype(BF16).astype(F32)
    rest = panel - high
    mid = rest.astype(BF16).astype(F32)
    parts = jnp.concatenate([high, mid, rest - mid], 1).astype(BF16)
    full = jnp.dot(matrix, parts, preferred_element_type=F32)
    return full[:, :cols] + full[:, cols:2 * cols] + full[:, 2 * cols:]


def table_kernel(at, parents_row, parents_col, mask, mask_t, out):
    count = mask.shape[0]
    top = count // 2
    row, col = at[0], at[1]
    down = lax.broadcasted_iota(jnp.int32, (count, count), 0)
    across = lax.broadcasted_iota(jnp.int32, (count, count), 1)
    step = (parents_col[...] == across).astype(F32)
    step_t = (parents_row[...] == down).astype(F32)
    identity = (down == across).astype(F32)
    anc = power = anc_t = power_t = identity
    for _ in range(LEVELS - 1):
        power = jnp.dot(power, step, preferred_element_type=F32)
        power_t = jnp.dot(step_t, power_t, preferred_element_type=F32)
        anc = anc + power
        anc_t = anc_t + power_t
    anc = jnp.minimum(anc, 1.0)
    anc_t = jnp.minimum(anc_t, 1.0)
    weights_t = mask_t[...].astype(F32) * (1.0 - identity)
    upper_t = weights_t * anc_t
    lower_t = weights_t * anc

    def line(matrix, index):
        return jnp.sum(jnp.where(down == index, matrix, 0.0), axis=0, keepdims=True)

    def level(ids):
        total = jnp.zeros_like(ids)
        for depth in range(1, LEVELS):
            total = total + (ids >= count - count // 2**depth).astype(jnp.int32)
        return total

    levels = level(lax.broadcasted_iota(jnp.int32, (1, count), 1))
    mine = level(jnp.full((1, count), row, jnp.int32))
    low = (mine == 0).astype(F32)
    high = (mine >= 1).astype(F32)
    late = (mine >= 2).astype(F32)
    image = jnp.where(row < top, row + top, row)
    rows = [
        line(upper_t, image) * (levels == 0).astype(F32) * low,
        line(upper_t, row) * (levels == 1).astype(F32) * high,
        line(upper_t, row) * (levels == 2).astype(F32) * late,
        line(lower_t, row) * (levels == 3).astype(F32) * late,
        line(lower_t, row) * high,
        line(lower_t, col) * high,
        high,
    ]
    rows = rows + [jnp.zeros((1, count), F32)] * (out.shape[0] - len(rows))
    out[...] = jnp.concatenate(rows, 0)


def turn_kernel(block, out):
    turned = block[0, 0, 0, 0].astype(F32).T
    ncol, piece = out.shape[0], out.shape[1]
    ny = ncol // 2
    for y in range(ny):
        for core in range(2):
            start = (core * ny + y) * piece
            out[2 * y + core] = turned[start:start + piece]


def turn_whole_kernel(block, out):
    out[...] = block[0, 0, 0, 0].astype(F32).T.astype(BF16)


def slot_call(body, shape, factor, slot):
    width = factor.shape[-1]
    return pl.pallas_call(
        body,
        out_shape=shape,
        grid=(1,),
        in_specs=[pl.BlockSpec((1, 1, 1, 1, width, width), lambda k: (0, 0, 0, slot, 0, 0))],
        out_specs=pl.BlockSpec(shape.shape, lambda k: (0,) * len(shape.shape)),
        compiler_params=ROOMY,
    )(factor)


def leaf_kernel(slices, y0, out, own_out):
    top, piece, width = slices.shape
    own = slices[...].reshape(top * piece, width).astype(BF16)
    own_out[...] = own
    out[...] = product(own, y0[...]).reshape(out.shape)


def sum_kernel(line, first, table, got, out):
    total = table[line, first] * got[0]
    for k in range(1, got.shape[0]):
        total = total + table[line, first + k] * got[k]
    for k in range(out.shape[0]):
        out[k] = total


def sum_keep_kernel(line, first, table, got, out, part_out):
    sum_kernel(line, first, table, got, out)
    part_out[...] = out[0]


def sum_more_kernel(line, first, table, got, part, out):
    total = part[...]
    for k in range(got.shape[0]):
        total = total + table[line, first + k] * got[k]
    for k in range(out.shape[0]):
        out[k] = total


def one_kernel(update, base, up, own, rest_out, out):
    rest = base[...] - update[...]
    rest_out[...] = rest
    out[...] = product(own[...], product(up[...], rest)).reshape(out.shape)


def two_kernel(update, rest, up, own, out):
    rows = own.shape[0] // 2
    y = product(up[...], rest[...] - update[...])
    out[...] = product(own[rows:], y).reshape(out.shape)


def three_kernel(update, rest, up, low, own, y_out, out):
    rows = own.shape[0] // 2
    y = product(up[...], rest[...] - update[...])
    y_out[...] = y
    out[...] = product(own[rows:], product(low[...], y)).reshape(out.shape)


def two_back_kernel(update, y, low, own, out):
    x = product(low[...], y[...] - update[...])
    out[...] = product(own[...], x).reshape(out.shape)


def one_back_kernel(update, y, low, below, x_out, out):
    x = product(low[...], y[...] - update[...])
    x_out[...] = x
    out[...] = product(below[...], x).reshape(out.shape)


def order_kernel(got, out):
    ny = got.shape[1]
    for y in range(ny):
        for core in range(2):
            out[2 * y + core] = got[core, y]


def last_kernel(table, update, y0, low, x, out):
    leaf = product(low[...], y0[...] - update[...])
    out[0, 0] = jnp.where(table[FLAGS, 0] > 0.5, x[...], leaf)


def a2a(array, axes):
    array = lax.optimization_barrier(array)
    return lax.optimization_barrier(lax.all_to_all(array, axes, 0, 0, tiled=True))


def per_device(factor, rhs, upper_inverse, lower_inverse, parents, block_mask):
    ny, nz = lax.axis_size("y"), lax.axis_size("z")
    ncol = ny * lax.axis_size("core")
    base = rhs[0, 0]
    up = upper_inverse[0, 0]
    low = lower_inverse[0, 0]
    width, nrhs = base.shape
    piece = width // ncol
    count = parents.shape[0]
    top = count // 2
    late = count - nz
    row = lax.axis_index(ROW)
    col = lax.axis_index(COL)
    panel = shape_of(width, nrhs)
    slice_ = shape_of(piece, nrhs)
    copies = shape_of(ny, piece, nrhs)
    across = shape_of(2 * ny, piece, nrhs)
    to_top = shape_of(top, piece, nrhs)
    to_late = shape_of(nz, piece, nrhs)

    sent = slot_call(turn_kernel, shape_of(ncol, piece, width), factor, 1)
    below = slot_call(turn_whole_kernel, shape_of(width, width, kind=BF16), factor, 0)
    table = call(
        table_kernel, shape_of(8, count),
        jnp.stack([row, col]).astype(jnp.int32), parents[None, :], parents[:, None],
        block_mask, block_mask.T, scalars=1,
    )
    y0 = jnp.dot(up.astype(F32), base, precision=lax.Precision.HIGHEST)

    slices = lax.all_to_all(sent, COL, 0, 0, tiled=True)
    table, y0, base, up, low, below, slices = lax.optimization_barrier(
        (table, y0, base, up, low, below, slices)
    )

    def total(line, first, got, shape):
        return call(functools.partial(sum_kernel, line, first), shape, table, got, scalars=1)

    def whole(half):
        return lax.all_gather(half, "core", tiled=True).reshape(width, nrhs)

    def spread(copied):
        return whole(a2a(copied, "y"))

    out, own = call(leaf_kernel, (to_top, shape_of(width, width, kind=BF16)), slices, y0)
    got = total(FROM_LEAF, 0, a2a(out, HALF), across)
    update = whole(a2a(got, ACROSS)[:ny])
    rest, out = call(one_kernel, (panel, to_top), update, base, up, own)
    got, part = call(
        functools.partial(sum_keep_kernel, FROM_ONE, top), (copies, slice_),
        table, a2a(out, HALF), scalars=1,
    )
    out = call(two_kernel, to_late, spread(got), rest, up, own)
    got = call(
        functools.partial(sum_more_kernel, FROM_TWO, late), copies,
        table, a2a(out, "z"), part, scalars=1,
    )
    y, out = call(three_kernel, (panel, to_late), spread(got), rest, up, low, own)
    got = total(FROM_THREE, late, a2a(out, "z"), copies)
    out = call(two_back_kernel, to_top, spread(got), y, low, own)
    got = total(FROM_ABOVE, top, a2a(out, HALF), copies)
    x, out = call(one_back_kernel, (panel, to_top), spread(got), y, low, below)
    got = total(TO_COLUMN, top, a2a(out, HALF), across)
    got = a2a(got, ACROSS)[ny:]
    got = lax.all_gather(got, "core")
    out = call(order_kernel, to_top, got)
    update = a2a(out, HALF).reshape(width, nrhs)
    return call(
        last_kernel, shape_of(1, 1, width, nrhs), table, update, y0, low, x, scalars=1
    )


def solution(mesh):
    grid = Mesh(mesh.devices.reshape(2, 2, 8, 8, 2), ("xh", "xl", "z", "y", "core"))
    placed = (
        P(ROW, None, COL, None, None, None),
        P(ROW, None, None, None),
        P(ROW, None, None, None),
        P(ROW, None, None, None),
        P(),
        P(),
    )
    return jax.shard_map(
        per_device,
        mesh=grid,
        in_specs=placed,
        out_specs=P(ROW, None, None, None),
        check_vma=False,
    )
```

time: 251 us -> 244 us (0.972)
  blocking collectives: 233 us -> 191 us
  waiting for transfers between devices: 0 us -> 24.5 us
  Pallas kernels: 0 us -> 11.4 us
  starting transfers between devices: 0 us -> 10.5 us
  matrix products: 9.55 us -> 0.6 us
    all_to_all x14 -> x13, blocking collectives: 205 us -> 162 us  [a2a(): lax.all_to_all(array, axes, 0, 0, tiled=True)]
    all_to_all x0 -> x1, waiting for transfers between devices: none -> 24.5 us  [per_device(): slices = lax.all_to_all(sent, COL, 0, 0, tiled=True)]
    pallas_call x0 -> x17, Pallas kernels: none -> 11.4 us  [the longest x15 11 us: call(): pl.pallas_call(body, out_shape=shape, in_specs=[SM] * scalars + [VM] * (l...]
    all_to_all x0 -> x1, starting transfers between devices: none -> 10.5 us  [per_device(): slices = lax.all_to_all(sent, COL, 0, 0, tiled=True)]
    dot_general x16 -> x1, matrix products: 8.55 us -> 0.6 us  [per_device(): y0 = jnp.dot(up.astype(F32), base, precision=lax.Precision.HIGHEST)]
  transfers between devices with their start and end apart: 0 -> 1, of which waited for: 0 -> 1; matrix products, arithmetic and copies ran while one was open for 0% -> 0% of each run, Pallas kernels for 0% -> 0%
where the time goes in v7:
time: 244 us; the launch traced here: 242 us
  blocking collectives  191 us (78%)
  waiting for transfers between devices  24.5 us (10%)
  Pallas kernels  11.4 us (5%)
  starting transfers between devices  10.5 us (4%)
  local copies, waits for them, and re-layouts  3.79 us (2%)
    all_to_all x13, blocking collectives, a2a(): lax.all_to_all(array, axes, 0, 0, tiled=True)  162 us
    all_to_all x1, waiting for transfers between devices, per_device(): slices = lax.all_to_all(sent, COL, 0, 0, tiled=True)  24.5 us
    all_gather x5, blocking collectives, whole(): return lax.all_gather(half, 'core', tiled=True).reshape(width, nrhs)  23.8 us
    pallas_call x15, Pallas kernels, call(): pl.pallas_call(body, out_shape=shape, in_specs=[SM] * scalars + [VM] * (l...  11 us
    all_to_all x1, starting transfers between devices, per_device(): slices = lax.all_to_all(sent, COL, 0, 0, tiled=True)  10.5 us
    all_gather x1, blocking collectives, per_device(): got = lax.all_gather(got, 'core')  5.15 us
  transfers between devices with their start and end apart: 1, of which 1 were waited for; matrix products, arithmetic and copies ran while one was open for 0% of the time, Pallas kernels for 0%

profile of v7, /device:TPU:1, one launch (start us, length us, event | category | flops | bytes accessed | tf_op | source)
XLA Modules:
  0.0 241.8 jit_solution(7198458760687354132)
XLA Ops:
  0.0 1.2 copy-done.2
  1.5 1.0 copy-done.4
  2.4 10.5 %all-to-all-start = ((f32[16,32,512]{2,1,0:T(8,128)}), f32[16,32,512]{2,1,0:T(8,128)S(1)}, u32[]{:S(2)}, u32[]{:S(2)}) async-start(f32[16,32,512]{2,1,0:T(8,128)} %copy-done.4), calls=%async_computation | async-start | bytes 2097152 | tf_op jit(solution)/shard_map/all_to_all | solution.py:228
  13.2 0.7 copy-done.6
  14.0 0.7 copy-done.7
  14.8 1.0 shard_map.64.table
  16.4 24.5 %all-to-all-done.slices = f32[16,32,512]{2,1,0:T(8,128)S(1)} async-done(((f32[16,32,512]{2,1,0:T(8,128)}), f32[16,32,512]{2,1,0:T(8,128)S(1)}, u32[]{:S(2)}, u32[]{:S(2)}) %all-to-all-start) | async-done | bytes 1048608 | tf_op jit(solution)/shard_map/all_to_all | solution.py:228
  41.3 19.0 %all_to_all.70.got = f32[16,32,128]{2,1,0:T(8,128)S(1)} all-to-all(f32[16,32,128]{2,1,0:T(8,128)S(1)} %get-tuple-element.25), channel_id=1, replica_groups=mesh['xh'=2,'xl'=2,'z'=8,'y'=8,'core'=2] {'xl','z'}, dimensions={0} | all-to-all | bytes 524288 | tf_op jit(solution)/shard_map/all_to_all | solution.py:196
  60.9 13.5 %all_to_all.71 = f32[16,32,128]{2,1,0:T(8,128)S(1)} all-to-all(f32[16,32,128]{2,1,0:T(8,128)S(1)} %shard_map.68), channel_id=1, replica_groups=mesh['xh'=2,'xl'=2,'z'=8,'y'=8,'core'=2] {'xh','y'}, dimensions={0} | all-to-all | bytes 524288 | tf_op jit(solution)/shard_map/all_to_all | solution.py:196
  74.5 5.1 %all_gather.21 = f32[16,32,128]{2,1,0:T(8,128)S(1)} all-gather(f32[8,32,128]{2,1,0:T(8,128)S(1)} %slice.8), channel_id=1, replica_groups=mesh['xh'=2,'xl'=2,'z'=8,'y'=8,'core'=2] {'core'}, dimensions={0}, use_global_device_ids=true | all-gather | bytes 393216 | tf_op jit(solution)/shard_map/all_gather | solution.py:237
  79.5 0.8 shard_map.69
  80.3 13.1 %all_to_all.72.got = f32[16,32,128]{2,1,0:T(8,128)S(1)} all-to-all(f32[16,32,128]{2,1,0:T(8,128)S(1)} %get-tuple-element.29), channel_id=1, replica_groups=mesh['xh'=2,'xl'=2,'z'=8,'y'=8,'core'=2] {'xl','z'}, dimensions={0} | all-to-all | bytes 524288 | tf_op jit(solution)/shard_map/all_to_all | solution.py:196
  94.1 11.9 %all_to_all.73 = f32[8,32,128]{2,1,0:T(8,128)S(1)} all-to-all(f32[8,32,128]{2,1,0:T(8,128)S(1)} %get-tuple-element.30), channel_id=1, replica_groups=mesh['xh'=2,'xl'=2,'z'=8,'y'=8,'core'=2] {'y'}, dimensions={0} | all-to-all | bytes 262144 | tf_op jit(solution)/shard_map/all_to_all | solution.py:196
  106.0 5.1 %all_gather.22 = f32[16,32,128]{2,1,0:T(8,128)S(1)} all-gather(f32[8,32,128]{2,1,0:T(8,128)S(1)} %all_to_all.73), channel_id=1, replica_groups=mesh['xh'=2,'xl'=2,'z'=8,'y'=8,'core'=2] {'core'}, dimensions={0}, use_global_device_ids=true | all-gather | bytes 393216 | tf_op jit(solution)/shard_map/all_gather | solution.py:237
  111.1 0.7 shard_map.71
  111.7 11.6 %all_to_all.74.got = f32[8,32,128]{2,1,0:T(8,128)S(1)} all-to-all(f32[8,32,128]{2,1,0:T(8,128)S(1)} %shard_map.71), channel_id=1, replica_groups=mesh['xh'=2,'xl'=2,'z'=8,'y'=8,'core'=2] {'z'}, dimensions={0} | all-to-all | bytes 262144 | tf_op jit(solution)/shard_map/all_to_all | solution.py:196
  124.0 10.4 %all_to_all.75 = f32[8,32,128]{2,1,0:T(8,128)S(1)} all-to-all(f32[8,32,128]{2,1,0:T(8,128)S(1)} %shard_map.72), channel_id=1, replica_groups=mesh['xh'=2,'xl'=2,'z'=8,'y'=8,'core'=2] {'y'}, dimensions={0} | all-to-all | bytes 262144 | tf_op jit(solution)/shard_map/all_to_all | solution.py:196
  134.4 4.8 %all_gather.23 = f32[16,32,128]{2,1,0:T(8,128)S(1)} all-gather(f32[8,32,128]{2,1,0:T(8,128)S(1)} %all_to_all.75), channel_id=1, replica_groups=mesh['xh'=2,'xl'=2,'z'=8,'y'=8,'core'=2] {'core'}, dimensions={0}, use_global_device_ids=true | all-gather | bytes 393216 | tf_op jit(solution)/shard_map/all_gather | solution.py:237
  139.2 1.0 shard_map.73
  140.2 10.8 %all_to_all.76.got = f32[8,32,128]{2,1,0:T(8,128)S(1)} all-to-all(f32[8,32,128]{2,1,0:T(8,128)S(1)} %get-tuple-element.34), channel_id=1, replica_groups=mesh['xh'=2,'xl'=2,'z'=8,'y'=8,'core'=2] {'z'}, dimensions={0} | all-to-all | bytes 262144 | tf_op jit(solution)/shard_map/all_to_all | solution.py:196
  151.6 10.3 %all_to_all.77 = f32[8,32,128]{2,1,0:T(8,128)S(1)} all-to-all(f32[8,32,128]{2,1,0:T(8,128)S(1)} %shard_map.74), channel_id=1, replica_groups=mesh['xh'=2,'xl'=2,'z'=8,'y'=8,'core'=2] {'y'}, dimensions={0} | all-to-all | bytes 262144 | tf_op jit(solution)/shard_map/all_to_all | solution.py:196
  162.0 4.3 %all_gather.24 = f32[16,32,128]{2,1,0:T(8,128)S(1)} all-gather(f32[8,32,128]{2,1,0:T(8,128)S(1)} %all_to_all.77), channel_id=1, replica_groups=mesh['xh'=2,'xl'=2,'z'=8,'y'=8,'core'=2] {'core'}, dimensions={0}, use_global_device_ids=true | all-gather | bytes 393216 | tf_op jit(solution)/shard_map/all_gather | solution.py:237
  166.3 0.8 shard_map.75
  167.1 11.8 %all_to_all.78.got = f32[16,32,128]{2,1,0:T(8,128)S(1)} all-to-all(f32[16,32,128]{2,1,0:T(8,128)S(1)} %shard_map.75), channel_id=1, replica_groups=mesh['xh'=2,'xl'=2,'z'=8,'y'=8,'core'=2] {'xl','z'}, dimensions={0} | all-to-all | bytes 524288 | tf_op jit(solution)/shard_map/all_to_all | solution.py:196
  179.6 10.3 %all_to_all.79 = f32[8,32,128]{2,1,0:T(8,128)S(1)} all-to-all(f32[8,32,128]{2,1,0:T(8,128)S(1)} %shard_map.76), channel_id=1, replica_groups=mesh['xh'=2,'xl'=2,'z'=8,'y'=8,'core'=2] {'y'}, dimensions={0} | all-to-all | bytes 262144 | tf_op jit(solution)/shard_map/all_to_all | solution.py:196
  189.9 4.5 %all_gather.25 = f32[16,32,128]{2,1,0:T(8,128)S(1)} all-gather(f32[8,32,128]{2,1,0:T(8,128)S(1)} %all_to_all.79), channel_id=1, replica_groups=mesh['xh'=2,'xl'=2,'z'=8,'y'=8,'core'=2] {'core'}, dimensions={0}, use_global_device_ids=true | all-gather | bytes 393216 | tf_op jit(solution)/shard_map/all_gather | solution.py:237
  194.4 0.8 shard_map.77
  195.2 13.2 %all_to_all.80.got = f32[16,32,128]{2,1,0:T(8,128)S(1)} all-to-all(f32[16,32,128]{2,1,0:T(8,128)S(1)} %get-tuple-element.37), channel_id=1, replica_groups=mesh['xh'=2,'xl'=2,'z'=8,'y'=8,'core'=2] {'xl','z'}, dimensions={0} | all-to-all | bytes 524288 | tf_op jit(solution)/shard_map/all_to_all | solution.py:196
  209.1 11.9 %all_to_all.81 = f32[16,32,128]{2,1,0:T(8,128)S(1)} all-to-all(f32[16,32,128]{2,1,0:T(8,128)S(1)} %shard_map.78), channel_id=1, replica_groups=mesh['xh'=2,'xl'=2,'z'=8,'y'=8,'core'=2] {'xh','y'}, dimensions={0} | all-to-all | bytes 524288 | tf_op jit(solution)/shard_map/all_to_all | solution.py:196
  221.0 5.1 %all-gather = f32[16,32,128]{2,1,0:T(8,128)S(1)} all-gather(f32[8,32,128]{2,1,0:T(8,128)S(1)} %slice.9), channel_id=2, replica_groups=mesh['xh'=2,'xl'=2,'z'=8,'y'=8,'core'=2] {'core'}, dimensions={0}, use_global_device_ids=true | all-gather | bytes 393216 | tf_op jit(solution)/shard_map/all_gather | solution.py:262
  226.1 14.0 %all_to_all.82 = f32[16,32,128]{2,1,0:T(8,128)S(1)} all-to-all(f32[16,32,128]{2,1,0:T(8,128)S(1)} %shard_map.79), channel_id=1, replica_groups=mesh['xh'=2,'xl'=2,'z'=8,'y'=8,'core'=2] {'xl','z'}, dimensions={0} | all-to-all | bytes 524288 | tf_op jit(solution)/shard_map/all_to_all | solution.py:196
  240.1 1.8 shard_map.80
  (28 shorter events, 5.5 us)
Async XLA Ops:
  0.0 1.2 copy-start.2
  1.5 1.0 copy-start.4
  2.4 10.5 %copy-start.3 = (bf16[1,1,1,2,512,512]{5,4,3,2,1,0:T(8,128)(2,1)S(1)}, bf16[1,1,1,2,512,512]{5,4,3,2,1,0:T(8,128)(2,1)}, u32[]{:S(2)}) copy-start(bf16[1,1,1,2,512,512]{5,4,3,2,1,0:T(8,128)(2,1)} %block.3) | copy-start | bytes 3145732
  2.4 38.4 %all-to-all-start = ((f32[16,32,512]{2,1,0:T(8,128)}), f32[16,32,512]{2,1,0:T(8,128)S(1)}, u32[]{:S(2)}, u32[]{:S(2)}) async-start(f32[16,32,512]{2,1,0:T(8,128)} %copy-done.4), calls=%async_computation | async-start | bytes 2097152 | tf_op jit(solution)/shard_map/all_to_all | solution.py:228
  12.9 2.9 %copy-start.1 = (bf16[1,1,512,512]{3,2,1,0:T(8,128)(2,1)S(1)}, bf16[1,1,512,512]{3,2,1,0:T(8,128)(2,1)}, u32[]{:S(2)}) copy-start(bf16[1,1,512,512]{3,2,1,0:T(8,128)(2,1)} %param.8) | copy-start | bytes 1572868
  12.9 2.9 %copy-start.5 = (f32[1,1,512,128]{3,2,1,0:T(8,128)S(1)}, f32[1,1,512,128]{3,2,1,0:T(8,128)}, u32[]{:S(2)}) copy-start(f32[1,1,512,128]{3,2,1,0:T(8,128)} %param.7) | copy-start | bytes 786436
  13.1 0.7 copy-start.6
  14.0 0.7 copy-start.7
  123.3 15.8 %copy-start = (bf16[1,1,512,512]{3,2,1,0:T(8,128)(2,1)S(1)}, bf16[1,1,512,512]{3,2,1,0:T(8,128)(2,1)}, u32[]{:S(2)}) copy-start(bf16[1,1,512,512]{3,2,1,0:T(8,128)(2,1)} %param.9) | copy-start | bytes 1572868

commit v8 on v7

--- a/solution.py
+++ b/solution.py
@@ -18,7 +18,7 @@
 VM = pl.BlockSpec(memory_space=pltpu.VMEM)
 SM = pl.BlockSpec(memory_space=pltpu.SMEM)
 
-FROM_LEAF, FROM_ONE, FROM_TWO, FROM_THREE, FROM_ABOVE, TO_COLUMN, FLAGS = range(7)
+LEAF_COLUMN, FROM_ONE, FROM_TWO, FROM_THREE, FROM_ABOVE, TO_COLUMN, FLAGS = range(7)
 
 
 def shape_of(*dims, kind=F32):
@@ -81,9 +81,8 @@
     low = (mine == 0).astype(F32)
     high = (mine >= 1).astype(F32)
     late = (mine >= 2).astype(F32)
-    image = jnp.where(row < top, row + top, row)
     rows = [
-        line(upper_t, image) * (levels == 0).astype(F32) * low,
+        line(upper_t, top + col) * (levels == 0).astype(F32) * low,
         line(upper_t, row) * (levels == 1).astype(F32) * high,
         line(upper_t, row) * (levels == 2).astype(F32) * late,
         line(lower_t, row) * (levels == 3).astype(F32) * late,
@@ -95,18 +94,38 @@
     out[...] = jnp.concatenate(rows, 0)
 
 
-def turn_kernel(block, out):
+def turn_kernel(at, block, whole, keep, send):
+    rows = keep.shape[0]
     turned = block[0, 0, 0, 0].astype(F32).T
-    ncol, piece = out.shape[0], out.shape[1]
-    ny = ncol // 2
-    for y in range(ny):
-        for core in range(2):
-            start = (core * ny + y) * piece
-            out[2 * y + core] = turned[start:start + piece]
+    whole[...] = turned.astype(BF16)
+    mine = at[0] == 0
+    keep[...] = jnp.where(mine, turned[:rows], turned[rows:])
+    send[...] = jnp.where(mine, turned[rows:], turned[:rows])
 
 
 def turn_whole_kernel(block, out):
     out[...] = block[0, 0, 0, 0].astype(F32).T.astype(BF16)
+
+
+def parcel_kernel(at, own, other, *outs):
+    ny = len(outs)
+    piece = own.shape[0] // ny
+    for step, out in enumerate(outs):
+        start = pl.multiple_of(lax.rem(at[1] + step, ny) * piece, piece)
+        out[:piece] = own[pl.ds(start, piece), :]
+        out[piece:] = other[pl.ds(start, piece), :]
+
+
+def unpack_kernel(at, *refs):
+    parcels, out = refs[:-1], refs[-1]
+    ny = len(parcels)
+    piece = parcels[0].shape[0] // 2
+    for step, parcel in enumerate(parcels):
+        chip = 2 * lax.rem(at[1] + ny - step, ny)
+        first = pl.multiple_of((chip + at[0]) * piece, piece)
+        second = pl.multiple_of((chip + 1 - at[0]) * piece, piece)
+        out[pl.ds(first, piece), :] = parcel[:piece].astype(BF16)
+        out[pl.ds(second, piece), :] = parcel[piece:].astype(BF16)
 
 
 def slot_call(body, shape, factor, slot):
@@ -121,11 +140,8 @@
     )(factor)
 
 
-def leaf_kernel(slices, y0, out, own_out):
-    top, piece, width = slices.shape
-    own = slices[...].reshape(top * piece, width).astype(BF16)
-    own_out[...] = own
-    out[...] = product(own, y0[...]).reshape(out.shape)
+def leaf_kernel(block, y0, out):
+    out[...] = product(block[...], y0[...]).reshape(out.shape)
 
 
 def sum_kernel(line, first, table, got, out):
@@ -216,7 +232,23 @@
     to_top = shape_of(top, piece, nrhs)
     to_late = shape_of(nz, piece, nrhs)
 
-    sent = slot_call(turn_kernel, shape_of(ncol, piece, width), factor, 1)
+    at = jnp.stack([lax.axis_index("core"), lax.axis_index("y")]).astype(jnp.int32)
+    half_block = shape_of(width // 2, width)
+    turned, keep, send = pl.pallas_call(
+        turn_kernel,
+        out_shape=(shape_of(width, width, kind=BF16), half_block, half_block),
+        grid=(1,),
+        in_specs=[
+            SM,
+            pl.BlockSpec((1, 1, 1, 1, width, width), lambda k: (0, 0, 0, 1, 0, 0)),
+        ],
+        out_specs=(
+            pl.BlockSpec((width, width), lambda k: (0, 0)),
+            pl.BlockSpec((width // 2, width), lambda k: (0, 0)),
+            pl.BlockSpec((width // 2, width), lambda k: (0, 0)),
+        ),
+        compiler_params=ROOMY,
+    )(at, factor)
     below = slot_call(turn_whole_kernel, shape_of(width, width, kind=BF16), factor, 0)
     table = call(
         table_kernel, shape_of(8, count),
@@ -225,10 +257,11 @@
     )
     y0 = jnp.dot(up.astype(F32), base, precision=lax.Precision.HIGHEST)
 
-    slices = lax.all_to_all(sent, COL, 0, 0, tiled=True)
-    table, y0, base, up, low, below, slices = lax.optimization_barrier(
-        (table, y0, base, up, low, below, slices)
-    )
+    def shifted(parcel, step):
+        return lax.ppermute(parcel, "y", [(k, (k + step) % ny) for k in range(ny)])
+
+    def together(*arrays):
+        return lax.optimization_barrier(arrays)
 
     def total(line, first, got, shape):
         return call(functools.partial(sum_kernel, line, first), shape, table, got, scalars=1)
@@ -239,9 +272,26 @@
     def spread(copied):
         return whole(a2a(copied, "y"))
 
-    out, own = call(leaf_kernel, (to_top, shape_of(width, width, kind=BF16)), slices, y0)
-    got = total(FROM_LEAF, 0, a2a(out, HALF), across)
-    update = whole(a2a(got, ACROSS)[:ny])
+    out = call(leaf_kernel, to_top, turned, y0)
+    out, send = together(out, send)
+    other = lax.ppermute(send, "core", [(0, 1), (1, 0)])
+    got = a2a(out, HALF)
+    parcels = list(call(
+        parcel_kernel, (shape_of(2 * piece, width),) * ny, at, keep, other, scalars=1
+    ))
+    got = total(LEAF_COLUMN, 0, got, across)
+    got, parcels[1], parcels[7], parcels[2] = together(got, parcels[1], parcels[7], parcels[2])
+    for step in (1, 7, 2):
+        parcels[step] = shifted(parcels[step], step)
+    got = lax.all_gather(a2a(got, ACROSS)[:ny], "core")
+    out = call(order_kernel, to_top, got)
+    out, parcels[6], parcels[3], parcels[5], parcels[4] = together(
+        out, parcels[6], parcels[3], parcels[5], parcels[4]
+    )
+    for step in (6, 3, 5, 4):
+        parcels[step] = shifted(parcels[step], step)
+    update = a2a(out, HALF).reshape(width, nrhs)
+    own = call(unpack_kernel, shape_of(width, width, kind=BF16), at, *parcels, scalars=1)
     rest, out = call(one_kernel, (panel, to_top), update, base, up, own)
     got, part = call(
         functools.partial(sum_keep_kernel, FROM_ONE, top), (copies, slice_),

time: 244 us -> 269 us (1.10)
  starting transfers between devices: 10.5 us -> 47.6 us
  blocking collectives: 191 us -> 170 us
  waiting for transfers between devices: 24.5 us -> 29.5 us
  Pallas kernels: 11.4 us -> 16 us
    ppermute x0 -> x8, starting transfers between devices: none -> 34.1 us  [the longest x7 25.3 us: shifted(): return lax.ppermute(parcel, 'y', [(k, (k + step) % ny) for k in range(ny)])]
    all_to_all x13 -> x11, blocking collectives: 162 us -> 141 us  [a2a(): lax.all_to_all(array, axes, 0, 0, tiled=True)]
    ppermute x0 -> x8, waiting for transfers between devices: none -> 15.2 us  [the longest x7 15.2 us: shifted(): return lax.ppermute(parcel, 'y', [(k, (k + step) % ny) for k in range(ny)])]
    all_to_all x1 -> x3, waiting for transfers between devices: 24.5 us -> 14.3 us  [a2a(): lax.all_to_all(array, axes, 0, 0, tiled=True)]
    all_gather x0 -> x1, blocking collectives: none -> 5.17 us  [per_device(): got = lax.all_gather(a2a(got, ACROSS)[:ny], 'core')]
    all_gather x5 -> x4, blocking collectives: 23.8 us -> 18.9 us  [whole(): return lax.all_gather(half, 'core', tiled=True).reshape(width, nrhs)]
    pallas_call x15 -> x18, Pallas kernels: 11 us -> 15 us  [call(): pl.pallas_call(body, out_shape=shape, in_specs=[SM] * scalars + [VM] * (l...]
    all_to_all x1 -> x3, starting transfers between devices: 10.5 us -> 13.5 us  [a2a(): lax.all_to_all(array, axes, 0, 0, tiled=True)]
  transfers between devices with their start and end apart: 1 -> 11, of which waited for: 1 -> 4; matrix products, arithmetic and copies ran while one was open for 0% -> 0% of each run, Pallas kernels for 0% -> 1%
where the time goes in v8:
time: 269 us; the launch traced here: 267 us
  blocking collectives  170 us (63%)
  starting transfers between devices  47.6 us (18%)
  waiting for transfers between devices  29.5 us (11%)
  Pallas kernels  16 us (6%)
  local copies, waits for them, and re-layouts  3.12 us (1%)
    all_to_all x11, blocking collectives, a2a(): lax.all_to_all(array, axes, 0, 0, tiled=True)  141 us
    ppermute x7, starting transfers between devices, shifted(): return lax.ppermute(parcel, 'y', [(k, (k + step) % ny) for k in range(ny)])  25.3 us
    all_gather x4, blocking collectives, whole(): return lax.all_gather(half, 'core', tiled=True).reshape(width, nrhs)  18.9 us
    ppermute x7, waiting for transfers between devices, shifted(): return lax.ppermute(parcel, 'y', [(k, (k + step) % ny) for k in range(ny)])  15.2 us
    pallas_call x18, Pallas kernels, call(): pl.pallas_call(body, out_shape=shape, in_specs=[SM] * scalars + [VM] * (l...  15 us
    all_to_all x3, waiting for transfers between devices, a2a(): lax.all_to_all(array, axes, 0, 0, tiled=True)  14.3 us
    all_to_all x3, starting transfers between devices, a2a(): lax.all_to_all(array, axes, 0, 0, tiled=True)  13.5 us
    ppermute x1, starting transfers between devices, per_device(): other = lax.ppermute(send, 'core', [(0, 1), (1, 0)])  8.77 us
  transfers between devices with their start and end apart: 11, of which 4 were waited for; matrix products, arithmetic and copies ran while one was open for 0% of the time, Pallas kernels for 1%

profile of v8, /device:TPU:1, one launch (start us, length us, event | category | flops | bytes accessed | tf_op | source)
XLA Modules:
  0.0 267.4 jit_solution(5685276874330278101)
XLA Ops:
  4.2 8.8 %collective-permute-start = (f32[256,512]{1,0:T(8,128)S(1)}, f32[256,512]{1,0:T(8,128)S(1)}, u32[]{:S(2)}, u32[]{:S(2)}) collective-permute-start(f32[256,512]{1,0:T(8,128)S(1)} %get-tuple-element.39), channel_id=1, source_target_pairs={{0,1},{1,0},{2,3},{3,2},{4,5},{5,4},{6,7},{7,6},{8,9},{9,8},{10,11... | collective-permute-start | bytes 1572872 | tf_op jit(solution)/shard_map/ppermute | solution.py:277
  12.9 5.7 %all-to-all-start = ((f32[16,32,128]{2,1,0:T(8,128)}), f32[16,32,128]{2,1,0:T(8,128)S(1)}, u32[]{:S(2)}, u32[]{:S(2)}) async-start(f32[16,32,128]{2,1,0:T(8,128)} %shard_map.66), calls=%async_computation | async-start | bytes 524288 | tf_op jit(solution)/shard_map/all_to_all | solution.py:212
  21.2 6.6 %all-to-all-done.got = f32[16,32,128]{2,1,0:T(8,128)S(1)} async-done(((f32[16,32,128]{2,1,0:T(8,128)}), f32[16,32,128]{2,1,0:T(8,128)S(1)}, u32[]{:S(2)}, u32[]{:S(2)}) %all-to-all-start) | async-done | bytes 262176 | tf_op jit(solution)/shard_map/all_to_all | solution.py:212
  29.9 18.1 %all_to_all.70 = f32[16,32,128]{2,1,0:T(8,128)S(1)} all-to-all(f32[16,32,128]{2,1,0:T(8,128)S(1)} %shard_map.67), channel_id=1, replica_groups=mesh['xh'=2,'xl'=2,'z'=8,'y'=8,'core'=2] {'xh','y'}, dimensions={0} | all-to-all | bytes 524288 | tf_op jit(solution)/shard_map/all_to_all | solution.py:212
  48.0 5.2 %all-gather = f32[16,32,128]{2,1,0:T(8,128)S(1)} all-gather(f32[8,32,128]{2,1,0:T(8,128)S(1)} %slice.8), channel_id=2, replica_groups=mesh['xh'=2,'xl'=2,'z'=8,'y'=8,'core'=2] {'core'}, dimensions={0}, use_global_device_ids=true | all-gather | bytes 393216 | tf_op jit(solution)/shard_map/all_gather | solution.py:286
  53.9 4.4 %all-to-all-start.2 = ((f32[16,32,128]{2,1,0:T(8,128)}), f32[16,32,128]{2,1,0:T(8,128)S(1)}, u32[]{:S(2)}, u32[]{:S(2)}) async-start(f32[16,32,128]{2,1,0:T(8,128)} %shard_map.69), calls=%async_computation.2 | async-start | bytes 524288 | tf_op jit(solution)/shard_map/all_to_all | solution.py:212
  58.4 3.6 %collective-permute-start.1 = (f32[64,512]{1,0:T(8,128)}, f32[64,512]{1,0:T(8,128)S(1)}, u32[]{:S(2)}, u32[]{:S(2)}) collective-permute-start(f32[64,512]{1,0:T(8,128)} %get-tuple-element.50), channel_id=1, source_target_pairs={{0,2},{2,4},{4,6},{6,8},{8,10},{10,12},{12,14},{14,0},{1,3},{3,5},... | collective-permute-start | bytes 393224 | tf_op jit(solution)/shard_map/ppermute | solution.py:261
  61.9 2.7 %collective-permute-start.2 = (f32[64,512]{1,0:T(8,128)}, f32[64,512]{1,0:T(8,128)S(1)}, u32[]{:S(2)}, u32[]{:S(2)}) collective-permute-start(f32[64,512]{1,0:T(8,128)} %get-tuple-element.51), channel_id=1, source_target_pairs={{0,4},{2,6},{4,8},{6,10},{8,12},{10,14},{12,0},{14,2},{1,5},{3,7},... | collective-permute-start | bytes 393224 | tf_op jit(solution)/shard_map/ppermute | solution.py:261
  64.7 4.1 %collective-permute-start.7 = (f32[64,512]{1,0:T(8,128)S(1)}, f32[64,512]{1,0:T(8,128)S(1)}, u32[]{:S(2)}, u32[]{:S(2)}) collective-permute-start(f32[64,512]{1,0:T(8,128)S(1)} %get-tuple-element.56), channel_id=1, source_target_pairs={{0,14},{2,0},{4,2},{6,4},{8,6},{10,8},{12,10},{14,12},{1,15},{3,1}... | collective-permute-start | bytes 393224 | tf_op jit(solution)/shard_map/ppermute | solution.py:261
  68.8 2.6 collective-permute-start.3
  71.4 5.0 %collective-permute-start.4 = (f32[64,512]{1,0:T(8,128)S(1)}, f32[64,512]{1,0:T(8,128)S(1)}, u32[]{:S(2)}, u32[]{:S(2)}) collective-permute-start(f32[64,512]{1,0:T(8,128)S(1)} %get-tuple-element.53), channel_id=1, source_target_pairs={{0,8},{2,10},{4,12},{6,14},{8,0},{10,2},{12,4},{14,6},{1,9},{3,11}... | collective-permute-start | bytes 393224 | tf_op jit(solution)/shard_map/ppermute | solution.py:261
  76.5 5.0 %collective-permute-start.5 = (f32[64,512]{1,0:T(8,128)S(1)}, f32[64,512]{1,0:T(8,128)S(1)}, u32[]{:S(2)}, u32[]{:S(2)}) collective-permute-start(f32[64,512]{1,0:T(8,128)S(1)} %get-tuple-element.54), channel_id=1, source_target_pairs={{0,10},{2,12},{4,14},{6,0},{8,2},{10,4},{12,6},{14,8},{1,11},{3,13... | collective-permute-start | bytes 393224 | tf_op jit(solution)/shard_map/ppermute | solution.py:261
  81.5 2.3 collective-permute-start.6
  83.8 5.6 %collective-permute-done.4.refs_4_ = f32[64,512]{1,0:T(8,128)S(1)} collective-permute-done((f32[64,512]{1,0:T(8,128)S(1)}, f32[64,512]{1,0:T(8,128)S(1)}, u32[]{:S(2)}, u32[]{:S(2)}) %collective-permute-start.4) | collective-permute-done | bytes 131104 | tf_op jit(solution)/shard_map/ppermute | solution.py:261
  89.4 9.6 %collective-permute-done.6.refs_6_ = f32[64,512]{1,0:T(8,128)S(1)} collective-permute-done((f32[64,512]{1,0:T(8,128)S(1)}, f32[64,512]{1,0:T(8,128)S(1)}, u32[]{:S(2)}, u32[]{:S(2)}) %collective-permute-start.6) | collective-permute-done | bytes 131104 | tf_op jit(solution)/shard_map/ppermute | solution.py:261
  100.4 16.4 %all_to_all.71.got = f32[16,32,128]{2,1,0:T(8,128)S(1)} all-to-all(f32[16,32,128]{2,1,0:T(8,128)S(1)} %get-tuple-element.57), channel_id=1, replica_groups=mesh['xh'=2,'xl'=2,'z'=8,'y'=8,'core'=2] {'xl','z'}, dimensions={0} | all-to-all | bytes 524288 | tf_op jit(solution)/shard_map/all_to_all | solution.py:212
  117.5 12.1 %all_to_all.72 = f32[8,32,128]{2,1,0:T(8,128)S(1)} all-to-all(f32[8,32,128]{2,1,0:T(8,128)S(1)} %get-tuple-element.58), channel_id=1, replica_groups=mesh['xh'=2,'xl'=2,'z'=8,'y'=8,'core'=2] {'y'}, dimensions={0} | all-to-all | bytes 262144 | tf_op jit(solution)/shard_map/all_to_all | solution.py:212
  129.6 5.2 %all_gather.26 = f32[16,32,128]{2,1,0:T(8,128)S(1)} all-gather(f32[8,32,128]{2,1,0:T(8,128)S(1)} %all_to_all.72), channel_id=1, replica_groups=mesh['xh'=2,'xl'=2,'z'=8,'y'=8,'core'=2] {'core'}, dimensions={0}, use_global_device_ids=true | all-gather | bytes 393216 | tf_op jit(solution)/shard_map/all_gather | solution.py:270
  135.5 11.7 %all_to_all.73.got = f32[8,32,128]{2,1,0:T(8,128)S(1)} all-to-all(f32[8,32,128]{2,1,0:T(8,128)S(1)} %shard_map.73), channel_id=1, replica_groups=mesh['xh'=2,'xl'=2,'z'=8,'y'=8,'core'=2] {'z'}, dimensions={0} | all-to-all | bytes 262144 | tf_op jit(solution)/shard_map/all_to_all | solution.py:212
  147.8 10.4 %all_to_all.74 = f32[8,32,128]{2,1,0:T(8,128)S(1)} all-to-all(f32[8,32,128]{2,1,0:T(8,128)S(1)} %shard_map.74), channel_id=1, replica_groups=mesh['xh'=2,'xl'=2,'z'=8,'y'=8,'core'=2] {'y'}, dimensions={0} | all-to-all | bytes 262144 | tf_op jit(solution)/shard_map/all_to_all | solution.py:212
  158.2 4.8 %all_gather.27 = f32[16,32,128]{2,1,0:T(8,128)S(1)} all-gather(f32[8,32,128]{2,1,0:T(8,128)S(1)} %all_to_all.74), channel_id=1, replica_groups=mesh['xh'=2,'xl'=2,'z'=8,'y'=8,'core'=2] {'core'}, dimensions={0}, use_global_device_ids=true | all-gather | bytes 393216 | tf_op jit(solution)/shard_map/all_gather | solution.py:270
  164.0 10.8 %all_to_all.75.got = f32[8,32,128]{2,1,0:T(8,128)S(1)} all-to-all(f32[8,32,128]{2,1,0:T(8,128)S(1)} %get-tuple-element.61), channel_id=1, replica_groups=mesh['xh'=2,'xl'=2,'z'=8,'y'=8,'core'=2] {'z'}, dimensions={0} | all-to-all | bytes 262144 | tf_op jit(solution)/shard_map/all_to_all | solution.py:212
  175.4 10.3 %all_to_all.76 = f32[8,32,128]{2,1,0:T(8,128)S(1)} all-to-all(f32[8,32,128]{2,1,0:T(8,128)S(1)} %shard_map.76), channel_id=1, replica_groups=mesh['xh'=2,'xl'=2,'z'=8,'y'=8,'core'=2] {'y'}, dimensions={0} | all-to-all | bytes 262144 | tf_op jit(solution)/shard_map/all_to_all | solution.py:212
  185.8 4.3 %all_gather.28 = f32[16,32,128]{2,1,0:T(8,128)S(1)} all-gather(f32[8,32,128]{2,1,0:T(8,128)S(1)} %all_to_all.76), channel_id=1, replica_groups=mesh['xh'=2,'xl'=2,'z'=8,'y'=8,'core'=2] {'core'}, dimensions={0}, use_global_device_ids=true | all-gather | bytes 393216 | tf_op jit(solution)/shard_map/all_gather | solution.py:270
  190.9 12.0 %all_to_all.77.got = f32[16,32,128]{2,1,0:T(8,128)S(1)} all-to-all(f32[16,32,128]{2,1,0:T(8,128)S(1)} %shard_map.77), channel_id=1, replica_groups=mesh['xh'=2,'xl'=2,'z'=8,'y'=8,'core'=2] {'xl','z'}, dimensions={0} | all-to-all | bytes 524288 | tf_op jit(solution)/shard_map/all_to_all | solution.py:212
  204.2 3.4 %all-to-all-start.10 = ((f32[8,32,128]{2,1,0:T(8,128)}), f32[8,32,128]{2,1,0:T(8,128)S(1)}, u32[]{:S(2)}, u32[]{:S(2)}) async-start(f32[8,32,128]{2,1,0:T(8,128)} %shard_map.78), calls=%async_computation.10 | async-start | bytes 262144 | tf_op jit(solution)/shard_map/all_to_all | solution.py:212
  207.8 7.6 %all-to-all-done.10 = f32[8,32,128]{2,1,0:T(8,128)S(1)} async-done(((f32[8,32,128]{2,1,0:T(8,128)}), f32[8,32,128]{2,1,0:T(8,128)S(1)}, u32[]{:S(2)}, u32[]{:S(2)}) %all-to-all-start.10) | async-done | bytes 131104 | tf_op jit(solution)/shard_map/all_to_all | solution.py:212
  215.4 4.5 %all_gather.29 = f32[16,32,128]{2,1,0:T(8,128)S(1)} all-gather(f32[8,32,128]{2,1,0:T(8,128)S(1)} %all-to-all-done.10), channel_id=1, replica_groups=mesh['xh'=2,'xl'=2,'z'=8,'y'=8,'core'=2] {'core'}, dimensions={0}, use_global_device_ids=true | all-gather | bytes 393216 | tf_op jit(solution)/shard_map/all_gather | solution.py:270
  220.7 13.2 %all_to_all.78.got = f32[16,32,128]{2,1,0:T(8,128)S(1)} all-to-all(f32[16,32,128]{2,1,0:T(8,128)S(1)} %get-tuple-element.63), channel_id=1, replica_groups=mesh['xh'=2,'xl'=2,'z'=8,'y'=8,'core'=2] {'xl','z'}, dimensions={0} | all-to-all | bytes 524288 | tf_op jit(solution)/shard_map/all_to_all | solution.py:212
  234.6 12.1 %all_to_all.79 = f32[16,32,128]{2,1,0:T(8,128)S(1)} all-to-all(f32[16,32,128]{2,1,0:T(8,128)S(1)} %shard_map.81), channel_id=1, replica_groups=mesh['xh'=2,'xl'=2,'z'=8,'y'=8,'core'=2] {'xh','y'}, dimensions={0} | all-to-all | bytes 524288 | tf_op jit(solution)/shard_map/all_to_all | solution.py:212
  246.7 5.3 %all-gather.1 = f32[16,32,128]{2,1,0:T(8,128)S(1)} all-gather(f32[8,32,128]{2,1,0:T(8,128)S(1)} %slice.9), channel_id=3, replica_groups=mesh['xh'=2,'xl'=2,'z'=8,'y'=8,'core'=2] {'core'}, dimensions={0}, use_global_device_ids=true | all-gather | bytes 393216 | tf_op jit(solution)/shard_map/all_gather | solution.py:312
  252.0 13.6 %all_to_all.80 = f32[16,32,128]{2,1,0:T(8,128)S(1)} all-to-all(f32[16,32,128]{2,1,0:T(8,128)S(1)} %shard_map.82), channel_id=1, replica_groups=mesh['xh'=2,'xl'=2,'z'=8,'y'=8,'core'=2] {'xl','z'}, dimensions={0} | all-to-all | bytes 524288 | tf_op jit(solution)/shard_map/all_to_all | solution.py:212
  (48 shorter events, 19.9 us)
Async XLA Ops:
  0.1 1.2 copy-start.2
  1.3 1.0 copy-start.1
  1.3 1.1 copy-start.4
  4.2 24.4 %collective-permute-start = (f32[256,512]{1,0:T(8,128)S(1)}, f32[256,512]{1,0:T(8,128)S(1)}, u32[]{:S(2)}, u32[]{:S(2)}) collective-permute-start(f32[256,512]{1,0:T(8,128)S(1)} %get-tuple-element.39), channel_id=1, source_target_pairs={{0,1},{1,0},{2,3},{3,2},{4,5},{5,4},{6,7},{7,6},{8,9},{9,8},{10,11... | collective-permute-start | bytes 1572872 | tf_op jit(solution)/shard_map/ppermute | solution.py:277
  12.9 14.9 %all-to-all-start = ((f32[16,32,128]{2,1,0:T(8,128)}), f32[16,32,128]{2,1,0:T(8,128)S(1)}, u32[]{:S(2)}, u32[]{:S(2)}) async-start(f32[16,32,128]{2,1,0:T(8,128)} %shard_map.66), calls=%async_computation | async-start | bytes 524288 | tf_op jit(solution)/shard_map/all_to_all | solution.py:212
  18.7 0.7 copy-start.5
  19.4 0.7 copy-start.6
  53.9 45.7 %all-to-all-start.2 = ((f32[16,32,128]{2,1,0:T(8,128)}), f32[16,32,128]{2,1,0:T(8,128)S(1)}, u32[]{:S(2)}, u32[]{:S(2)}) async-start(f32[16,32,128]{2,1,0:T(8,128)} %shard_map.69), calls=%async_computation.2 | async-start | bytes 524288 | tf_op jit(solution)/shard_map/all_to_all | solution.py:212
  58.4 18.1 %collective-permute-start.1 = (f32[64,512]{1,0:T(8,128)}, f32[64,512]{1,0:T(8,128)S(1)}, u32[]{:S(2)}, u32[]{:S(2)}) collective-permute-start(f32[64,512]{1,0:T(8,128)} %get-tuple-element.50), channel_id=1, source_target_pairs={{0,2},{2,4},{4,6},{6,8},{8,10},{10,12},{12,14},{14,0},{1,3},{3,5},... | collective-permute-start | bytes 393224 | tf_op jit(solution)/shard_map/ppermute | solution.py:261
  61.9 19.5 %collective-permute-start.2 = (f32[64,512]{1,0:T(8,128)}, f32[64,512]{1,0:T(8,128)S(1)}, u32[]{:S(2)}, u32[]{:S(2)}) collective-permute-start(f32[64,512]{1,0:T(8,128)} %get-tuple-element.51), channel_id=1, source_target_pairs={{0,4},{2,6},{4,8},{6,10},{8,12},{10,14},{12,0},{14,2},{1,5},{3,7},... | collective-permute-start | bytes 393224 | tf_op jit(solution)/shard_map/ppermute | solution.py:261
  64.7 19.1 %collective-permute-start.7 = (f32[64,512]{1,0:T(8,128)S(1)}, f32[64,512]{1,0:T(8,128)S(1)}, u32[]{:S(2)}, u32[]{:S(2)}) collective-permute-start(f32[64,512]{1,0:T(8,128)S(1)} %get-tuple-element.56), channel_id=1, source_target_pairs={{0,14},{2,0},{4,2},{6,4},{8,6},{10,8},{12,10},{14,12},{1,15},{3,1}... | collective-permute-start | bytes 393224 | tf_op jit(solution)/shard_map/ppermute | solution.py:261
  68.8 15.0 %collective-permute-start.3 = (f32[64,512]{1,0:T(8,128)S(1)}, f32[64,512]{1,0:T(8,128)S(1)}, u32[]{:S(2)}, u32[]{:S(2)}) collective-permute-start(f32[64,512]{1,0:T(8,128)S(1)} %get-tuple-element.52), channel_id=1, source_target_pairs={{0,6},{2,8},{4,10},{6,12},{8,14},{10,0},{12,2},{14,4},{1,7},{3,9},... | collective-permute-start | bytes 393224 | tf_op jit(solution)/shard_map/ppermute | solution.py:261
  71.4 18.0 %collective-permute-start.4 = (f32[64,512]{1,0:T(8,128)S(1)}, f32[64,512]{1,0:T(8,128)S(1)}, u32[]{:S(2)}, u32[]{:S(2)}) collective-permute-start(f32[64,512]{1,0:T(8,128)S(1)} %get-tuple-element.53), channel_id=1, source_target_pairs={{0,8},{2,10},{4,12},{6,14},{8,0},{10,2},{12,4},{14,6},{1,9},{3,11}... | collective-permute-start | bytes 393224 | tf_op jit(solution)/shard_map/ppermute | solution.py:261
  76.5 12.9 %collective-permute-start.5 = (f32[64,512]{1,0:T(8,128)S(1)}, f32[64,512]{1,0:T(8,128)S(1)}, u32[]{:S(2)}, u32[]{:S(2)}) collective-permute-start(f32[64,512]{1,0:T(8,128)S(1)} %get-tuple-element.54), channel_id=1, source_target_pairs={{0,10},{2,12},{4,14},{6,0},{8,2},{10,4},{12,6},{14,8},{1,11},{3,13... | collective-permute-start | bytes 393224 | tf_op jit(solution)/shard_map/ppermute | solution.py:261
  81.5 17.5 %collective-permute-start.6 = (f32[64,512]{1,0:T(8,128)S(1)}, f32[64,512]{1,0:T(8,128)S(1)}, u32[]{:S(2)}, u32[]{:S(2)}) collective-permute-start(f32[64,512]{1,0:T(8,128)S(1)} %get-tuple-element.55), channel_id=1, source_target_pairs={{0,12},{2,14},{4,0},{6,2},{8,4},{10,6},{12,8},{14,10},{1,13},{3,15... | collective-permute-start | bytes 393224 | tf_op jit(solution)/shard_map/ppermute | solution.py:261
  147.2 15.8 %copy-start = (bf16[1,1,512,512]{3,2,1,0:T(8,128)(2,1)S(1)}, bf16[1,1,512,512]{3,2,1,0:T(8,128)(2,1)}, u32[]{:S(2)}) copy-start(bf16[1,1,512,512]{3,2,1,0:T(8,128)(2,1)} %param.9) | copy-start | bytes 1572868
  190.9 16.7 %copy-start.3 = (bf16[1,1,1,2,512,512]{5,4,3,2,1,0:T(8,128)(2,1)S(1)}, bf16[1,1,1,2,512,512]{5,4,3,2,1,0:T(8,128)(2,1)}, u32[]{:S(2)}) copy-start(bf16[1,1,1,2,512,512]{5,4,3,2,1,0:T(8,128)(2,1)} %block.3) | copy-start | bytes 3145732
  204.2 11.2 %all-to-all-start.10 = ((f32[8,32,128]{2,1,0:T(8,128)}), f32[8,32,128]{2,1,0:T(8,128)S(1)}, u32[]{:S(2)}, u32[]{:S(2)}) async-start(f32[8,32,128]{2,1,0:T(8,128)} %shard_map.78), calls=%async_computation.10 | async-start | bytes 262144 | tf_op jit(solution)/shard_map/all_to_all | solution.py:212

commit v9 on v7

--- a/solution.py
+++ b/solution.py
@@ -12,6 +12,7 @@
 ROW = ("xh", "xl", "z")
 COL = ("y", "core")
 ACROSS = ("xh", "y")
+BESIDE = ("xl", "y")
 F32 = jnp.float32
 BF16 = jnp.bfloat16
 ROOMY = pltpu.CompilerParams(vmem_limit_bytes=40 * 1024 * 1024)
@@ -82,41 +83,54 @@
     high = (mine >= 1).astype(F32)
     late = (mine >= 2).astype(F32)
     image = jnp.where(row < top, row + top, row)
+    one = high - late
+    below_late = row + jnp.where(row < count - top // 2, top // 2, 0)
+    above_one = row - jnp.where(row >= count - top // 2, top // 2, 0)
+    flags = lax.broadcasted_iota(jnp.int32, (1, count), 1)
     rows = [
         line(upper_t, image) * (levels == 0).astype(F32) * low,
-        line(upper_t, row) * (levels == 1).astype(F32) * high,
+        line(upper_t, below_late) * (levels == 1).astype(F32) * high,
         line(upper_t, row) * (levels == 2).astype(F32) * late,
         line(lower_t, row) * (levels == 3).astype(F32) * late,
-        line(lower_t, row) * high,
+        line(lower_t, above_one) * high,
         line(lower_t, col) * high,
-        high,
+        jnp.where(flags == 0, high, jnp.where(flags == 1, late, one)),
     ]
     rows = rows + [jnp.zeros((1, count), F32)] * (out.shape[0] - len(rows))
     out[...] = jnp.concatenate(rows, 0)
 
 
-def turn_kernel(block, out):
-    turned = block[0, 0, 0, 0].astype(F32).T
-    ncol, piece = out.shape[0], out.shape[1]
+def turn_kernel(blocks, out, block, turned, arrived, gone):
+    copy = pltpu.make_async_copy(blocks.at[0, 0, 0, 1], block, arrived)
+    copy.start()
+    copy.wait()
+    whole = block[...].astype(F32).T
+    ncol, piece = turned.shape[0], turned.shape[1]
     ny = ncol // 2
     for y in range(ny):
         for core in range(2):
             start = (core * ny + y) * piece
-            out[2 * y + core] = turned[start:start + piece]
-
-
-def turn_whole_kernel(block, out):
-    out[...] = block[0, 0, 0, 0].astype(F32).T.astype(BF16)
-
-
-def slot_call(body, shape, factor, slot):
+            turned[2 * y + core] = whole[start:start + piece]
+    copy = pltpu.make_async_copy(turned, out, gone)
+    copy.start()
+    copy.wait()
+
+
+def turn_whole_kernel(blocks, out, block, arrived):
+    copy = pltpu.make_async_copy(blocks.at[0, 0, 0, 0], block, arrived)
+    copy.start()
+    copy.wait()
+    out[...] = block[...].astype(F32).T.astype(BF16)
+
+
+def slot_call(body, shape, factor, space, scratch):
     width = factor.shape[-1]
     return pl.pallas_call(
         body,
         out_shape=shape,
-        grid=(1,),
-        in_specs=[pl.BlockSpec((1, 1, 1, 1, width, width), lambda k: (0, 0, 0, slot, 0, 0))],
-        out_specs=pl.BlockSpec(shape.shape, lambda k: (0,) * len(shape.shape)),
+        in_specs=[pl.BlockSpec(memory_space=pltpu.HBM)],
+        out_specs=pl.BlockSpec(memory_space=space),
+        scratch_shapes=[pltpu.VMEM((width, width), BF16)] + scratch,
         compiler_params=ROOMY,
     )(factor)
 
@@ -136,29 +150,38 @@
         out[k] = total
 
 
-def sum_keep_kernel(line, first, table, got, out, part_out):
-    sum_kernel(line, first, table, got, out)
-    part_out[...] = out[0]
-
-
-def sum_more_kernel(line, first, table, got, part, out):
-    total = part[...]
-    for k in range(got.shape[0]):
-        total = total + table[line, first + k] * got[k]
-    for k in range(out.shape[0]):
-        out[k] = total
+def halves(out, panel, piece):
+    slices = panel.reshape(panel.shape[0] // piece, piece, panel.shape[1])
+    count = slices.shape[0]
+    out[:count] = slices[:, :piece // 2]
+    out[count:] = slices[:, piece // 2:]
+
+
+def joined(update):
+    cores, parts, ny = update.shape[:3]
+    return jnp.concatenate(
+        [
+            update[core, part, y]
+            for core in range(cores)
+            for y in range(ny)
+            for part in range(parts)
+        ],
+        0,
+    )
 
 
 def one_kernel(update, base, up, own, rest_out, out):
+    rows = own.shape[0] // 2
     rest = base[...] - update[...]
     rest_out[...] = rest
-    out[...] = product(own[...], product(up[...], rest)).reshape(out.shape)
-
-
-def two_kernel(update, rest, up, own, out):
+    halves(out, product(own[rows:], product(up[...], rest)), 2 * out.shape[1])
+
+
+def two_kernel(table, update, rest_in, up, own, rest_out, out):
     rows = own.shape[0] // 2
-    y = product(up[...], rest[...] - update[...])
-    out[...] = product(own[rows:], y).reshape(out.shape)
+    rest = rest_in[...] - joined(update) * table[FLAGS, 1]
+    rest_out[...] = rest
+    out[...] = product(own[rows:], product(up[...], rest)).reshape(out.shape)
 
 
 def three_kernel(update, rest, up, low, own, y_out, out):
@@ -168,13 +191,15 @@
     out[...] = product(own[rows:], product(low[...], y)).reshape(out.shape)
 
 
-def two_back_kernel(update, y, low, own, out):
-    x = product(low[...], y[...] - update[...])
-    out[...] = product(own[...], x).reshape(out.shape)
-
-
-def one_back_kernel(update, y, low, below, x_out, out):
-    x = product(low[...], y[...] - update[...])
+def two_back_kernel(update, y, low, own, rest_out, out):
+    rows = own.shape[0] // 2
+    rest = y[...] - update[...]
+    rest_out[...] = rest
+    halves(out, product(own[:rows], product(low[...], rest)), 2 * out.shape[1])
+
+
+def one_back_kernel(table, update, rest, low, below, x_out, out):
+    x = product(low[...], rest[...] - joined(update) * table[FLAGS, 2])
     x_out[...] = x
     out[...] = product(below[...], x).reshape(out.shape)
 
@@ -210,14 +235,20 @@
     row = lax.axis_index(ROW)
     col = lax.axis_index(COL)
     panel = shape_of(width, nrhs)
-    slice_ = shape_of(piece, nrhs)
+    half_to_top = shape_of(top, piece // 2, nrhs)
     copies = shape_of(ny, piece, nrhs)
     across = shape_of(2 * ny, piece, nrhs)
     to_top = shape_of(top, piece, nrhs)
     to_late = shape_of(nz, piece, nrhs)
 
-    sent = slot_call(turn_kernel, shape_of(ncol, piece, width), factor, 1)
-    below = slot_call(turn_whole_kernel, shape_of(width, width, kind=BF16), factor, 0)
+    sent = slot_call(
+        turn_kernel, shape_of(ncol, piece, width), factor, pltpu.HBM,
+        [pltpu.VMEM((ncol, piece, width), F32), pltpu.SemaphoreType.DMA, pltpu.SemaphoreType.DMA],
+    )
+    below = slot_call(
+        turn_whole_kernel, shape_of(width, width, kind=BF16), factor, pltpu.VMEM,
+        [pltpu.SemaphoreType.DMA],
+    )
     table = call(
         table_kernel, shape_of(8, count),
         jnp.stack([row, col]).astype(jnp.int32), parents[None, :], parents[:, None],
@@ -239,24 +270,26 @@
     def spread(copied):
         return whole(a2a(copied, "y"))
 
+    def spread_halves(copied):
+        both = lax.all_gather(a2a(copied, BESIDE), "core", tiled=True)
+        return both.reshape(ncol // ny, 2, ny, piece // 2, nrhs)
+
     out, own = call(leaf_kernel, (to_top, shape_of(width, width, kind=BF16)), slices, y0)
     got = total(FROM_LEAF, 0, a2a(out, HALF), across)
     update = whole(a2a(got, ACROSS)[:ny])
-    rest, out = call(one_kernel, (panel, to_top), update, base, up, own)
-    got, part = call(
-        functools.partial(sum_keep_kernel, FROM_ONE, top), (copies, slice_),
-        table, a2a(out, HALF), scalars=1,
-    )
-    out = call(two_kernel, to_late, spread(got), rest, up, own)
-    got = call(
-        functools.partial(sum_more_kernel, FROM_TWO, late), copies,
-        table, a2a(out, "z"), part, scalars=1,
-    )
+    rest, out = call(one_kernel, (panel, half_to_top), update, base, up, own)
+    got = total(FROM_ONE, top, a2a(out, HALF), half_to_top)
+    rest, out = call(
+        two_kernel, (panel, to_late), table, spread_halves(got), rest, up, own, scalars=1
+    )
+    got = total(FROM_TWO, late, a2a(out, "z"), copies)
     y, out = call(three_kernel, (panel, to_late), spread(got), rest, up, low, own)
     got = total(FROM_THREE, late, a2a(out, "z"), copies)
-    out = call(two_back_kernel, to_top, spread(got), y, low, own)
-    got = total(FROM_ABOVE, top, a2a(out, HALF), copies)
-    x, out = call(one_back_kernel, (panel, to_top), spread(got), y, low, below)
+    rest, out = call(two_back_kernel, (panel, half_to_top), spread(got), y, low, own)
+    got = total(FROM_ABOVE, top, a2a(out, HALF), half_to_top)
+    x, out = call(
+        one_back_kernel, (panel, to_top), table, spread_halves(got), rest, low, below, scalars=1
+    )
     got = total(TO_COLUMN, top, a2a(out, HALF), across)
     got = a2a(got, ACROSS)[ny:]
     got = lax.all_gather(got, "core")

time: 244 us -> 239 us (0.980)
  blocking collectives: 191 us -> 185 us
    all_gather x5 -> x3, blocking collectives: 23.8 us -> 14.3 us  [whole(): return lax.all_gather(half, 'core', tiled=True).reshape(width, nrhs)]
    all_gather x0 -> x2, blocking collectives: none -> 9.44 us  [spread_halves(): both = lax.all_gather(a2a(copied, BESIDE), 'core', tiled=True)]
    all_to_all x13, blocking collectives: 162 us -> 156 us  [a2a(): lax.all_to_all(array, axes, 0, 0, tiled=True)]
  transfers between devices with their start and end apart: 1 -> 1, of which waited for: 1 -> 1; matrix products, arithmetic and copies ran while one was open for 0% -> 0% of each run, Pallas kernels for 0% -> 1%
where the time goes in v9:
time: 239 us; the launch traced here: 237 us
  blocking collectives  185 us (77%)
  waiting for transfers between devices  24.5 us (10%)
  Pallas kernels  12.6 us (5%)
  starting transfers between devices  10.5 us (4%)
  local copies, waits for them, and re-layouts  3.75 us (2%)
    all_to_all x13, blocking collectives, a2a(): lax.all_to_all(array, axes, 0, 0, tiled=True)  156 us
    all_to_all x1, waiting for transfers between devices, per_device(): slices = lax.all_to_all(sent, COL, 0, 0, tiled=True)  24.5 us
    all_gather x3, blocking collectives, whole(): return lax.all_gather(half, 'core', tiled=True).reshape(width, nrhs)  14.3 us
    pallas_call x15, Pallas kernels, call(): pl.pallas_call(body, out_shape=shape, in_specs=[SM] * scalars + [VM] * (l...  12 us
    all_to_all x1, starting transfers between devices, per_device(): slices = lax.all_to_all(sent, COL, 0, 0, tiled=True)  10.5 us
    all_gather x2, blocking collectives, spread_halves(): both = lax.all_gather(a2a(copied, BESIDE), 'core', tiled=True)  9.44 us
    all_gather x1, blocking collectives, per_device(): got = lax.all_gather(got, 'core')  5.25 us
  transfers between devices with their start and end apart: 1, of which 1 were waited for; matrix products, arithmetic and copies ran while one was open for 0% of the time, Pallas kernels for 1%

profile of v9, /device:TPU:1, one launch (start us, length us, event | category | flops | bytes accessed | tf_op | source)
XLA Modules:
  0.0 237.4 jit_solution(14719732567278047686)
XLA Ops:
  0.0 1.2 copy-done.2
  1.6 1.0 copy-done.4
  2.6 10.5 %all-to-all-start = ((f32[16,32,512]{2,1,0:T(8,128)}), f32[16,32,512]{2,1,0:T(8,128)S(1)}, u32[]{:S(2)}, u32[]{:S(2)}) async-start(f32[16,32,512]{2,1,0:T(8,128)} %copy-done.4), calls=%async_computation | async-start | bytes 2097152 | tf_op jit(solution)/shard_map/all_to_all | solution.py:259
  13.3 0.7 copy-done.6
  14.1 0.7 copy-done.7
  14.9 1.0 shard_map.64.table
  16.5 24.5 %all-to-all-done.slices = f32[16,32,512]{2,1,0:T(8,128)S(1)} async-done(((f32[16,32,512]{2,1,0:T(8,128)}), f32[16,32,512]{2,1,0:T(8,128)S(1)}, u32[]{:S(2)}, u32[]{:S(2)}) %all-to-all-start) | async-done | bytes 1048608 | tf_op jit(solution)/shard_map/all_to_all | solution.py:259
  41.5 19.0 %all_to_all.70.got = f32[16,32,128]{2,1,0:T(8,128)S(1)} all-to-all(f32[16,32,128]{2,1,0:T(8,128)S(1)} %get-tuple-element.27), channel_id=1, replica_groups=mesh['xh'=2,'xl'=2,'z'=8,'y'=8,'core'=2] {'xl','z'}, dimensions={0} | all-to-all | bytes 524288 | tf_op jit(solution)/shard_map/all_to_all | solution.py:221
  61.1 13.5 %all_to_all.71 = f32[16,32,128]{2,1,0:T(8,128)S(1)} all-to-all(f32[16,32,128]{2,1,0:T(8,128)S(1)} %shard_map.68), channel_id=1, replica_groups=mesh['xh'=2,'xl'=2,'z'=8,'y'=8,'core'=2] {'xh','y'}, dimensions={0} | all-to-all | bytes 524288 | tf_op jit(solution)/shard_map/all_to_all | solution.py:221
  74.6 5.1 %all_gather.21 = f32[16,32,128]{2,1,0:T(8,128)S(1)} all-gather(f32[8,32,128]{2,1,0:T(8,128)S(1)} %slice.8), channel_id=1, replica_groups=mesh['xh'=2,'xl'=2,'z'=8,'y'=8,'core'=2] {'core'}, dimensions={0}, use_global_device_ids=true | all-gather | bytes 393216 | tf_op jit(solution)/shard_map/all_gather | solution.py:268
  79.7 0.7 shard_map.69
  80.4 11.6 %all_to_all.72.got = f32[16,16,128]{2,1,0:T(8,128)S(1)} all-to-all(f32[16,16,128]{2,1,0:T(8,128)S(1)} %get-tuple-element.31), channel_id=1, replica_groups=mesh['xh'=2,'xl'=2,'z'=8,'y'=8,'core'=2] {'xl','z'}, dimensions={0} | all-to-all | bytes 262144 | tf_op jit(solution)/shard_map/all_to_all | solution.py:221
  92.6 11.7 %all_to_all.73 = f32[16,16,128]{2,1,0:T(8,128)S(1)} all-to-all(f32[16,16,128]{2,1,0:T(8,128)S(1)} %shard_map.70), channel_id=1, replica_groups=mesh['xh'=2,'xl'=2,'z'=8,'y'=8,'core'=2] {'xl','y'}, dimensions={0} | all-to-all | bytes 262144 | tf_op jit(solution)/shard_map/all_to_all | solution.py:221
  104.3 5.1 %all_gather.22 = f32[32,16,128]{2,1,0:T(8,128)S(1)} all-gather(f32[16,16,128]{2,1,0:T(8,128)S(1)} %all_to_all.73), channel_id=1, replica_groups=mesh['xh'=2,'xl'=2,'z'=8,'y'=8,'core'=2] {'core'}, dimensions={0}, use_global_device_ids=true | all-gather | bytes 393216 | tf_op jit(solution)/shard_map/all_gather | solution.py:274
  109.4 1.3 shard_map.71
  110.7 10.4 %all_to_all.74.got = f32[8,32,128]{2,1,0:T(8,128)S(1)} all-to-all(f32[8,32,128]{2,1,0:T(8,128)S(1)} %get-tuple-element.33), channel_id=1, replica_groups=mesh['xh'=2,'xl'=2,'z'=8,'y'=8,'core'=2] {'z'}, dimensions={0} | all-to-all | bytes 262144 | tf_op jit(solution)/shard_map/all_to_all | solution.py:221
  121.7 10.7 %all_to_all.75 = f32[8,32,128]{2,1,0:T(8,128)S(1)} all-to-all(f32[8,32,128]{2,1,0:T(8,128)S(1)} %shard_map.72), channel_id=1, replica_groups=mesh['xh'=2,'xl'=2,'z'=8,'y'=8,'core'=2] {'y'}, dimensions={0} | all-to-all | bytes 262144 | tf_op jit(solution)/shard_map/all_to_all | solution.py:221
  132.4 4.9 %all_gather.23 = f32[16,32,128]{2,1,0:T(8,128)S(1)} all-gather(f32[8,32,128]{2,1,0:T(8,128)S(1)} %all_to_all.75), channel_id=1, replica_groups=mesh['xh'=2,'xl'=2,'z'=8,'y'=8,'core'=2] {'core'}, dimensions={0}, use_global_device_ids=true | all-gather | bytes 393216 | tf_op jit(solution)/shard_map/all_gather | solution.py:268
  137.3 1.0 shard_map.73
  138.3 10.8 %all_to_all.76.got = f32[8,32,128]{2,1,0:T(8,128)S(1)} all-to-all(f32[8,32,128]{2,1,0:T(8,128)S(1)} %get-tuple-element.36), channel_id=1, replica_groups=mesh['xh'=2,'xl'=2,'z'=8,'y'=8,'core'=2] {'z'}, dimensions={0} | all-to-all | bytes 262144 | tf_op jit(solution)/shard_map/all_to_all | solution.py:221
  149.8 10.3 %all_to_all.77 = f32[8,32,128]{2,1,0:T(8,128)S(1)} all-to-all(f32[8,32,128]{2,1,0:T(8,128)S(1)} %shard_map.74), channel_id=1, replica_groups=mesh['xh'=2,'xl'=2,'z'=8,'y'=8,'core'=2] {'y'}, dimensions={0} | all-to-all | bytes 262144 | tf_op jit(solution)/shard_map/all_to_all | solution.py:221
  160.1 4.3 %all_gather.24 = f32[16,32,128]{2,1,0:T(8,128)S(1)} all-gather(f32[8,32,128]{2,1,0:T(8,128)S(1)} %all_to_all.77), channel_id=1, replica_groups=mesh['xh'=2,'xl'=2,'z'=8,'y'=8,'core'=2] {'core'}, dimensions={0}, use_global_device_ids=true | all-gather | bytes 393216 | tf_op jit(solution)/shard_map/all_gather | solution.py:268
  164.4 0.7 shard_map.75
  165.1 10.1 %all_to_all.78.got = f32[16,16,128]{2,1,0:T(8,128)S(1)} all-to-all(f32[16,16,128]{2,1,0:T(8,128)S(1)} %get-tuple-element.38), channel_id=1, replica_groups=mesh['xh'=2,'xl'=2,'z'=8,'y'=8,'core'=2] {'xl','z'}, dimensions={0} | all-to-all | bytes 262144 | tf_op jit(solution)/shard_map/all_to_all | solution.py:221
  175.8 10.0 %all_to_all.79 = f32[16,16,128]{2,1,0:T(8,128)S(1)} all-to-all(f32[16,16,128]{2,1,0:T(8,128)S(1)} %shard_map.76), channel_id=1, replica_groups=mesh['xh'=2,'xl'=2,'z'=8,'y'=8,'core'=2] {'xl','y'}, dimensions={0} | all-to-all | bytes 262144 | tf_op jit(solution)/shard_map/all_to_all | solution.py:221
  185.8 4.3 %all_gather.25 = f32[32,16,128]{2,1,0:T(8,128)S(1)} all-gather(f32[16,16,128]{2,1,0:T(8,128)S(1)} %all_to_all.79), channel_id=1, replica_groups=mesh['xh'=2,'xl'=2,'z'=8,'y'=8,'core'=2] {'core'}, dimensions={0}, use_global_device_ids=true | all-gather | bytes 393216 | tf_op jit(solution)/shard_map/all_gather | solution.py:274
  190.1 1.4 shard_map.77
  191.5 12.5 %all_to_all.80.got = f32[16,32,128]{2,1,0:T(8,128)S(1)} all-to-all(f32[16,32,128]{2,1,0:T(8,128)S(1)} %get-tuple-element.41), channel_id=1, replica_groups=mesh['xh'=2,'xl'=2,'z'=8,'y'=8,'core'=2] {'xl','z'}, dimensions={0} | all-to-all | bytes 524288 | tf_op jit(solution)/shard_map/all_to_all | solution.py:221
  204.7 12.5 %all_to_all.81 = f32[16,32,128]{2,1,0:T(8,128)S(1)} all-to-all(f32[16,32,128]{2,1,0:T(8,128)S(1)} %shard_map.78), channel_id=1, replica_groups=mesh['xh'=2,'xl'=2,'z'=8,'y'=8,'core'=2] {'xh','y'}, dimensions={0} | all-to-all | bytes 524288 | tf_op jit(solution)/shard_map/all_to_all | solution.py:221
  217.2 5.3 %all-gather = f32[16,32,128]{2,1,0:T(8,128)S(1)} all-gather(f32[8,32,128]{2,1,0:T(8,128)S(1)} %slice.9), channel_id=2, replica_groups=mesh['xh'=2,'xl'=2,'z'=8,'y'=8,'core'=2] {'core'}, dimensions={0}, use_global_device_ids=true | all-gather | bytes 393216 | tf_op jit(solution)/shard_map/all_gather | solution.py:295
  222.5 13.2 %all_to_all.82 = f32[16,32,128]{2,1,0:T(8,128)S(1)} all-to-all(f32[16,32,128]{2,1,0:T(8,128)S(1)} %shard_map.79), channel_id=1, replica_groups=mesh['xh'=2,'xl'=2,'z'=8,'y'=8,'core'=2] {'xl','z'}, dimensions={0} | all-to-all | bytes 524288 | tf_op jit(solution)/shard_map/all_to_all | solution.py:221
  235.6 1.8 shard_map.80
  (28 shorter events, 5.7 us)
Async XLA Ops:
  0.0 1.2 copy-start.2
  1.6 1.0 copy-start.4
  2.6 10.5 %copy-start.3 = (bf16[1,1,1,2,512,512]{5,4,3,2,1,0:T(8,128)(2,1)S(1)}, bf16[1,1,1,2,512,512]{5,4,3,2,1,0:T(8,128)(2,1)}, u32[]{:S(2)}) copy-start(bf16[1,1,1,2,512,512]{5,4,3,2,1,0:T(8,128)(2,1)} %blocks.3) | copy-start | bytes 3145732
  2.6 38.4 %all-to-all-start = ((f32[16,32,512]{2,1,0:T(8,128)}), f32[16,32,512]{2,1,0:T(8,128)S(1)}, u32[]{:S(2)}, u32[]{:S(2)}) async-start(f32[16,32,512]{2,1,0:T(8,128)} %copy-done.4), calls=%async_computation | async-start | bytes 2097152 | tf_op jit(solution)/shard_map/all_to_all | solution.py:259
  13.0 2.9 %copy-start.1 = (bf16[1,1,512,512]{3,2,1,0:T(8,128)(2,1)S(1)}, bf16[1,1,512,512]{3,2,1,0:T(8,128)(2,1)}, u32[]{:S(2)}) copy-start(bf16[1,1,512,512]{3,2,1,0:T(8,128)(2,1)} %param.8) | copy-start | bytes 1572868
  13.0 2.9 %copy-start.5 = (f32[1,1,512,128]{3,2,1,0:T(8,128)S(1)}, f32[1,1,512,128]{3,2,1,0:T(8,128)}, u32[]{:S(2)}) copy-start(f32[1,1,512,128]{3,2,1,0:T(8,128)} %param.7) | copy-start | bytes 786436
  13.3 0.7 copy-start.6
  14.1 0.7 copy-start.7
  121.1 16.2 %copy-start = (bf16[1,1,512,512]{3,2,1,0:T(8,128)(2,1)S(1)}, bf16[1,1,512,512]{3,2,1,0:T(8,128)(2,1)}, u32[]{:S(2)}) copy-start(bf16[1,1,512,512]{3,2,1,0:T(8,128)(2,1)} %param.9) | copy-start | bytes 1572868

commit v10 on v9

--- a/solution.py
+++ b/solution.py
@@ -19,7 +19,7 @@
 VM = pl.BlockSpec(memory_space=pltpu.VMEM)
 SM = pl.BlockSpec(memory_space=pltpu.SMEM)
 
-FROM_LEAF, FROM_ONE, FROM_TWO, FROM_THREE, FROM_ABOVE, TO_COLUMN, FLAGS = range(7)
+FROM_LEAF, FROM_ONE, FROM_TWO, FROM_THREE, FROM_ABOVE, TO_COLUMN, HIGH = range(7)
 
 
 def shape_of(*dims, kind=F32):
@@ -47,7 +47,7 @@
     return full[:, :cols] + full[:, cols:2 * cols] + full[:, 2 * cols:]
 
 
-def table_kernel(at, parents_row, parents_col, mask, mask_t, out):
+def table_kernel(at, parents_row, parents_col, mask, out):
     count = mask.shape[0]
     top = count // 2
     row, col = at[0], at[1]
@@ -62,14 +62,12 @@
         power_t = jnp.dot(step_t, power_t, preferred_element_type=F32)
         anc = anc + power
         anc_t = anc_t + power_t
-    anc = jnp.minimum(anc, 1.0)
-    anc_t = jnp.minimum(anc_t, 1.0)
-    weights_t = mask_t[...].astype(F32) * (1.0 - identity)
-    upper_t = weights_t * anc_t
-    lower_t = weights_t * anc
-
-    def line(matrix, index):
-        return jnp.sum(jnp.where(down == index, matrix, 0.0), axis=0, keepdims=True)
+    weights = mask[...].astype(F32) * (1.0 - identity)
+    upper = weights * jnp.minimum(anc, 1.0)
+    lower = weights * jnp.minimum(anc_t, 1.0)
+
+    def column(matrix, index):
+        return jnp.sum(jnp.where(across == index, matrix, 0.0), axis=1, keepdims=True)
 
     def level(ids):
         total = jnp.zeros_like(ids)
@@ -77,27 +75,25 @@
             total = total + (ids >= count - count // 2**depth).astype(jnp.int32)
         return total
 
-    levels = level(lax.broadcasted_iota(jnp.int32, (1, count), 1))
-    mine = level(jnp.full((1, count), row, jnp.int32))
+    levels = level(lax.broadcasted_iota(jnp.int32, (count, 1), 0))
+    mine = level(jnp.full((count, 1), row, jnp.int32))
     low = (mine == 0).astype(F32)
     high = (mine >= 1).astype(F32)
     late = (mine >= 2).astype(F32)
     image = jnp.where(row < top, row + top, row)
-    one = high - late
     below_late = row + jnp.where(row < count - top // 2, top // 2, 0)
     above_one = row - jnp.where(row >= count - top // 2, top // 2, 0)
-    flags = lax.broadcasted_iota(jnp.int32, (1, count), 1)
-    rows = [
-        line(upper_t, image) * (levels == 0).astype(F32) * low,
-        line(upper_t, below_late) * (levels == 1).astype(F32) * high,
-        line(upper_t, row) * (levels == 2).astype(F32) * late,
-        line(lower_t, row) * (levels == 3).astype(F32) * late,
-        line(lower_t, above_one) * high,
-        line(lower_t, col) * high,
-        jnp.where(flags == 0, high, jnp.where(flags == 1, late, one)),
+    lines = [
+        column(upper, image) * (levels == 0).astype(F32) * low,
+        column(upper, below_late) * (levels == 1).astype(F32) * high,
+        column(upper, row) * (levels == 2).astype(F32) * late,
+        column(lower, row) * (levels == 3).astype(F32) * late,
+        column(lower, above_one) * high,
+        column(lower, col) * high,
+        high,
     ]
-    rows = rows + [jnp.zeros((1, count), F32)] * (out.shape[0] - len(rows))
-    out[...] = jnp.concatenate(rows, 0)
+    for index, values in enumerate(lines):
+        out[index] = jnp.broadcast_to(values, (count, out.shape[2]))
 
 
 def turn_kernel(blocks, out, block, turned, arrived, gone):
@@ -131,7 +127,7 @@
         in_specs=[pl.BlockSpec(memory_space=pltpu.HBM)],
         out_specs=pl.BlockSpec(memory_space=space),
         scratch_shapes=[pltpu.VMEM((width, width), BF16)] + scratch,
-        compiler_params=ROOMY,
+        compiler_params=pltpu.CompilerParams(vmem_limit_bytes=60 * 1024 * 1024),
     )(factor)
 
 
@@ -142,12 +138,12 @@
     out[...] = product(own, y0[...]).reshape(out.shape)
 
 
-def sum_kernel(line, first, table, got, out):
-    total = table[line, first] * got[0]
+def sum_kernel(line, first, start, stop, table, got, out):
+    total = table[line, first:first + 1] * got[0]
     for k in range(1, got.shape[0]):
-        total = total + table[line, first + k] * got[k]
+        total = total + table[line, first + k:first + k + 1] * got[k]
     for k in range(out.shape[0]):
-        out[k] = total
+        out[k] = total if start <= k < stop else jnp.zeros_like(total)
 
 
 def halves(out, panel, piece):
@@ -177,9 +173,9 @@
     halves(out, product(own[rows:], product(up[...], rest)), 2 * out.shape[1])
 
 
-def two_kernel(table, update, rest_in, up, own, rest_out, out):
+def two_kernel(update, rest_in, up, own, rest_out, out):
     rows = own.shape[0] // 2
-    rest = rest_in[...] - joined(update) * table[FLAGS, 1]
+    rest = rest_in[...] - joined(update)
     rest_out[...] = rest
     out[...] = product(own[rows:], product(up[...], rest)).reshape(out.shape)
 
@@ -198,8 +194,8 @@
     halves(out, product(own[:rows], product(low[...], rest)), 2 * out.shape[1])
 
 
-def one_back_kernel(table, update, rest, low, below, x_out, out):
-    x = product(low[...], rest[...] - joined(update) * table[FLAGS, 2])
+def one_back_kernel(update, rest, low, below, x_out, out):
+    x = product(low[...], rest[...] - joined(update))
     x_out[...] = x
     out[...] = product(below[...], x).reshape(out.shape)
 
@@ -213,7 +209,7 @@
 
 def last_kernel(table, update, y0, low, x, out):
     leaf = product(low[...], y0[...] - update[...])
-    out[0, 0] = jnp.where(table[FLAGS, 0] > 0.5, x[...], leaf)
+    out[0, 0] = jnp.where(table[HIGH, 0:1] > 0.5, x[...], leaf)
 
 
 def a2a(array, axes):
@@ -250,9 +246,9 @@
         [pltpu.SemaphoreType.DMA],
     )
     table = call(
-        table_kernel, shape_of(8, count),
+        table_kernel, shape_of(HIGH + 1, count, nrhs),
         jnp.stack([row, col]).astype(jnp.int32), parents[None, :], parents[:, None],
-        block_mask, block_mask.T, scalars=1,
+        block_mask, scalars=1,
     )
     y0 = jnp.dot(up.astype(F32), base, precision=lax.Precision.HIGHEST)
 
@@ -261,8 +257,9 @@
         (table, y0, base, up, low, below, slices)
     )
 
-    def total(line, first, got, shape):
-        return call(functools.partial(sum_kernel, line, first), shape, table, got, scalars=1)
+    def total(line, first, got, shape, start=0, stop=ncol):
+        body = functools.partial(sum_kernel, line, first, start, stop)
+        return call(body, shape, table, got)
 
     def whole(half):
         return lax.all_gather(half, "core", tiled=True).reshape(width, nrhs)
@@ -275,28 +272,28 @@
         return both.reshape(ncol // ny, 2, ny, piece // 2, nrhs)
 
     out, own = call(leaf_kernel, (to_top, shape_of(width, width, kind=BF16)), slices, y0)
-    got = total(FROM_LEAF, 0, a2a(out, HALF), across)
+    got = total(FROM_LEAF, 0, a2a(out, HALF), across, start=ny)
     update = whole(a2a(got, ACROSS)[:ny])
     rest, out = call(one_kernel, (panel, half_to_top), update, base, up, own)
-    got = total(FROM_ONE, top, a2a(out, HALF), half_to_top)
+    got = total(FROM_ONE, top, a2a(out, HALF), half_to_top, start=ny)
     rest, out = call(
-        two_kernel, (panel, to_late), table, spread_halves(got), rest, up, own, scalars=1
+        two_kernel, (panel, to_late), spread_halves(got), rest, up, own
     )
     got = total(FROM_TWO, late, a2a(out, "z"), copies)
     y, out = call(three_kernel, (panel, to_late), spread(got), rest, up, low, own)
     got = total(FROM_THREE, late, a2a(out, "z"), copies)
     rest, out = call(two_back_kernel, (panel, half_to_top), spread(got), y, low, own)
-    got = total(FROM_ABOVE, top, a2a(out, HALF), half_to_top)
+    got = total(FROM_ABOVE, top, a2a(out, HALF), half_to_top, stop=ny)
     x, out = call(
-        one_back_kernel, (panel, to_top), table, spread_halves(got), rest, low, below, scalars=1
-    )
-    got = total(TO_COLUMN, top, a2a(out, HALF), across)
+        one_back_kernel, (panel, to_top), spread_halves(got), rest, low, below
+    )
+    got = total(TO_COLUMN, top, a2a(out, HALF), across, stop=ny)
     got = a2a(got, ACROSS)[ny:]
     got = lax.all_gather(got, "core")
     out = call(order_kernel, to_top, got)
     update = a2a(out, HALF).reshape(width, nrhs)
     return call(
-        last_kernel, shape_of(1, 1, width, nrhs), table, update, y0, low, x, scalars=1
+        last_kernel, shape_of(1, 1, width, nrhs), table, update, y0, low, x
     )
 
 

time: 239 us -> 234 us (0.979)
  local copies, waits for them, and re-layouts: 3.75 us -> 1.33 us
    pallas_call x15, Pallas kernels: 12 us -> 6.59 us  [call(): pl.pallas_call(body, out_shape=shape, in_specs=[SM] * scalars + [VM] * (l...]
    pallas_call x2, Pallas kernels: 0.61 us -> 4.41 us  [slot_call(): pl.pallas_call(body, out_shape=shape, in_specs=[pl.BlockSpec(memory_space...]
    unnamed x17 -> x12, local copies, waits for them, and re-layouts: 3.65 us -> 1.22 us
where the time goes in v10:
time: 234 us; the launch traced here: 232 us
  blocking collectives  186 us (79%)
  waiting for transfers between devices  22.7 us (10%)
  Pallas kernels  11 us (5%)
  starting transfers between devices  10.3 us (4%)
    all_to_all x13, blocking collectives, a2a(): lax.all_to_all(array, axes, 0, 0, tiled=True)  156 us
    all_to_all x1, waiting for transfers between devices, per_device(): slices = lax.all_to_all(sent, COL, 0, 0, tiled=True)  22.7 us
    all_gather x3, blocking collectives, whole(): return lax.all_gather(half, 'core', tiled=True).reshape(width, nrhs)  14.4 us
    all_to_all x1, starting transfers between devices, per_device(): slices = lax.all_to_all(sent, COL, 0, 0, tiled=True)  10.3 us
    all_gather x2, blocking collectives, spread_halves(): both = lax.all_gather(a2a(copied, BESIDE), 'core', tiled=True)  9.44 us
    pallas_call x15, Pallas kernels, call(): pl.pallas_call(body, out_shape=shape, in_specs=[SM] * scalars + [VM] * (l...  6.59 us
    all_gather x1, blocking collectives, per_device(): got = lax.all_gather(got, 'core')  5.25 us
  transfers between devices with their start and end apart: 1, of which 1 were waited for; matrix products, arithmetic and copies ran while one was open for 0% of the time, Pallas kernels for 1%

profile of v10, /device:TPU:1, one launch (start us, length us, event | category | flops | bytes accessed | tf_op | source)
XLA Modules:
  0.0 231.8 jit_solution(13151773298794454907)
XLA Ops:
  0.0 2.3 shard_map.66
  2.3 10.3 %all-to-all-start = ((f32[16,32,512]{2,1,0:T(8,128)}), f32[16,32,512]{2,1,0:T(8,128)S(1)}, u32[]{:S(2)}, u32[]{:S(2)}) async-start(f32[16,32,512]{2,1,0:T(8,128)} %shard_map.66), calls=%async_computation | async-start | bytes 2097152 | tf_op jit(solution)/shard_map/all_to_all | solution.py:255
  12.6 2.2 shard_map.65.below
  14.8 0.6 copy-done.5
  16.2 1.0 shard_map.64.table
  17.2 0.6 fusion.y0
  17.8 22.7 %all-to-all-done.slices = f32[16,32,512]{2,1,0:T(8,128)S(1)} async-done(((f32[16,32,512]{2,1,0:T(8,128)}), f32[16,32,512]{2,1,0:T(8,128)S(1)}, u32[]{:S(2)}, u32[]{:S(2)}) %all-to-all-start) | async-done | bytes 1048608 | tf_op jit(solution)/shard_map/all_to_all | solution.py:255
  41.0 19.0 %all_to_all.70.got = f32[16,32,128]{2,1,0:T(8,128)S(1)} all-to-all(f32[16,32,128]{2,1,0:T(8,128)S(1)} %get-tuple-element.27), channel_id=1, replica_groups=mesh['xh'=2,'xl'=2,'z'=8,'y'=8,'core'=2] {'xl','z'}, dimensions={0} | all-to-all | bytes 524288 | tf_op jit(solution)/shard_map/all_to_all | solution.py:217
  60.1 13.5 %all_to_all.71 = f32[16,32,128]{2,1,0:T(8,128)S(1)} all-to-all(f32[16,32,128]{2,1,0:T(8,128)S(1)} %shard_map.68), channel_id=1, replica_groups=mesh['xh'=2,'xl'=2,'z'=8,'y'=8,'core'=2] {'xh','y'}, dimensions={0} | all-to-all | bytes 524288 | tf_op jit(solution)/shard_map/all_to_all | solution.py:217
  73.6 5.1 %all_gather.21 = f32[16,32,128]{2,1,0:T(8,128)S(1)} all-gather(f32[8,32,128]{2,1,0:T(8,128)S(1)} %slice.8), channel_id=1, replica_groups=mesh['xh'=2,'xl'=2,'z'=8,'y'=8,'core'=2] {'core'}, dimensions={0}, use_global_device_ids=true | all-gather | bytes 393216 | tf_op jit(solution)/shard_map/all_gather | solution.py:265
  78.7 0.7 shard_map.69
  79.3 11.6 %all_to_all.72.got = f32[16,16,128]{2,1,0:T(8,128)S(1)} all-to-all(f32[16,16,128]{2,1,0:T(8,128)S(1)} %get-tuple-element.31), channel_id=1, replica_groups=mesh['xh'=2,'xl'=2,'z'=8,'y'=8,'core'=2] {'xl','z'}, dimensions={0} | all-to-all | bytes 262144 | tf_op jit(solution)/shard_map/all_to_all | solution.py:217
  90.9 11.7 %all_to_all.73 = f32[16,16,128]{2,1,0:T(8,128)S(1)} all-to-all(f32[16,16,128]{2,1,0:T(8,128)S(1)} %shard_map.70), channel_id=1, replica_groups=mesh['xh'=2,'xl'=2,'z'=8,'y'=8,'core'=2] {'xl','y'}, dimensions={0} | all-to-all | bytes 262144 | tf_op jit(solution)/shard_map/all_to_all | solution.py:217
  102.6 5.1 %all_gather.22 = f32[32,16,128]{2,1,0:T(8,128)S(1)} all-gather(f32[16,16,128]{2,1,0:T(8,128)S(1)} %all_to_all.73), channel_id=1, replica_groups=mesh['xh'=2,'xl'=2,'z'=8,'y'=8,'core'=2] {'core'}, dimensions={0}, use_global_device_ids=true | all-gather | bytes 393216 | tf_op jit(solution)/shard_map/all_gather | solution.py:271
  107.8 0.7 shard_map.71
  108.5 10.4 %all_to_all.74.got = f32[8,32,128]{2,1,0:T(8,128)S(1)} all-to-all(f32[8,32,128]{2,1,0:T(8,128)S(1)} %get-tuple-element.33), channel_id=1, replica_groups=mesh['xh'=2,'xl'=2,'z'=8,'y'=8,'core'=2] {'z'}, dimensions={0} | all-to-all | bytes 262144 | tf_op jit(solution)/shard_map/all_to_all | solution.py:217
  118.9 10.8 %all_to_all.75 = f32[8,32,128]{2,1,0:T(8,128)S(1)} all-to-all(f32[8,32,128]{2,1,0:T(8,128)S(1)} %shard_map.72), channel_id=1, replica_groups=mesh['xh'=2,'xl'=2,'z'=8,'y'=8,'core'=2] {'y'}, dimensions={0} | all-to-all | bytes 262144 | tf_op jit(solution)/shard_map/all_to_all | solution.py:217
  129.6 4.9 %all_gather.23 = f32[16,32,128]{2,1,0:T(8,128)S(1)} all-gather(f32[8,32,128]{2,1,0:T(8,128)S(1)} %all_to_all.75), channel_id=1, replica_groups=mesh['xh'=2,'xl'=2,'z'=8,'y'=8,'core'=2] {'core'}, dimensions={0}, use_global_device_ids=true | all-gather | bytes 393216 | tf_op jit(solution)/shard_map/all_gather | solution.py:265
  134.6 1.0 shard_map.73
  135.6 10.8 %all_to_all.76.got = f32[8,32,128]{2,1,0:T(8,128)S(1)} all-to-all(f32[8,32,128]{2,1,0:T(8,128)S(1)} %get-tuple-element.36), channel_id=1, replica_groups=mesh['xh'=2,'xl'=2,'z'=8,'y'=8,'core'=2] {'z'}, dimensions={0} | all-to-all | bytes 262144 | tf_op jit(solution)/shard_map/all_to_all | solution.py:217
  146.4 10.3 %all_to_all.77 = f32[8,32,128]{2,1,0:T(8,128)S(1)} all-to-all(f32[8,32,128]{2,1,0:T(8,128)S(1)} %shard_map.74), channel_id=1, replica_groups=mesh['xh'=2,'xl'=2,'z'=8,'y'=8,'core'=2] {'y'}, dimensions={0} | all-to-all | bytes 262144 | tf_op jit(solution)/shard_map/all_to_all | solution.py:217
  156.7 4.3 %all_gather.24 = f32[16,32,128]{2,1,0:T(8,128)S(1)} all-gather(f32[8,32,128]{2,1,0:T(8,128)S(1)} %all_to_all.77), channel_id=1, replica_groups=mesh['xh'=2,'xl'=2,'z'=8,'y'=8,'core'=2] {'core'}, dimensions={0}, use_global_device_ids=true | all-gather | bytes 393216 | tf_op jit(solution)/shard_map/all_gather | solution.py:265
  161.1 0.7 shard_map.75
  161.8 10.1 %all_to_all.78.got = f32[16,16,128]{2,1,0:T(8,128)S(1)} all-to-all(f32[16,16,128]{2,1,0:T(8,128)S(1)} %get-tuple-element.38), channel_id=1, replica_groups=mesh['xh'=2,'xl'=2,'z'=8,'y'=8,'core'=2] {'xl','z'}, dimensions={0} | all-to-all | bytes 262144 | tf_op jit(solution)/shard_map/all_to_all | solution.py:217
  171.9 10.1 %all_to_all.79 = f32[16,16,128]{2,1,0:T(8,128)S(1)} all-to-all(f32[16,16,128]{2,1,0:T(8,128)S(1)} %shard_map.76), channel_id=1, replica_groups=mesh['xh'=2,'xl'=2,'z'=8,'y'=8,'core'=2] {'xl','y'}, dimensions={0} | all-to-all | bytes 262144 | tf_op jit(solution)/shard_map/all_to_all | solution.py:217
  182.0 4.3 %all_gather.25 = f32[32,16,128]{2,1,0:T(8,128)S(1)} all-gather(f32[16,16,128]{2,1,0:T(8,128)S(1)} %all_to_all.79), channel_id=1, replica_groups=mesh['xh'=2,'xl'=2,'z'=8,'y'=8,'core'=2] {'core'}, dimensions={0}, use_global_device_ids=true | all-gather | bytes 393216 | tf_op jit(solution)/shard_map/all_gather | solution.py:271
  186.3 0.8 shard_map.77
  187.1 12.5 %all_to_all.80.got = f32[16,32,128]{2,1,0:T(8,128)S(1)} all-to-all(f32[16,32,128]{2,1,0:T(8,128)S(1)} %get-tuple-element.41), channel_id=1, replica_groups=mesh['xh'=2,'xl'=2,'z'=8,'y'=8,'core'=2] {'xl','z'}, dimensions={0} | all-to-all | bytes 524288 | tf_op jit(solution)/shard_map/all_to_all | solution.py:217
  199.7 12.5 %all_to_all.81 = f32[16,32,128]{2,1,0:T(8,128)S(1)} all-to-all(f32[16,32,128]{2,1,0:T(8,128)S(1)} %shard_map.78), channel_id=1, replica_groups=mesh['xh'=2,'xl'=2,'z'=8,'y'=8,'core'=2] {'xh','y'}, dimensions={0} | all-to-all | bytes 524288 | tf_op jit(solution)/shard_map/all_to_all | solution.py:217
  212.2 5.3 %all-gather = f32[16,32,128]{2,1,0:T(8,128)S(1)} all-gather(f32[8,32,128]{2,1,0:T(8,128)S(1)} %slice.9), channel_id=2, replica_groups=mesh['xh'=2,'xl'=2,'z'=8,'y'=8,'core'=2] {'core'}, dimensions={0}, use_global_device_ids=true | all-gather | bytes 393216 | tf_op jit(solution)/shard_map/all_gather | solution.py:292
  217.4 13.2 %all_to_all.82 = f32[16,32,128]{2,1,0:T(8,128)S(1)} all-to-all(f32[16,32,128]{2,1,0:T(8,128)S(1)} %shard_map.79), channel_id=1, replica_groups=mesh['xh'=2,'xl'=2,'z'=8,'y'=8,'core'=2] {'xl','z'}, dimensions={0} | all-to-all | bytes 524288 | tf_op jit(solution)/shard_map/all_to_all | solution.py:217
  230.6 1.2 shard_map.80
  (23 shorter events, 1.4 us)
Async XLA Ops:
  2.3 38.3 %all-to-all-start = ((f32[16,32,512]{2,1,0:T(8,128)}), f32[16,32,512]{2,1,0:T(8,128)S(1)}, u32[]{:S(2)}, u32[]{:S(2)}) async-start(f32[16,32,512]{2,1,0:T(8,128)} %shard_map.66), calls=%async_computation | async-start | bytes 2097152 | tf_op jit(solution)/shard_map/all_to_all | solution.py:255
  12.6 4.6 %copy-start.1 = (bf16[1,1,512,512]{3,2,1,0:T(8,128)(2,1)S(1)}, bf16[1,1,512,512]{3,2,1,0:T(8,128)(2,1)}, u32[]{:S(2)}) copy-start(bf16[1,1,512,512]{3,2,1,0:T(8,128)(2,1)} %param.8) | copy-start | bytes 1572868
  12.6 4.6 %copy-start.3 = (f32[1,1,512,128]{3,2,1,0:T(8,128)S(1)}, f32[1,1,512,128]{3,2,1,0:T(8,128)}, u32[]{:S(2)}) copy-start(f32[1,1,512,128]{3,2,1,0:T(8,128)} %param.7) | copy-start | bytes 786436
  14.8 0.7 copy-start.5
  15.4 0.7 copy-start.4
  118.8 15.7 %copy-start = (bf16[1,1,512,512]{3,2,1,0:T(8,128)(2,1)S(1)}, bf16[1,1,512,512]{3,2,1,0:T(8,128)(2,1)}, u32[]{:S(2)}) copy-start(bf16[1,1,512,512]{3,2,1,0:T(8,128)(2,1)} %param.9) | copy-start | bytes 1572868
  171.9 14.5 %copy-start.2 = (bf16[512,512]{1,0:T(8,128)(2,1)S(1)}, bf16[512,512]{1,0:T(8,128)(2,1)}, u32[]{:S(2)}) copy-start(bf16[512,512]{1,0:T(8,128)(2,1)} %shard_map.65.below) | copy-start | bytes 1572868

commit v11 on v10

--- a/solution.py
+++ b/solution.py
@@ -97,19 +97,30 @@
 
 
 def turn_kernel(blocks, out, block, turned, arrived, gone):
-    copy = pltpu.make_async_copy(blocks.at[0, 0, 0, 1], block, arrived)
-    copy.start()
-    copy.wait()
-    whole = block[...].astype(F32).T
     ncol, piece = turned.shape[0], turned.shape[1]
     ny = ncol // 2
-    for y in range(ny):
-        for core in range(2):
-            start = (core * ny + y) * piece
-            turned[2 * y + core] = whole[start:start + piece]
-    copy = pltpu.make_async_copy(turned, out, gone)
-    copy.start()
-    copy.wait()
+    part = 128
+    inward = []
+    for k in range(block.shape[1] // part):
+        lanes = pl.ds(k * part, part)
+        copy = pltpu.make_async_copy(
+            blocks.at[0, 0, 0, 1, :, lanes], block.at[:, lanes], arrived.at[k]
+        )
+        copy.start()
+        inward.append(copy)
+    outward = []
+    for k, copy in enumerate(inward):
+        copy.wait()
+        rows = block[:, k * part:(k + 1) * part].astype(F32).T
+        for j in range(part // piece):
+            core, y = divmod(k * (part // piece) + j, ny)
+            to = 2 * y + core
+            turned[to] = rows[j * piece:(j + 1) * piece]
+            copy = pltpu.make_async_copy(turned.at[to], out.at[to], gone.at[to])
+            copy.start()
+            outward.append(copy)
+    for copy in outward:
+        copy.wait()
 
 
 def turn_whole_kernel(blocks, out, block, arrived):
@@ -239,7 +250,11 @@
 
     sent = slot_call(
         turn_kernel, shape_of(ncol, piece, width), factor, pltpu.HBM,
-        [pltpu.VMEM((ncol, piece, width), F32), pltpu.SemaphoreType.DMA, pltpu.SemaphoreType.DMA],
+        [
+            pltpu.VMEM((ncol, piece, width), F32),
+            pltpu.SemaphoreType.DMA((width // 128,)),
+            pltpu.SemaphoreType.DMA((ncol,)),
+        ],
     )
     below = slot_call(
         turn_whole_kernel, shape_of(width, width, kind=BF16), factor, pltpu.VMEM,

time: 234 us -> 234 us (level)
  no operation moved by 1% of the time
where the time goes in v11:
time: 234 us; the launch traced here: 232 us
  blocking collectives  186 us (79%)
  waiting for transfers between devices  22.7 us (10%)
  Pallas kernels  10.9 us (5%)
  starting transfers between devices  10.3 us (4%)
    all_to_all x13, blocking collectives, a2a(): lax.all_to_all(array, axes, 0, 0, tiled=True)  156 us
    all_to_all x1, waiting for transfers between devices, per_device(): slices = lax.all_to_all(sent, COL, 0, 0, tiled=True)  22.7 us
    all_gather x3, blocking collectives, whole(): return lax.all_gather(half, 'core', tiled=True).reshape(width, nrhs)  14.4 us
    all_to_all x1, starting transfers between devices, per_device(): slices = lax.all_to_all(sent, COL, 0, 0, tiled=True)  10.3 us
    all_gather x2, blocking collectives, spread_halves(): both = lax.all_gather(a2a(copied, BESIDE), 'core', tiled=True)  9.44 us
    pallas_call x15, Pallas kernels, call(): pl.pallas_call(body, out_shape=shape, in_specs=[SM] * scalars + [VM] * (l...  6.59 us
    all_gather x1, blocking collectives, per_device(): got = lax.all_gather(got, 'core')  5.25 us
  transfers between devices with their start and end apart: 1, of which 1 were waited for; matrix products, arithmetic and copies ran while one was open for 0% of the time, Pallas kernels for 1%

profile of v11, /device:TPU:1, one launch (start us, length us, event | category | flops | bytes accessed | tf_op | source)
XLA Modules:
  0.0 231.7 jit_solution(8003671435600765759)
XLA Ops:
  0.0 2.2 shard_map.66
  2.2 10.3 %all-to-all-start = ((f32[16,32,512]{2,1,0:T(8,128)}), f32[16,32,512]{2,1,0:T(8,128)S(1)}, u32[]{:S(2)}, u32[]{:S(2)}) async-start(f32[16,32,512]{2,1,0:T(8,128)} %shard_map.66), calls=%async_computation | async-start | bytes 2097152 | tf_op jit(solution)/shard_map/all_to_all | solution.py:270
  12.5 2.2 shard_map.65.below
  14.7 0.6 copy-done.5
  16.1 1.0 shard_map.64.table
  17.2 0.6 fusion.y0
  17.8 22.7 %all-to-all-done.slices = f32[16,32,512]{2,1,0:T(8,128)S(1)} async-done(((f32[16,32,512]{2,1,0:T(8,128)}), f32[16,32,512]{2,1,0:T(8,128)S(1)}, u32[]{:S(2)}, u32[]{:S(2)}) %all-to-all-start) | async-done | bytes 1048608 | tf_op jit(solution)/shard_map/all_to_all | solution.py:270
  41.0 19.0 %all_to_all.70.got = f32[16,32,128]{2,1,0:T(8,128)S(1)} all-to-all(f32[16,32,128]{2,1,0:T(8,128)S(1)} %get-tuple-element.27), channel_id=1, replica_groups=mesh['xh'=2,'xl'=2,'z'=8,'y'=8,'core'=2] {'xl','z'}, dimensions={0} | all-to-all | bytes 524288 | tf_op jit(solution)/shard_map/all_to_all | solution.py:228
  60.0 13.5 %all_to_all.71 = f32[16,32,128]{2,1,0:T(8,128)S(1)} all-to-all(f32[16,32,128]{2,1,0:T(8,128)S(1)} %shard_map.68), channel_id=1, replica_groups=mesh['xh'=2,'xl'=2,'z'=8,'y'=8,'core'=2] {'xh','y'}, dimensions={0} | all-to-all | bytes 524288 | tf_op jit(solution)/shard_map/all_to_all | solution.py:228
  73.5 5.1 %all_gather.21 = f32[16,32,128]{2,1,0:T(8,128)S(1)} all-gather(f32[8,32,128]{2,1,0:T(8,128)S(1)} %slice.8), channel_id=1, replica_groups=mesh['xh'=2,'xl'=2,'z'=8,'y'=8,'core'=2] {'core'}, dimensions={0}, use_global_device_ids=true | all-gather | bytes 393216 | tf_op jit(solution)/shard_map/all_gather | solution.py:280
  78.6 0.7 shard_map.69
  79.2 11.6 %all_to_all.72.got = f32[16,16,128]{2,1,0:T(8,128)S(1)} all-to-all(f32[16,16,128]{2,1,0:T(8,128)S(1)} %get-tuple-element.31), channel_id=1, replica_groups=mesh['xh'=2,'xl'=2,'z'=8,'y'=8,'core'=2] {'xl','z'}, dimensions={0} | all-to-all | bytes 262144 | tf_op jit(solution)/shard_map/all_to_all | solution.py:228
  90.9 11.7 %all_to_all.73 = f32[16,16,128]{2,1,0:T(8,128)S(1)} all-to-all(f32[16,16,128]{2,1,0:T(8,128)S(1)} %shard_map.70), channel_id=1, replica_groups=mesh['xh'=2,'xl'=2,'z'=8,'y'=8,'core'=2] {'xl','y'}, dimensions={0} | all-to-all | bytes 262144 | tf_op jit(solution)/shard_map/all_to_all | solution.py:228
  102.6 5.1 %all_gather.22 = f32[32,16,128]{2,1,0:T(8,128)S(1)} all-gather(f32[16,16,128]{2,1,0:T(8,128)S(1)} %all_to_all.73), channel_id=1, replica_groups=mesh['xh'=2,'xl'=2,'z'=8,'y'=8,'core'=2] {'core'}, dimensions={0}, use_global_device_ids=true | all-gather | bytes 393216 | tf_op jit(solution)/shard_map/all_gather | solution.py:286
  107.7 0.7 shard_map.71
  108.4 10.4 %all_to_all.74.got = f32[8,32,128]{2,1,0:T(8,128)S(1)} all-to-all(f32[8,32,128]{2,1,0:T(8,128)S(1)} %get-tuple-element.33), channel_id=1, replica_groups=mesh['xh'=2,'xl'=2,'z'=8,'y'=8,'core'=2] {'z'}, dimensions={0} | all-to-all | bytes 262144 | tf_op jit(solution)/shard_map/all_to_all | solution.py:228
  118.8 10.8 %all_to_all.75 = f32[8,32,128]{2,1,0:T(8,128)S(1)} all-to-all(f32[8,32,128]{2,1,0:T(8,128)S(1)} %shard_map.72), channel_id=1, replica_groups=mesh['xh'=2,'xl'=2,'z'=8,'y'=8,'core'=2] {'y'}, dimensions={0} | all-to-all | bytes 262144 | tf_op jit(solution)/shard_map/all_to_all | solution.py:228
  129.6 4.9 %all_gather.23 = f32[16,32,128]{2,1,0:T(8,128)S(1)} all-gather(f32[8,32,128]{2,1,0:T(8,128)S(1)} %all_to_all.75), channel_id=1, replica_groups=mesh['xh'=2,'xl'=2,'z'=8,'y'=8,'core'=2] {'core'}, dimensions={0}, use_global_device_ids=true | all-gather | bytes 393216 | tf_op jit(solution)/shard_map/all_gather | solution.py:280
  134.5 1.0 shard_map.73
  135.5 10.8 %all_to_all.76.got = f32[8,32,128]{2,1,0:T(8,128)S(1)} all-to-all(f32[8,32,128]{2,1,0:T(8,128)S(1)} %get-tuple-element.36), channel_id=1, replica_groups=mesh['xh'=2,'xl'=2,'z'=8,'y'=8,'core'=2] {'z'}, dimensions={0} | all-to-all | bytes 262144 | tf_op jit(solution)/shard_map/all_to_all | solution.py:228
  146.4 10.3 %all_to_all.77 = f32[8,32,128]{2,1,0:T(8,128)S(1)} all-to-all(f32[8,32,128]{2,1,0:T(8,128)S(1)} %shard_map.74), channel_id=1, replica_groups=mesh['xh'=2,'xl'=2,'z'=8,'y'=8,'core'=2] {'y'}, dimensions={0} | all-to-all | bytes 262144 | tf_op jit(solution)/shard_map/all_to_all | solution.py:228
  156.7 4.3 %all_gather.24 = f32[16,32,128]{2,1,0:T(8,128)S(1)} all-gather(f32[8,32,128]{2,1,0:T(8,128)S(1)} %all_to_all.77), channel_id=1, replica_groups=mesh['xh'=2,'xl'=2,'z'=8,'y'=8,'core'=2] {'core'}, dimensions={0}, use_global_device_ids=true | all-gather | bytes 393216 | tf_op jit(solution)/shard_map/all_gather | solution.py:280
  161.0 0.7 shard_map.75
  161.7 10.1 %all_to_all.78.got = f32[16,16,128]{2,1,0:T(8,128)S(1)} all-to-all(f32[16,16,128]{2,1,0:T(8,128)S(1)} %get-tuple-element.38), channel_id=1, replica_groups=mesh['xh'=2,'xl'=2,'z'=8,'y'=8,'core'=2] {'xl','z'}, dimensions={0} | all-to-all | bytes 262144 | tf_op jit(solution)/shard_map/all_to_all | solution.py:228
  171.8 10.1 %all_to_all.79 = f32[16,16,128]{2,1,0:T(8,128)S(1)} all-to-all(f32[16,16,128]{2,1,0:T(8,128)S(1)} %shard_map.76), channel_id=1, replica_groups=mesh['xh'=2,'xl'=2,'z'=8,'y'=8,'core'=2] {'xl','y'}, dimensions={0} | all-to-all | bytes 262144 | tf_op jit(solution)/shard_map/all_to_all | solution.py:228
  182.0 4.3 %all_gather.25 = f32[32,16,128]{2,1,0:T(8,128)S(1)} all-gather(f32[16,16,128]{2,1,0:T(8,128)S(1)} %all_to_all.79), channel_id=1, replica_groups=mesh['xh'=2,'xl'=2,'z'=8,'y'=8,'core'=2] {'core'}, dimensions={0}, use_global_device_ids=true | all-gather | bytes 393216 | tf_op jit(solution)/shard_map/all_gather | solution.py:286
  186.3 0.8 shard_map.77
  187.1 12.5 %all_to_all.80.got = f32[16,32,128]{2,1,0:T(8,128)S(1)} all-to-all(f32[16,32,128]{2,1,0:T(8,128)S(1)} %get-tuple-element.41), channel_id=1, replica_groups=mesh['xh'=2,'xl'=2,'z'=8,'y'=8,'core'=2] {'xl','z'}, dimensions={0} | all-to-all | bytes 524288 | tf_op jit(solution)/shard_map/all_to_all | solution.py:228
  199.6 12.5 %all_to_all.81 = f32[16,32,128]{2,1,0:T(8,128)S(1)} all-to-all(f32[16,32,128]{2,1,0:T(8,128)S(1)} %shard_map.78), channel_id=1, replica_groups=mesh['xh'=2,'xl'=2,'z'=8,'y'=8,'core'=2] {'xh','y'}, dimensions={0} | all-to-all | bytes 524288 | tf_op jit(solution)/shard_map/all_to_all | solution.py:228
  212.1 5.3 %all-gather = f32[16,32,128]{2,1,0:T(8,128)S(1)} all-gather(f32[8,32,128]{2,1,0:T(8,128)S(1)} %slice.9), channel_id=2, replica_groups=mesh['xh'=2,'xl'=2,'z'=8,'y'=8,'core'=2] {'core'}, dimensions={0}, use_global_device_ids=true | all-gather | bytes 393216 | tf_op jit(solution)/shard_map/all_gather | solution.py:307
  217.4 13.2 %all_to_all.82 = f32[16,32,128]{2,1,0:T(8,128)S(1)} all-to-all(f32[16,32,128]{2,1,0:T(8,128)S(1)} %shard_map.79), channel_id=1, replica_groups=mesh['xh'=2,'xl'=2,'z'=8,'y'=8,'core'=2] {'xl','z'}, dimensions={0} | all-to-all | bytes 524288 | tf_op jit(solution)/shard_map/all_to_all | solution.py:228
  230.5 1.2 shard_map.80
  (23 shorter events, 1.4 us)
Async XLA Ops:
  2.2 38.3 %all-to-all-start = ((f32[16,32,512]{2,1,0:T(8,128)}), f32[16,32,512]{2,1,0:T(8,128)S(1)}, u32[]{:S(2)}, u32[]{:S(2)}) async-start(f32[16,32,512]{2,1,0:T(8,128)} %shard_map.66), calls=%async_computation | async-start | bytes 2097152 | tf_op jit(solution)/shard_map/all_to_all | solution.py:270
  12.5 4.6 %copy-start.1 = (bf16[1,1,512,512]{3,2,1,0:T(8,128)(2,1)S(1)}, bf16[1,1,512,512]{3,2,1,0:T(8,128)(2,1)}, u32[]{:S(2)}) copy-start(bf16[1,1,512,512]{3,2,1,0:T(8,128)(2,1)} %param.8) | copy-start | bytes 1572868
  12.5 4.6 %copy-start.3 = (f32[1,1,512,128]{3,2,1,0:T(8,128)S(1)}, f32[1,1,512,128]{3,2,1,0:T(8,128)}, u32[]{:S(2)}) copy-start(f32[1,1,512,128]{3,2,1,0:T(8,128)} %param.7) | copy-start | bytes 786436
  14.7 0.7 copy-start.5
  15.4 0.7 copy-start.4
  118.8 15.7 %copy-start = (bf16[1,1,512,512]{3,2,1,0:T(8,128)(2,1)S(1)}, bf16[1,1,512,512]{3,2,1,0:T(8,128)(2,1)}, u32[]{:S(2)}) copy-start(bf16[1,1,512,512]{3,2,1,0:T(8,128)(2,1)} %param.9) | copy-start | bytes 1572868
  171.8 14.5 %copy-start.2 = (bf16[512,512]{1,0:T(8,128)(2,1)S(1)}, bf16[512,512]{1,0:T(8,128)(2,1)}, u32[]{:S(2)}) copy-start(bf16[512,512]{1,0:T(8,128)(2,1)} %shard_map.65.below) | copy-start | bytes 1572868

commit v12 on v10

--- a/solution.py
+++ b/solution.py
@@ -96,20 +96,19 @@
         out[index] = jnp.broadcast_to(values, (count, out.shape[2]))
 
 
-def turn_kernel(blocks, out, block, turned, arrived, gone):
-    copy = pltpu.make_async_copy(blocks.at[0, 0, 0, 1], block, arrived)
-    copy.start()
-    copy.wait()
-    whole = block[...].astype(F32).T
-    ncol, piece = turned.shape[0], turned.shape[1]
-    ny = ncol // 2
+def turn_kernel(at, block, keep, send):
+    rows = keep.shape[0]
+    turned = block[0, 0, 0, 0].astype(F32).T
+    mine = at[0] == 0
+    keep[...] = jnp.where(mine, turned[:rows], turned[rows:])
+    send[...] = jnp.where(mine, turned[rows:], turned[:rows])
+
+
+def parcel_kernel(own, other, out):
+    ny, piece = out.shape[0], out.shape[1] // 2
     for y in range(ny):
-        for core in range(2):
-            start = (core * ny + y) * piece
-            turned[2 * y + core] = whole[start:start + piece]
-    copy = pltpu.make_async_copy(turned, out, gone)
-    copy.start()
-    copy.wait()
+        out[y, :piece] = own[y * piece:(y + 1) * piece]
+        out[y, piece:] = other[y * piece:(y + 1) * piece]
 
 
 def turn_whole_kernel(blocks, out, block, arrived):
@@ -131,11 +130,14 @@
     )(factor)
 
 
-def leaf_kernel(slices, y0, out, own_out):
-    top, piece, width = slices.shape
-    own = slices[...].reshape(top * piece, width).astype(BF16)
-    own_out[...] = own
-    out[...] = product(own, y0[...]).reshape(out.shape)
+def leaf_kernel(at, slices, y0, out, own_out):
+    ny, piece = slices.shape[0], slices.shape[1] // 2
+    for y in range(ny):
+        first = pl.multiple_of((2 * y + at[0]) * piece, piece)
+        second = pl.multiple_of((2 * y + 1 - at[0]) * piece, piece)
+        own_out[pl.ds(first, piece), :] = slices[y, :piece].astype(BF16)
+        own_out[pl.ds(second, piece), :] = slices[y, piece:].astype(BF16)
+    out[...] = product(own_out[...], y0[...]).reshape(out.shape)
 
 
 def sum_kernel(line, first, start, stop, table, got, out):
@@ -237,10 +239,23 @@
     to_top = shape_of(top, piece, nrhs)
     to_late = shape_of(nz, piece, nrhs)
 
-    sent = slot_call(
-        turn_kernel, shape_of(ncol, piece, width), factor, pltpu.HBM,
-        [pltpu.VMEM((ncol, piece, width), F32), pltpu.SemaphoreType.DMA, pltpu.SemaphoreType.DMA],
-    )
+    core = lax.axis_index("core")[None].astype(jnp.int32)
+    half_block = shape_of(width // 2, width)
+    keep, send = pl.pallas_call(
+        turn_kernel,
+        out_shape=(half_block, half_block),
+        grid=(1,),
+        in_specs=[
+            SM,
+            pl.BlockSpec((1, 1, 1, 1, width, width), lambda k: (0, 0, 0, 1, 0, 0)),
+        ],
+        out_specs=(
+            pl.BlockSpec((width // 2, width), lambda k: (0, 0)),
+            pl.BlockSpec((width // 2, width), lambda k: (0, 0)),
+        ),
+        compiler_params=ROOMY,
+    )(core, factor)
+    other = lax.ppermute(send, "core", [(0, 1), (1, 0)])
     below = slot_call(
         turn_whole_kernel, shape_of(width, width, kind=BF16), factor, pltpu.VMEM,
         [pltpu.SemaphoreType.DMA],
@@ -252,10 +267,11 @@
     )
     y0 = jnp.dot(up.astype(F32), base, precision=lax.Precision.HIGHEST)
 
-    slices = lax.all_to_all(sent, COL, 0, 0, tiled=True)
-    table, y0, base, up, low, below, slices = lax.optimization_barrier(
-        (table, y0, base, up, low, below, slices)
-    )
+    parcels = call(parcel_kernel, shape_of(ny, 2 * piece, width), keep, other)
+    table, y0, base, up, low, below, parcels = lax.optimization_barrier(
+        (table, y0, base, up, low, below, parcels)
+    )
+    slices = a2a(parcels, "y")
 
     def total(line, first, got, shape, start=0, stop=ncol):
         body = functools.partial(sum_kernel, line, first, start, stop)
@@ -271,7 +287,7 @@
         both = lax.all_gather(a2a(copied, BESIDE), "core", tiled=True)
         return both.reshape(ncol // ny, 2, ny, piece // 2, nrhs)
 
-    out, own = call(leaf_kernel, (to_top, shape_of(width, width, kind=BF16)), slices, y0)
+    out, own = call(leaf_kernel, (to_top, shape_of(width, width, kind=BF16)), core, slices, y0, scalars=1)
     got = total(FROM_LEAF, 0, a2a(out, HALF), across, start=ny)
     update = whole(a2a(got, ACROSS)[:ny])
     rest, out = call(one_kernel, (panel, half_to_top), update, base, up, own)

time: 234 us -> 240 us (1.026)
  blocking collectives: 186 us -> 216 us
  waiting for transfers between devices: 22.7 us -> 0.01 us
    all_to_all x13 -> x14, blocking collectives: 156 us -> 187 us  [a2a(): lax.all_to_all(array, axes, 0, 0, tiled=True)]
    all_to_all x1 -> x0, waiting for transfers between devices: 22.7 us -> none  [per_device(): slices = lax.all_to_all(sent, COL, 0, 0, tiled=True)]
    all_to_all x1 -> x0, starting transfers between devices: 10.3 us -> none  [per_device(): slices = lax.all_to_all(sent, COL, 0, 0, tiled=True)]
    ppermute x0 -> x1, starting transfers between devices: none -> 8.79 us  [per_device(): other = lax.ppermute(send, 'core', [(0, 1), (1, 0)])]
    pallas_call x15 -> x16, Pallas kernels: 6.59 us -> 6.7 us  [call(): pl.pallas_call(body, out_shape=shape, in_specs=[SM] * scalars + [VM] * (l...]
  transfers between devices with their start and end apart: 1 -> 1, of which waited for: 1 -> 0; matrix products, arithmetic and copies ran while one was open for 0% -> 0% of each run, Pallas kernels for 1% -> 1%
where the time goes in v12:
time: 240 us; the launch traced here: 238 us
  blocking collectives  216 us (90%)
  Pallas kernels  9.02 us (4%)
  starting transfers between devices  8.79 us (4%)
  local copies, waits for them, and re-layouts  2.55 us (1%)
    all_to_all x14, blocking collectives, a2a(): lax.all_to_all(array, axes, 0, 0, tiled=True)  187 us
    all_gather x3, blocking collectives, whole(): return lax.all_gather(half, 'core', tiled=True).reshape(width, nrhs)  14.6 us
    all_gather x2, blocking collectives, spread_halves(): both = lax.all_gather(a2a(copied, BESIDE), 'core', tiled=True)  9.44 us
    ppermute x1, starting transfers between devices, per_device(): other = lax.ppermute(send, 'core', [(0, 1), (1, 0)])  8.79 us
    pallas_call x16, Pallas kernels, call(): pl.pallas_call(body, out_shape=shape, in_specs=[SM] * scalars + [VM] * (l...  6.7 us
    all_gather x1, blocking collectives, per_device(): got = lax.all_gather(got, 'core')  5.25 us
  transfers between devices with their start and end apart: 1, of which 0 were waited for; matrix products, arithmetic and copies ran while one was open for 0% of the time, Pallas kernels for 1%

profile of v12, /device:TPU:1, one launch (start us, length us, event | category | flops | bytes accessed | tf_op | source)
XLA Modules:
  0.0 237.7 jit_solution(7528577568079926886)
XLA Ops:
  0.0 1.2 copy-done.2
  1.4 8.8 %collective-permute-start = (f32[256,512]{1,0:T(8,128)S(1)}, f32[256,512]{1,0:T(8,128)S(1)}, u32[]{:S(2)}, u32[]{:S(2)}) collective-permute-start(f32[256,512]{1,0:T(8,128)S(1)} %get-tuple-element.27), channel_id=1, source_target_pairs={{0,1},{1,0},{2,3},{3,2},{4,5},{5,4},{6,7},{7,6},{8,9},{9,8},{10,11... | collective-permute-start | bytes 1572872 | tf_op jit(solution)/shard_map/ppermute | solution.py:258
  10.3 2.1 shard_map.65.below
  12.4 0.6 copy-done.6
  13.8 1.0 shard_map.64.table
  14.8 0.6 fusion.y0
  15.5 31.7 %all_to_all.70.slices = f32[8,64,512]{2,1,0:T(8,128)S(1)} all-to-all(f32[8,64,512]{2,1,0:T(8,128)S(1)} %shard_map.67), channel_id=1, replica_groups=mesh['xh'=2,'xl'=2,'z'=8,'y'=8,'core'=2] {'y'}, dimensions={0} | all-to-all | bytes 2097152 | tf_op jit(solution)/shard_map/all_to_all | solution.py:219
  47.7 18.5 %all_to_all.71.got = f32[16,32,128]{2,1,0:T(8,128)S(1)} all-to-all(f32[16,32,128]{2,1,0:T(8,128)S(1)} %get-tuple-element.31), channel_id=1, replica_groups=mesh['xh'=2,'xl'=2,'z'=8,'y'=8,'core'=2] {'xl','z'}, dimensions={0} | all-to-all | bytes 524288 | tf_op jit(solution)/shard_map/all_to_all | solution.py:219
  66.2 13.0 %all_to_all.72 = f32[16,32,128]{2,1,0:T(8,128)S(1)} all-to-all(f32[16,32,128]{2,1,0:T(8,128)S(1)} %shard_map.69), channel_id=1, replica_groups=mesh['xh'=2,'xl'=2,'z'=8,'y'=8,'core'=2] {'xh','y'}, dimensions={0} | all-to-all | bytes 524288 | tf_op jit(solution)/shard_map/all_to_all | solution.py:219
  79.2 5.3 %all_gather.21 = f32[16,32,128]{2,1,0:T(8,128)S(1)} all-gather(f32[8,32,128]{2,1,0:T(8,128)S(1)} %slice.8), channel_id=1, replica_groups=mesh['xh'=2,'xl'=2,'z'=8,'y'=8,'core'=2] {'core'}, dimensions={0}, use_global_device_ids=true | all-gather | bytes 393216 | tf_op jit(solution)/shard_map/all_gather | solution.py:281
  84.6 0.7 shard_map.70
  85.2 11.6 %all_to_all.73.got = f32[16,16,128]{2,1,0:T(8,128)S(1)} all-to-all(f32[16,16,128]{2,1,0:T(8,128)S(1)} %get-tuple-element.35), channel_id=1, replica_groups=mesh['xh'=2,'xl'=2,'z'=8,'y'=8,'core'=2] {'xl','z'}, dimensions={0} | all-to-all | bytes 262144 | tf_op jit(solution)/shard_map/all_to_all | solution.py:219
  96.9 11.7 %all_to_all.74 = f32[16,16,128]{2,1,0:T(8,128)S(1)} all-to-all(f32[16,16,128]{2,1,0:T(8,128)S(1)} %shard_map.71), channel_id=1, replica_groups=mesh['xh'=2,'xl'=2,'z'=8,'y'=8,'core'=2] {'xl','y'}, dimensions={0} | all-to-all | bytes 262144 | tf_op jit(solution)/shard_map/all_to_all | solution.py:219
  108.5 5.1 %all_gather.22 = f32[32,16,128]{2,1,0:T(8,128)S(1)} all-gather(f32[16,16,128]{2,1,0:T(8,128)S(1)} %all_to_all.74), channel_id=1, replica_groups=mesh['xh'=2,'xl'=2,'z'=8,'y'=8,'core'=2] {'core'}, dimensions={0}, use_global_device_ids=true | all-gather | bytes 393216 | tf_op jit(solution)/shard_map/all_gather | solution.py:287
  113.7 0.7 shard_map.72
  114.4 10.4 %all_to_all.75.got = f32[8,32,128]{2,1,0:T(8,128)S(1)} all-to-all(f32[8,32,128]{2,1,0:T(8,128)S(1)} %get-tuple-element.37), channel_id=1, replica_groups=mesh['xh'=2,'xl'=2,'z'=8,'y'=8,'core'=2] {'z'}, dimensions={0} | all-to-all | bytes 262144 | tf_op jit(solution)/shard_map/all_to_all | solution.py:219
  124.8 10.8 %all_to_all.76 = f32[8,32,128]{2,1,0:T(8,128)S(1)} all-to-all(f32[8,32,128]{2,1,0:T(8,128)S(1)} %shard_map.73), channel_id=1, replica_groups=mesh['xh'=2,'xl'=2,'z'=8,'y'=8,'core'=2] {'y'}, dimensions={0} | all-to-all | bytes 262144 | tf_op jit(solution)/shard_map/all_to_all | solution.py:219
  135.5 4.9 %all_gather.23 = f32[16,32,128]{2,1,0:T(8,128)S(1)} all-gather(f32[8,32,128]{2,1,0:T(8,128)S(1)} %all_to_all.76), channel_id=1, replica_groups=mesh['xh'=2,'xl'=2,'z'=8,'y'=8,'core'=2] {'core'}, dimensions={0}, use_global_device_ids=true | all-gather | bytes 393216 | tf_op jit(solution)/shard_map/all_gather | solution.py:281
  140.5 1.0 shard_map.74
  141.5 10.8 %all_to_all.77.got = f32[8,32,128]{2,1,0:T(8,128)S(1)} all-to-all(f32[8,32,128]{2,1,0:T(8,128)S(1)} %get-tuple-element.40), channel_id=1, replica_groups=mesh['xh'=2,'xl'=2,'z'=8,'y'=8,'core'=2] {'z'}, dimensions={0} | all-to-all | bytes 262144 | tf_op jit(solution)/shard_map/all_to_all | solution.py:219
  152.3 10.3 %all_to_all.78 = f32[8,32,128]{2,1,0:T(8,128)S(1)} all-to-all(f32[8,32,128]{2,1,0:T(8,128)S(1)} %shard_map.75), channel_id=1, replica_groups=mesh['xh'=2,'xl'=2,'z'=8,'y'=8,'core'=2] {'y'}, dimensions={0} | all-to-all | bytes 262144 | tf_op jit(solution)/shard_map/all_to_all | solution.py:219
  162.7 4.3 %all_gather.24 = f32[16,32,128]{2,1,0:T(8,128)S(1)} all-gather(f32[8,32,128]{2,1,0:T(8,128)S(1)} %all_to_all.78), channel_id=1, replica_groups=mesh['xh'=2,'xl'=2,'z'=8,'y'=8,'core'=2] {'core'}, dimensions={0}, use_global_device_ids=true | all-gather | bytes 393216 | tf_op jit(solution)/shard_map/all_gather | solution.py:281
  167.0 0.7 shard_map.76
  167.7 10.1 %all_to_all.79.got = f32[16,16,128]{2,1,0:T(8,128)S(1)} all-to-all(f32[16,16,128]{2,1,0:T(8,128)S(1)} %get-tuple-element.42), channel_id=1, replica_groups=mesh['xh'=2,'xl'=2,'z'=8,'y'=8,'core'=2] {'xl','z'}, dimensions={0} | all-to-all | bytes 262144 | tf_op jit(solution)/shard_map/all_to_all | solution.py:219
  177.8 10.1 %all_to_all.80 = f32[16,16,128]{2,1,0:T(8,128)S(1)} all-to-all(f32[16,16,128]{2,1,0:T(8,128)S(1)} %shard_map.77), channel_id=1, replica_groups=mesh['xh'=2,'xl'=2,'z'=8,'y'=8,'core'=2] {'xl','y'}, dimensions={0} | all-to-all | bytes 262144 | tf_op jit(solution)/shard_map/all_to_all | solution.py:219
  187.9 4.3 %all_gather.25 = f32[32,16,128]{2,1,0:T(8,128)S(1)} all-gather(f32[16,16,128]{2,1,0:T(8,128)S(1)} %all_to_all.80), channel_id=1, replica_groups=mesh['xh'=2,'xl'=2,'z'=8,'y'=8,'core'=2] {'core'}, dimensions={0}, use_global_device_ids=true | all-gather | bytes 393216 | tf_op jit(solution)/shard_map/all_gather | solution.py:287
  192.2 0.8 shard_map.78
  193.0 12.5 %all_to_all.81.got = f32[16,32,128]{2,1,0:T(8,128)S(1)} all-to-all(f32[16,32,128]{2,1,0:T(8,128)S(1)} %get-tuple-element.45), channel_id=1, replica_groups=mesh['xh'=2,'xl'=2,'z'=8,'y'=8,'core'=2] {'xl','z'}, dimensions={0} | all-to-all | bytes 524288 | tf_op jit(solution)/shard_map/all_to_all | solution.py:219
  205.6 12.5 %all_to_all.82 = f32[16,32,128]{2,1,0:T(8,128)S(1)} all-to-all(f32[16,32,128]{2,1,0:T(8,128)S(1)} %shard_map.79), channel_id=1, replica_groups=mesh['xh'=2,'xl'=2,'z'=8,'y'=8,'core'=2] {'xh','y'}, dimensions={0} | all-to-all | bytes 524288 | tf_op jit(solution)/shard_map/all_to_all | solution.py:219
  218.1 5.3 %all-gather = f32[16,32,128]{2,1,0:T(8,128)S(1)} all-gather(f32[8,32,128]{2,1,0:T(8,128)S(1)} %slice.9), channel_id=2, replica_groups=mesh['xh'=2,'xl'=2,'z'=8,'y'=8,'core'=2] {'core'}, dimensions={0}, use_global_device_ids=true | all-gather | bytes 393216 | tf_op jit(solution)/shard_map/all_gather | solution.py:308
  223.3 13.2 %all_to_all.83 = f32[16,32,128]{2,1,0:T(8,128)S(1)} all-to-all(f32[16,32,128]{2,1,0:T(8,128)S(1)} %shard_map.80), channel_id=1, replica_groups=mesh['xh'=2,'xl'=2,'z'=8,'y'=8,'core'=2] {'xl','z'}, dimensions={0} | all-to-all | bytes 524288 | tf_op jit(solution)/shard_map/all_to_all | solution.py:219
  236.5 1.2 shard_map.81
  (27 shorter events, 1.7 us)
Async XLA Ops:
  0.0 1.2 copy-start.2
  1.4 14.0 %collective-permute-start = (f32[256,512]{1,0:T(8,128)S(1)}, f32[256,512]{1,0:T(8,128)S(1)}, u32[]{:S(2)}, u32[]{:S(2)}) collective-permute-start(f32[256,512]{1,0:T(8,128)S(1)} %get-tuple-element.27), channel_id=1, source_target_pairs={{0,1},{1,0},{2,3},{3,2},{4,5},{5,4},{6,7},{7,6},{8,9},{9,8},{10,11... | collective-permute-start | bytes 1572872 | tf_op jit(solution)/shard_map/ppermute | solution.py:258
  10.2 4.6 %copy-start.1 = (bf16[1,1,512,512]{3,2,1,0:T(8,128)(2,1)S(1)}, bf16[1,1,512,512]{3,2,1,0:T(8,128)(2,1)}, u32[]{:S(2)}) copy-start(bf16[1,1,512,512]{3,2,1,0:T(8,128)(2,1)} %param.8) | copy-start | bytes 1572868
  10.2 4.6 %copy-start.4 = (f32[1,1,512,128]{3,2,1,0:T(8,128)S(1)}, f32[1,1,512,128]{3,2,1,0:T(8,128)}, u32[]{:S(2)}) copy-start(f32[1,1,512,128]{3,2,1,0:T(8,128)} %param.7) | copy-start | bytes 786436
  12.4 0.7 copy-start.6
  13.0 0.7 copy-start.5
  124.7 15.7 %copy-start = (bf16[1,1,512,512]{3,2,1,0:T(8,128)(2,1)S(1)}, bf16[1,1,512,512]{3,2,1,0:T(8,128)(2,1)}, u32[]{:S(2)}) copy-start(bf16[1,1,512,512]{3,2,1,0:T(8,128)(2,1)} %param.9) | copy-start | bytes 1572868
  177.8 14.5 %copy-start.3 = (bf16[512,512]{1,0:T(8,128)(2,1)S(1)}, bf16[512,512]{1,0:T(8,128)(2,1)}, u32[]{:S(2)}) copy-start(bf16[512,512]{1,0:T(8,128)(2,1)} %shard_map.65.below) | copy-start | bytes 1572868

commit v13 on v11

--- a/solution.py
+++ b/solution.py
@@ -8,11 +8,12 @@
 from jax.sharding import Mesh, PartitionSpec as P
 
 LEVELS = 4
-HALF = ("xl", "z")
+HALF = ("z", "xl")
 ROW = ("xh", "xl", "z")
 COL = ("y", "core")
-ACROSS = ("xh", "y")
-BESIDE = ("xl", "y")
+SLICES = ("core", "y")
+ACROSS = ("y", "xh")
+BESIDE = ("y", "xl")
 F32 = jnp.float32
 BF16 = jnp.bfloat16
 ROOMY = pltpu.CompilerParams(vmem_limit_bytes=40 * 1024 * 1024)
@@ -97,8 +98,7 @@
 
 
 def turn_kernel(blocks, out, block, turned, arrived, gone):
-    ncol, piece = turned.shape[0], turned.shape[1]
-    ny = ncol // 2
+    piece = turned.shape[1]
     part = 128
     inward = []
     for k in range(block.shape[1] // part):
@@ -113,8 +113,7 @@
         copy.wait()
         rows = block[:, k * part:(k + 1) * part].astype(F32).T
         for j in range(part // piece):
-            core, y = divmod(k * (part // piece) + j, ny)
-            to = 2 * y + core
+            to = k * (part // piece) + j
             turned[to] = rows[j * piece:(j + 1) * piece]
             copy = pltpu.make_async_copy(turned.at[to], out.at[to], gone.at[to])
             copy.start()
@@ -142,51 +141,42 @@
     )(factor)
 
 
+def paired(k, count):
+    return 2 * (k % (count // 2)) + k // (count // 2)
+
+
 def leaf_kernel(slices, y0, out, own_out):
     top, piece, width = slices.shape
-    own = slices[...].reshape(top * piece, width).astype(BF16)
+    ny = top // 2
+    own = jnp.concatenate(
+        [slices[core * ny + y] for y in range(ny) for core in range(2)], 0
+    ).astype(BF16)
     own_out[...] = own
-    out[...] = product(own, y0[...]).reshape(out.shape)
-
-
-def sum_kernel(line, first, start, stop, table, got, out):
-    total = table[line, first:first + 1] * got[0]
-    for k in range(1, got.shape[0]):
-        total = total + table[line, first + k:first + k + 1] * got[k]
+    result = product(own, y0[...])
+    for k in range(top):
+        out[paired(k, top)] = result[k * piece:(k + 1) * piece]
+
+
+def sum_kernel(line, first, pairs, side, table, got, out):
+    count = got.shape[0]
+    total = jnp.zeros(got.shape[1:], F32)
+    for k in range(count):
+        at = paired(k, count) if pairs else k
+        total = total + table[line, first + k:first + k + 1] * got[at]
     for k in range(out.shape[0]):
-        out[k] = total if start <= k < stop else jnp.zeros_like(total)
-
-
-def halves(out, panel, piece):
-    slices = panel.reshape(panel.shape[0] // piece, piece, panel.shape[1])
-    count = slices.shape[0]
-    out[:count] = slices[:, :piece // 2]
-    out[count:] = slices[:, piece // 2:]
-
-
-def joined(update):
-    cores, parts, ny = update.shape[:3]
-    return jnp.concatenate(
-        [
-            update[core, part, y]
-            for core in range(cores)
-            for y in range(ny)
-            for part in range(parts)
-        ],
-        0,
-    )
+        out[k] = total if side is None or k % 2 == side else jnp.zeros_like(total)
 
 
 def one_kernel(update, base, up, own, rest_out, out):
     rows = own.shape[0] // 2
     rest = base[...] - update[...]
     rest_out[...] = rest
-    halves(out, product(own[rows:], product(up[...], rest)), 2 * out.shape[1])
+    out[...] = product(own[rows:], product(up[...], rest)).reshape(out.shape)
 
 
 def two_kernel(update, rest_in, up, own, rest_out, out):
     rows = own.shape[0] // 2
-    rest = rest_in[...] - joined(update)
+    rest = rest_in[...] - update[...]
     rest_out[...] = rest
     out[...] = product(own[rows:], product(up[...], rest)).reshape(out.shape)
 
@@ -202,11 +192,11 @@
     rows = own.shape[0] // 2
     rest = y[...] - update[...]
     rest_out[...] = rest
-    halves(out, product(own[:rows], product(low[...], rest)), 2 * out.shape[1])
+    out[...] = product(own[:rows], product(low[...], rest)).reshape(out.shape)
 
 
 def one_back_kernel(update, rest, low, below, x_out, out):
-    x = product(low[...], rest[...] - joined(update))
+    x = product(low[...], rest[...] - update[...])
     x_out[...] = x
     out[...] = product(below[...], x).reshape(out.shape)
 
@@ -215,7 +205,7 @@
     ny = got.shape[1]
     for y in range(ny):
         for core in range(2):
-            out[2 * y + core] = got[core, y]
+            out[paired(2 * y + core, 2 * ny)] = got[core, y]
 
 
 def last_kernel(table, update, y0, low, x, out):
@@ -267,44 +257,42 @@
     )
     y0 = jnp.dot(up.astype(F32), base, precision=lax.Precision.HIGHEST)
 
-    slices = lax.all_to_all(sent, COL, 0, 0, tiled=True)
+    slices = lax.all_to_all(sent, SLICES, 0, 0, tiled=True)
     table, y0, base, up, low, below, slices = lax.optimization_barrier(
         (table, y0, base, up, low, below, slices)
     )
 
-    def total(line, first, got, shape, start=0, stop=ncol):
-        body = functools.partial(sum_kernel, line, first, start, stop)
+    def total(line, first, got, shape, pairs=True, side=None):
+        body = functools.partial(sum_kernel, line, first, pairs, side)
         return call(body, shape, table, got)
 
-    def whole(half):
-        return lax.all_gather(half, "core", tiled=True).reshape(width, nrhs)
-
-    def spread(copied):
-        return whole(a2a(copied, "y"))
-
-    def spread_halves(copied):
-        both = lax.all_gather(a2a(copied, BESIDE), "core", tiled=True)
-        return both.reshape(ncol // ny, 2, ny, piece // 2, nrhs)
+    def whole(part):
+        return lax.all_gather(part, "core", tiled=True).reshape(width, nrhs)
+
+    def spread(copied, axes):
+        return whole(a2a(copied, axes))
+
+    def from_side(copied, side):
+        return a2a(copied, ACROSS).reshape(ny, 2, piece, nrhs)[:, side]
 
     out, own = call(leaf_kernel, (to_top, shape_of(width, width, kind=BF16)), slices, y0)
-    got = total(FROM_LEAF, 0, a2a(out, HALF), across, start=ny)
-    update = whole(a2a(got, ACROSS)[:ny])
+    got = total(FROM_LEAF, 0, a2a(out, HALF), across, side=1)
+    update = whole(from_side(got, 0))
     rest, out = call(one_kernel, (panel, half_to_top), update, base, up, own)
-    got = total(FROM_ONE, top, a2a(out, HALF), half_to_top, start=ny)
+    got = total(FROM_ONE, top, a2a(out, HALF), half_to_top, side=1)
     rest, out = call(
-        two_kernel, (panel, to_late), spread_halves(got), rest, up, own
-    )
-    got = total(FROM_TWO, late, a2a(out, "z"), copies)
-    y, out = call(three_kernel, (panel, to_late), spread(got), rest, up, low, own)
-    got = total(FROM_THREE, late, a2a(out, "z"), copies)
-    rest, out = call(two_back_kernel, (panel, half_to_top), spread(got), y, low, own)
-    got = total(FROM_ABOVE, top, a2a(out, HALF), half_to_top, stop=ny)
+        two_kernel, (panel, to_late), spread(got, BESIDE), rest, up, own
+    )
+    got = total(FROM_TWO, late, a2a(out, "z"), copies, pairs=False)
+    y, out = call(three_kernel, (panel, to_late), spread(got, "y"), rest, up, low, own)
+    got = total(FROM_THREE, late, a2a(out, "z"), copies, pairs=False)
+    rest, out = call(two_back_kernel, (panel, half_to_top), spread(got, "y"), y, low, own)
+    got = total(FROM_ABOVE, top, a2a(out, HALF), half_to_top, side=0)
     x, out = call(
-        one_back_kernel, (panel, to_top), spread_halves(got), rest, low, below
-    )
-    got = total(TO_COLUMN, top, a2a(out, HALF), across, stop=ny)
-    got = a2a(got, ACROSS)[ny:]
-    got = lax.all_gather(got, "core")
+        one_back_kernel, (panel, to_top), spread(got, BESIDE), rest, low, below
+    )
+    got = total(TO_COLUMN, top, a2a(out, HALF), across, side=0)
+    got = lax.all_gather(from_side(got, 1), "core")
     out = call(order_kernel, to_top, got)
     update = a2a(out, HALF).reshape(width, nrhs)
     return call(

time: 234 us -> 241 us (1.030)
  blocking collectives: 186 us -> 196 us
    all_to_all x13, blocking collectives: 156 us -> 167 us  [a2a(): lax.all_to_all(array, axes, 0, 0, tiled=True)]
where the time goes in v13:
time: 241 us; the launch traced here: 240 us
  blocking collectives  196 us (81%)
  waiting for transfers between devices  21.4 us (9%)
  Pallas kernels  10.9 us (5%)
  starting transfers between devices  10.4 us (4%)
    all_to_all x13, blocking collectives, a2a(): lax.all_to_all(array, axes, 0, 0, tiled=True)  167 us
    all_gather x5, blocking collectives, whole(): return lax.all_gather(part, 'core', tiled=True).reshape(width, nrhs)  23.5 us
    all_to_all x1, waiting for transfers between devices, per_device(): slices = lax.all_to_all(sent, SLICES, 0, 0, tiled=True)  21.4 us
    all_to_all x1, starting transfers between devices, per_device(): slices = lax.all_to_all(sent, SLICES, 0, 0, tiled=True)  10.4 us
    pallas_call x15, Pallas kernels, call(): pl.pallas_call(body, out_shape=shape, in_specs=[SM] * scalars + [VM] * (l...  6.59 us
    all_gather x1, blocking collectives, per_device(): got = lax.all_gather(from_side(got, 1), 'core')  5.07 us
  transfers between devices with their start and end apart: 1, of which 1 were waited for; matrix products, arithmetic and copies ran while one was open for 0% of the time, Pallas kernels for 1%

profile of v13, /device:TPU:1, one launch (start us, length us, event | category | flops | bytes accessed | tf_op | source)
XLA Modules:
  0.0 240.4 jit_solution(9310833394742595537)
XLA Ops:
  0.0 2.2 shard_map.66
  2.2 10.4 %all-to-all-start = ((f32[16,32,512]{2,1,0:T(8,128)}), f32[16,32,512]{2,1,0:T(8,128)S(1)}, u32[]{:S(2)}, u32[]{:S(2)}) async-start(f32[16,32,512]{2,1,0:T(8,128)} %shard_map.66), calls=%async_computation | async-start | bytes 2097152 | tf_op jit(solution)/shard_map/all_to_all | solution.py:260
  12.6 2.2 shard_map.65.below
  14.8 0.6 copy-done.5
  16.1 1.0 shard_map.64.table
  17.2 0.6 fusion.y0
  17.8 21.4 %all-to-all-done.slices = f32[16,32,512]{2,1,0:T(8,128)S(1)} async-done(((f32[16,32,512]{2,1,0:T(8,128)}), f32[16,32,512]{2,1,0:T(8,128)S(1)}, u32[]{:S(2)}, u32[]{:S(2)}) %all-to-all-start) | async-done | bytes 1048608 | tf_op jit(solution)/shard_map/all_to_all | solution.py:260
  39.7 20.7 %all_to_all.70.got = f32[16,32,128]{2,1,0:T(8,128)S(1)} all-to-all(f32[16,32,128]{2,1,0:T(8,128)S(1)} %get-tuple-element.27), channel_id=1, replica_groups=mesh['xh'=2,'xl'=2,'z'=8,'y'=8,'core'=2] {'z','xl'}, dimensions={0} | all-to-all | bytes 524288 | tf_op jit(solution)/shard_map/all_to_all | solution.py:218
  60.4 16.4 %all_to_all.71 = f32[16,32,128]{2,1,0:T(8,128)S(1)} all-to-all(f32[16,32,128]{2,1,0:T(8,128)S(1)} %shard_map.68), channel_id=1, replica_groups=mesh['xh'=2,'xl'=2,'z'=8,'y'=8,'core'=2] {'y','xh'}, dimensions={0} | all-to-all | bytes 524288 | tf_op jit(solution)/shard_map/all_to_all | solution.py:218
  76.8 5.3 %all-gather = f32[16,1,32,128]{3,2,1,0:T(8,128)S(1)} all-gather(f32[8,1,32,128]{3,2,1,0:T(8,128)S(1)} %slice.8), channel_id=2, replica_groups=mesh['xh'=2,'xl'=2,'z'=8,'y'=8,'core'=2] {'core'}, dimensions={0}, use_global_device_ids=true | all-gather | bytes 393216 | tf_op jit(solution)/shard_map/all_gather | solution.py:270
  82.1 0.7 shard_map.69
  82.8 11.4 %all_to_all.72.got = f32[16,16,128]{2,1,0:T(8,128)S(1)} all-to-all(f32[16,16,128]{2,1,0:T(8,128)S(1)} %get-tuple-element.31), channel_id=1, replica_groups=mesh['xh'=2,'xl'=2,'z'=8,'y'=8,'core'=2] {'z','xl'}, dimensions={0} | all-to-all | bytes 262144 | tf_op jit(solution)/shard_map/all_to_all | solution.py:218
  94.2 11.1 %all_to_all.73 = f32[16,16,128]{2,1,0:T(8,128)S(1)} all-to-all(f32[16,16,128]{2,1,0:T(8,128)S(1)} %shard_map.70), channel_id=1, replica_groups=mesh['xh'=2,'xl'=2,'z'=8,'y'=8,'core'=2] {'y','xl'}, dimensions={0} | all-to-all | bytes 262144 | tf_op jit(solution)/shard_map/all_to_all | solution.py:218
  105.3 4.9 %all_gather.19 = f32[32,16,128]{2,1,0:T(8,128)S(1)} all-gather(f32[16,16,128]{2,1,0:T(8,128)S(1)} %all_to_all.73), channel_id=1, replica_groups=mesh['xh'=2,'xl'=2,'z'=8,'y'=8,'core'=2] {'core'}, dimensions={0}, use_global_device_ids=true | all-gather | bytes 393216 | tf_op jit(solution)/shard_map/all_gather | solution.py:270
  110.2 0.7 shard_map.71
  110.9 10.8 %all_to_all.74.got = f32[8,32,128]{2,1,0:T(8,128)S(1)} all-to-all(f32[8,32,128]{2,1,0:T(8,128)S(1)} %get-tuple-element.33), channel_id=1, replica_groups=mesh['xh'=2,'xl'=2,'z'=8,'y'=8,'core'=2] {'z'}, dimensions={0} | all-to-all | bytes 262144 | tf_op jit(solution)/shard_map/all_to_all | solution.py:218
  121.7 10.5 %all_to_all.75 = f32[8,32,128]{2,1,0:T(8,128)S(1)} all-to-all(f32[8,32,128]{2,1,0:T(8,128)S(1)} %shard_map.72), channel_id=1, replica_groups=mesh['xh'=2,'xl'=2,'z'=8,'y'=8,'core'=2] {'y'}, dimensions={0} | all-to-all | bytes 262144 | tf_op jit(solution)/shard_map/all_to_all | solution.py:218
  132.2 4.3 %all_gather.20 = f32[16,32,128]{2,1,0:T(8,128)S(1)} all-gather(f32[8,32,128]{2,1,0:T(8,128)S(1)} %all_to_all.75), channel_id=1, replica_groups=mesh['xh'=2,'xl'=2,'z'=8,'y'=8,'core'=2] {'core'}, dimensions={0}, use_global_device_ids=true | all-gather | bytes 393216 | tf_op jit(solution)/shard_map/all_gather | solution.py:270
  136.5 1.0 shard_map.73
  137.6 10.8 %all_to_all.76.got = f32[8,32,128]{2,1,0:T(8,128)S(1)} all-to-all(f32[8,32,128]{2,1,0:T(8,128)S(1)} %get-tuple-element.36), channel_id=1, replica_groups=mesh['xh'=2,'xl'=2,'z'=8,'y'=8,'core'=2] {'z'}, dimensions={0} | all-to-all | bytes 262144 | tf_op jit(solution)/shard_map/all_to_all | solution.py:218
  148.4 10.3 %all_to_all.77 = f32[8,32,128]{2,1,0:T(8,128)S(1)} all-to-all(f32[8,32,128]{2,1,0:T(8,128)S(1)} %shard_map.74), channel_id=1, replica_groups=mesh['xh'=2,'xl'=2,'z'=8,'y'=8,'core'=2] {'y'}, dimensions={0} | all-to-all | bytes 262144 | tf_op jit(solution)/shard_map/all_to_all | solution.py:218
  158.7 4.3 %all_gather.21 = f32[16,32,128]{2,1,0:T(8,128)S(1)} all-gather(f32[8,32,128]{2,1,0:T(8,128)S(1)} %all_to_all.77), channel_id=1, replica_groups=mesh['xh'=2,'xl'=2,'z'=8,'y'=8,'core'=2] {'core'}, dimensions={0}, use_global_device_ids=true | all-gather | bytes 393216 | tf_op jit(solution)/shard_map/all_gather | solution.py:270
  163.1 0.7 shard_map.75
  163.7 11.4 %all_to_all.78.got = f32[16,16,128]{2,1,0:T(8,128)S(1)} all-to-all(f32[16,16,128]{2,1,0:T(8,128)S(1)} %get-tuple-element.38), channel_id=1, replica_groups=mesh['xh'=2,'xl'=2,'z'=8,'y'=8,'core'=2] {'z','xl'}, dimensions={0} | all-to-all | bytes 262144 | tf_op jit(solution)/shard_map/all_to_all | solution.py:218
  175.2 11.3 %all_to_all.79 = f32[16,16,128]{2,1,0:T(8,128)S(1)} all-to-all(f32[16,16,128]{2,1,0:T(8,128)S(1)} %shard_map.76), channel_id=1, replica_groups=mesh['xh'=2,'xl'=2,'z'=8,'y'=8,'core'=2] {'y','xl'}, dimensions={0} | all-to-all | bytes 262144 | tf_op jit(solution)/shard_map/all_to_all | solution.py:218
  186.5 4.6 %all_gather.22 = f32[32,16,128]{2,1,0:T(8,128)S(1)} all-gather(f32[16,16,128]{2,1,0:T(8,128)S(1)} %all_to_all.79), channel_id=1, replica_groups=mesh['xh'=2,'xl'=2,'z'=8,'y'=8,'core'=2] {'core'}, dimensions={0}, use_global_device_ids=true | all-gather | bytes 393216 | tf_op jit(solution)/shard_map/all_gather | solution.py:270
  191.0 0.8 shard_map.77
  191.8 13.9 %all_to_all.80.got = f32[16,32,128]{2,1,0:T(8,128)S(1)} all-to-all(f32[16,32,128]{2,1,0:T(8,128)S(1)} %get-tuple-element.41), channel_id=1, replica_groups=mesh['xh'=2,'xl'=2,'z'=8,'y'=8,'core'=2] {'z','xl'}, dimensions={0} | all-to-all | bytes 524288 | tf_op jit(solution)/shard_map/all_to_all | solution.py:218
  205.8 13.8 %all_to_all.81 = f32[16,32,128]{2,1,0:T(8,128)S(1)} all-to-all(f32[16,32,128]{2,1,0:T(8,128)S(1)} %shard_map.78), channel_id=1, replica_groups=mesh['xh'=2,'xl'=2,'z'=8,'y'=8,'core'=2] {'y','xh'}, dimensions={0} | all-to-all | bytes 524288 | tf_op jit(solution)/shard_map/all_to_all | solution.py:218
  219.6 5.1 %all-gather.1 = f32[16,1,32,128]{3,2,1,0:T(8,128)S(1)} all-gather(f32[8,1,32,128]{3,2,1,0:T(8,128)S(1)} %slice.9), channel_id=3, replica_groups=mesh['xh'=2,'xl'=2,'z'=8,'y'=8,'core'=2] {'core'}, dimensions={0}, use_global_device_ids=true | all-gather | bytes 393216 | tf_op jit(solution)/shard_map/all_gather | solution.py:295
  224.7 14.5 %all_to_all.82 = f32[16,32,128]{2,1,0:T(8,128)S(1)} all-to-all(f32[16,32,128]{2,1,0:T(8,128)S(1)} %shard_map.79), channel_id=1, replica_groups=mesh['xh'=2,'xl'=2,'z'=8,'y'=8,'core'=2] {'z','xl'}, dimensions={0} | all-to-all | bytes 524288 | tf_op jit(solution)/shard_map/all_to_all | solution.py:218
  239.2 1.2 shard_map.80
  (23 shorter events, 1.4 us)
Async XLA Ops:
  2.2 37.0 %all-to-all-start = ((f32[16,32,512]{2,1,0:T(8,128)}), f32[16,32,512]{2,1,0:T(8,128)S(1)}, u32[]{:S(2)}, u32[]{:S(2)}) async-start(f32[16,32,512]{2,1,0:T(8,128)} %shard_map.66), calls=%async_computation | async-start | bytes 2097152 | tf_op jit(solution)/shard_map/all_to_all | solution.py:260
  12.6 4.6 %copy-start.1 = (bf16[1,1,512,512]{3,2,1,0:T(8,128)(2,1)S(1)}, bf16[1,1,512,512]{3,2,1,0:T(8,128)(2,1)}, u32[]{:S(2)}) copy-start(bf16[1,1,512,512]{3,2,1,0:T(8,128)(2,1)} %param.8) | copy-start | bytes 1572868
  12.6 4.6 %copy-start.3 = (f32[1,1,512,128]{3,2,1,0:T(8,128)S(1)}, f32[1,1,512,128]{3,2,1,0:T(8,128)}, u32[]{:S(2)}) copy-start(f32[1,1,512,128]{3,2,1,0:T(8,128)} %param.7) | copy-start | bytes 786436
  14.8 0.7 copy-start.5
  15.4 0.7 copy-start.4
  121.7 14.8 %copy-start = (bf16[1,1,512,512]{3,2,1,0:T(8,128)(2,1)S(1)}, bf16[1,1,512,512]{3,2,1,0:T(8,128)(2,1)}, u32[]{:S(2)}) copy-start(bf16[1,1,512,512]{3,2,1,0:T(8,128)(2,1)} %param.9) | copy-start | bytes 1572868
  175.2 15.9 %copy-start.2 = (bf16[512,512]{1,0:T(8,128)(2,1)S(1)}, bf16[512,512]{1,0:T(8,128)(2,1)}, u32[]{:S(2)}) copy-start(bf16[512,512]{1,0:T(8,128)(2,1)} %shard_map.65.below) | copy-start | bytes 1572868

commit v14 on v11

--- a/solution.py
+++ b/solution.py
@@ -12,7 +12,7 @@
 ROW = ("xh", "xl", "z")
 COL = ("y", "core")
 ACROSS = ("xh", "y")
-BESIDE = ("xl", "y")
+BESIDE = ("y", "xl")
 F32 = jnp.float32
 BF16 = jnp.bfloat16
 ROOMY = pltpu.CompilerParams(vmem_limit_bytes=40 * 1024 * 1024)
@@ -149,12 +149,12 @@
     out[...] = product(own, y0[...]).reshape(out.shape)
 
 
-def sum_kernel(line, first, start, stop, table, got, out):
+def sum_kernel(line, first, to, table, got, out):
     total = table[line, first:first + 1] * got[0]
     for k in range(1, got.shape[0]):
         total = total + table[line, first + k:first + k + 1] * got[k]
     for k in range(out.shape[0]):
-        out[k] = total if start <= k < stop else jnp.zeros_like(total)
+        out[k] = total if k in to else jnp.zeros_like(total)
 
 
 def halves(out, panel, piece):
@@ -164,19 +164,6 @@
     out[count:] = slices[:, piece // 2:]
 
 
-def joined(update):
-    cores, parts, ny = update.shape[:3]
-    return jnp.concatenate(
-        [
-            update[core, part, y]
-            for core in range(cores)
-            for y in range(ny)
-            for part in range(parts)
-        ],
-        0,
-    )
-
-
 def one_kernel(update, base, up, own, rest_out, out):
     rows = own.shape[0] // 2
     rest = base[...] - update[...]
@@ -186,7 +173,7 @@
 
 def two_kernel(update, rest_in, up, own, rest_out, out):
     rows = own.shape[0] // 2
-    rest = rest_in[...] - joined(update)
+    rest = rest_in[...] - update[...]
     rest_out[...] = rest
     out[...] = product(own[rows:], product(up[...], rest)).reshape(out.shape)
 
@@ -206,7 +193,7 @@
 
 
 def one_back_kernel(update, rest, low, below, x_out, out):
-    x = product(low[...], rest[...] - joined(update))
+    x = product(low[...], rest[...] - update[...])
     x_out[...] = x
     out[...] = product(below[...], x).reshape(out.shape)
 
@@ -272,8 +259,8 @@
         (table, y0, base, up, low, below, slices)
     )
 
-    def total(line, first, got, shape, start=0, stop=ncol):
-        body = functools.partial(sum_kernel, line, first, start, stop)
+    def total(line, first, got, shape, to):
+        body = functools.partial(sum_kernel, line, first, to)
         return call(body, shape, table, got)
 
     def whole(half):
@@ -283,26 +270,25 @@
         return whole(a2a(copied, "y"))
 
     def spread_halves(copied):
-        both = lax.all_gather(a2a(copied, BESIDE), "core", tiled=True)
-        return both.reshape(ncol // ny, 2, ny, piece // 2, nrhs)
+        return whole(a2a(copied, BESIDE))
 
     out, own = call(leaf_kernel, (to_top, shape_of(width, width, kind=BF16)), slices, y0)
-    got = total(FROM_LEAF, 0, a2a(out, HALF), across, start=ny)
+    got = total(FROM_LEAF, 0, a2a(out, HALF), across, range(ny, ncol))
     update = whole(a2a(got, ACROSS)[:ny])
     rest, out = call(one_kernel, (panel, half_to_top), update, base, up, own)
-    got = total(FROM_ONE, top, a2a(out, HALF), half_to_top, start=ny)
+    got = total(FROM_ONE, top, a2a(out, HALF), half_to_top, range(1, ncol, 2))
     rest, out = call(
         two_kernel, (panel, to_late), spread_halves(got), rest, up, own
     )
-    got = total(FROM_TWO, late, a2a(out, "z"), copies)
+    got = total(FROM_TWO, late, a2a(out, "z"), copies, range(ny))
     y, out = call(three_kernel, (panel, to_late), spread(got), rest, up, low, own)
-    got = total(FROM_THREE, late, a2a(out, "z"), copies)
+    got = total(FROM_THREE, late, a2a(out, "z"), copies, range(ny))
     rest, out = call(two_back_kernel, (panel, half_to_top), spread(got), y, low, own)
-    got = total(FROM_ABOVE, top, a2a(out, HALF), half_to_top, stop=ny)
+    got = total(FROM_ABOVE, top, a2a(out, HALF), half_to_top, range(0, ncol, 2))
     x, out = call(
         one_back_kernel, (panel, to_top), spread_halves(got), rest, low, below
     )
-    got = total(TO_COLUMN, top, a2a(out, HALF), across, stop=ny)
+    got = total(TO_COLUMN, top, a2a(out, HALF), across, range(ny))
     got = a2a(got, ACROSS)[ny:]
     got = lax.all_gather(got, "core")
     out = call(order_kernel, to_top, got)

time: 234 us -> 235 us (level)
    all_gather x2 -> x0, blocking collectives: 9.44 us -> none  [spread_halves(): both = lax.all_gather(a2a(copied, BESIDE), 'core', tiled=True)]
    all_gather x3 -> x5, blocking collectives: 14.4 us -> 23.5 us  [whole(): return lax.all_gather(half, 'core', tiled=True).reshape(width, nrhs)]
where the time goes in v14:
time: 235 us; the launch traced here: 233 us
  blocking collectives  187 us (80%)
  waiting for transfers between devices  22.7 us (10%)
  Pallas kernels  10.9 us (5%)
  starting transfers between devices  10.3 us (4%)
    all_to_all x13, blocking collectives, a2a(): lax.all_to_all(array, axes, 0, 0, tiled=True)  158 us
    all_gather x5, blocking collectives, whole(): return lax.all_gather(half, 'core', tiled=True).reshape(width, nrhs)  23.5 us
    all_to_all x1, waiting for transfers between devices, per_device(): slices = lax.all_to_all(sent, COL, 0, 0, tiled=True)  22.7 us
    all_to_all x1, starting transfers between devices, per_device(): slices = lax.all_to_all(sent, COL, 0, 0, tiled=True)  10.3 us
    pallas_call x15, Pallas kernels, call(): pl.pallas_call(body, out_shape=shape, in_specs=[SM] * scalars + [VM] * (l...  6.58 us
    all_gather x1, blocking collectives, per_device(): got = lax.all_gather(got, 'core')  5.14 us
  transfers between devices with their start and end apart: 1, of which 1 were waited for; matrix products, arithmetic and copies ran while one was open for 0% of the time, Pallas kernels for 1%

profile of v14, /device:TPU:1, one launch (start us, length us, event | category | flops | bytes accessed | tf_op | source)
XLA Modules:
  0.0 233.2 jit_solution(18225225019405532234)
XLA Ops:
  0.0 2.2 shard_map.66
  2.2 10.3 %all-to-all-start = ((f32[16,32,512]{2,1,0:T(8,128)}), f32[16,32,512]{2,1,0:T(8,128)S(1)}, u32[]{:S(2)}, u32[]{:S(2)}) async-start(f32[16,32,512]{2,1,0:T(8,128)} %shard_map.66), calls=%async_computation | async-start | bytes 2097152 | tf_op jit(solution)/shard_map/all_to_all | solution.py:257
  12.5 2.2 shard_map.65.below
  14.7 0.6 copy-done.5
  16.1 1.0 shard_map.64.table
  17.2 0.6 fusion.y0
  17.8 22.7 %all-to-all-done.slices = f32[16,32,512]{2,1,0:T(8,128)S(1)} async-done(((f32[16,32,512]{2,1,0:T(8,128)}), f32[16,32,512]{2,1,0:T(8,128)S(1)}, u32[]{:S(2)}, u32[]{:S(2)}) %all-to-all-start) | async-done | bytes 1048608 | tf_op jit(solution)/shard_map/all_to_all | solution.py:257
  41.0 19.0 %all_to_all.70.got = f32[16,32,128]{2,1,0:T(8,128)S(1)} all-to-all(f32[16,32,128]{2,1,0:T(8,128)S(1)} %get-tuple-element.27), channel_id=1, replica_groups=mesh['xh'=2,'xl'=2,'z'=8,'y'=8,'core'=2] {'xl','z'}, dimensions={0} | all-to-all | bytes 524288 | tf_op jit(solution)/shard_map/all_to_all | solution.py:215
  60.0 13.5 %all_to_all.71 = f32[16,32,128]{2,1,0:T(8,128)S(1)} all-to-all(f32[16,32,128]{2,1,0:T(8,128)S(1)} %shard_map.68), channel_id=1, replica_groups=mesh['xh'=2,'xl'=2,'z'=8,'y'=8,'core'=2] {'xh','y'}, dimensions={0} | all-to-all | bytes 524288 | tf_op jit(solution)/shard_map/all_to_all | solution.py:215
  73.5 5.1 %all_gather.21 = f32[16,32,128]{2,1,0:T(8,128)S(1)} all-gather(f32[8,32,128]{2,1,0:T(8,128)S(1)} %slice.8), channel_id=1, replica_groups=mesh['xh'=2,'xl'=2,'z'=8,'y'=8,'core'=2] {'core'}, dimensions={0}, use_global_device_ids=true | all-gather | bytes 393216 | tf_op jit(solution)/shard_map/all_gather | solution.py:267
  78.6 0.7 shard_map.69
  79.2 11.6 %all_to_all.72.got = f32[16,16,128]{2,1,0:T(8,128)S(1)} all-to-all(f32[16,16,128]{2,1,0:T(8,128)S(1)} %get-tuple-element.31), channel_id=1, replica_groups=mesh['xh'=2,'xl'=2,'z'=8,'y'=8,'core'=2] {'xl','z'}, dimensions={0} | all-to-all | bytes 262144 | tf_op jit(solution)/shard_map/all_to_all | solution.py:215
  90.9 12.9 %all_to_all.73 = f32[16,16,128]{2,1,0:T(8,128)S(1)} all-to-all(f32[16,16,128]{2,1,0:T(8,128)S(1)} %shard_map.70), channel_id=1, replica_groups=mesh['xh'=2,'xl'=2,'z'=8,'y'=8,'core'=2] {'y','xl'}, dimensions={0} | all-to-all | bytes 262144 | tf_op jit(solution)/shard_map/all_to_all | solution.py:215
  103.7 5.0 %all_gather.22 = f32[32,16,128]{2,1,0:T(8,128)S(1)} all-gather(f32[16,16,128]{2,1,0:T(8,128)S(1)} %all_to_all.73), channel_id=1, replica_groups=mesh['xh'=2,'xl'=2,'z'=8,'y'=8,'core'=2] {'core'}, dimensions={0}, use_global_device_ids=true | all-gather | bytes 393216 | tf_op jit(solution)/shard_map/all_gather | solution.py:267
  108.8 0.7 shard_map.71
  109.4 10.3 %all_to_all.74.got = f32[8,32,128]{2,1,0:T(8,128)S(1)} all-to-all(f32[8,32,128]{2,1,0:T(8,128)S(1)} %get-tuple-element.33), channel_id=1, replica_groups=mesh['xh'=2,'xl'=2,'z'=8,'y'=8,'core'=2] {'z'}, dimensions={0} | all-to-all | bytes 262144 | tf_op jit(solution)/shard_map/all_to_all | solution.py:215
  119.8 10.5 %all_to_all.75 = f32[8,32,128]{2,1,0:T(8,128)S(1)} all-to-all(f32[8,32,128]{2,1,0:T(8,128)S(1)} %shard_map.72), channel_id=1, replica_groups=mesh['xh'=2,'xl'=2,'z'=8,'y'=8,'core'=2] {'y'}, dimensions={0} | all-to-all | bytes 262144 | tf_op jit(solution)/shard_map/all_to_all | solution.py:215
  130.3 4.8 %all_gather.23 = f32[16,32,128]{2,1,0:T(8,128)S(1)} all-gather(f32[8,32,128]{2,1,0:T(8,128)S(1)} %all_to_all.75), channel_id=1, replica_groups=mesh['xh'=2,'xl'=2,'z'=8,'y'=8,'core'=2] {'core'}, dimensions={0}, use_global_device_ids=true | all-gather | bytes 393216 | tf_op jit(solution)/shard_map/all_gather | solution.py:267
  135.1 1.0 shard_map.73
  136.1 10.8 %all_to_all.76.got = f32[8,32,128]{2,1,0:T(8,128)S(1)} all-to-all(f32[8,32,128]{2,1,0:T(8,128)S(1)} %get-tuple-element.36), channel_id=1, replica_groups=mesh['xh'=2,'xl'=2,'z'=8,'y'=8,'core'=2] {'z'}, dimensions={0} | all-to-all | bytes 262144 | tf_op jit(solution)/shard_map/all_to_all | solution.py:215
  146.9 10.3 %all_to_all.77 = f32[8,32,128]{2,1,0:T(8,128)S(1)} all-to-all(f32[8,32,128]{2,1,0:T(8,128)S(1)} %shard_map.74), channel_id=1, replica_groups=mesh['xh'=2,'xl'=2,'z'=8,'y'=8,'core'=2] {'y'}, dimensions={0} | all-to-all | bytes 262144 | tf_op jit(solution)/shard_map/all_to_all | solution.py:215
  157.3 4.3 %all_gather.24 = f32[16,32,128]{2,1,0:T(8,128)S(1)} all-gather(f32[8,32,128]{2,1,0:T(8,128)S(1)} %all_to_all.77), channel_id=1, replica_groups=mesh['xh'=2,'xl'=2,'z'=8,'y'=8,'core'=2] {'core'}, dimensions={0}, use_global_device_ids=true | all-gather | bytes 393216 | tf_op jit(solution)/shard_map/all_gather | solution.py:267
  161.6 0.7 shard_map.75
  162.3 10.1 %all_to_all.78.got = f32[16,16,128]{2,1,0:T(8,128)S(1)} all-to-all(f32[16,16,128]{2,1,0:T(8,128)S(1)} %get-tuple-element.38), channel_id=1, replica_groups=mesh['xh'=2,'xl'=2,'z'=8,'y'=8,'core'=2] {'xl','z'}, dimensions={0} | all-to-all | bytes 262144 | tf_op jit(solution)/shard_map/all_to_all | solution.py:215
  172.4 11.3 %all_to_all.79 = f32[16,16,128]{2,1,0:T(8,128)S(1)} all-to-all(f32[16,16,128]{2,1,0:T(8,128)S(1)} %shard_map.76), channel_id=1, replica_groups=mesh['xh'=2,'xl'=2,'z'=8,'y'=8,'core'=2] {'y','xl'}, dimensions={0} | all-to-all | bytes 262144 | tf_op jit(solution)/shard_map/all_to_all | solution.py:215
  183.7 4.3 %all_gather.25 = f32[32,16,128]{2,1,0:T(8,128)S(1)} all-gather(f32[16,16,128]{2,1,0:T(8,128)S(1)} %all_to_all.79), channel_id=1, replica_groups=mesh['xh'=2,'xl'=2,'z'=8,'y'=8,'core'=2] {'core'}, dimensions={0}, use_global_device_ids=true | all-gather | bytes 393216 | tf_op jit(solution)/shard_map/all_gather | solution.py:267
  188.0 0.8 shard_map.77
  188.8 12.2 %all_to_all.80.got = f32[16,32,128]{2,1,0:T(8,128)S(1)} all-to-all(f32[16,32,128]{2,1,0:T(8,128)S(1)} %get-tuple-element.41), channel_id=1, replica_groups=mesh['xh'=2,'xl'=2,'z'=8,'y'=8,'core'=2] {'xl','z'}, dimensions={0} | all-to-all | bytes 524288 | tf_op jit(solution)/shard_map/all_to_all | solution.py:215
  201.0 11.9 %all_to_all.81 = f32[16,32,128]{2,1,0:T(8,128)S(1)} all-to-all(f32[16,32,128]{2,1,0:T(8,128)S(1)} %shard_map.78), channel_id=1, replica_groups=mesh['xh'=2,'xl'=2,'z'=8,'y'=8,'core'=2] {'xh','y'}, dimensions={0} | all-to-all | bytes 524288 | tf_op jit(solution)/shard_map/all_to_all | solution.py:215
  212.9 5.1 %all-gather = f32[16,32,128]{2,1,0:T(8,128)S(1)} all-gather(f32[8,32,128]{2,1,0:T(8,128)S(1)} %slice.9), channel_id=2, replica_groups=mesh['xh'=2,'xl'=2,'z'=8,'y'=8,'core'=2] {'core'}, dimensions={0}, use_global_device_ids=true | all-gather | bytes 393216 | tf_op jit(solution)/shard_map/all_gather | solution.py:293
  218.0 14.0 %all_to_all.82 = f32[16,32,128]{2,1,0:T(8,128)S(1)} all-to-all(f32[16,32,128]{2,1,0:T(8,128)S(1)} %shard_map.79), channel_id=1, replica_groups=mesh['xh'=2,'xl'=2,'z'=8,'y'=8,'core'=2] {'xl','z'}, dimensions={0} | all-to-all | bytes 524288 | tf_op jit(solution)/shard_map/all_to_all | solution.py:215
  232.0 1.2 shard_map.80
  (23 shorter events, 1.4 us)
Async XLA Ops:
  2.2 38.3 %all-to-all-start = ((f32[16,32,512]{2,1,0:T(8,128)}), f32[16,32,512]{2,1,0:T(8,128)S(1)}, u32[]{:S(2)}, u32[]{:S(2)}) async-start(f32[16,32,512]{2,1,0:T(8,128)} %shard_map.66), calls=%async_computation | async-start | bytes 2097152 | tf_op jit(solution)/shard_map/all_to_all | solution.py:257
  12.5 4.6 %copy-start.1 = (bf16[1,1,512,512]{3,2,1,0:T(8,128)(2,1)S(1)}, bf16[1,1,512,512]{3,2,1,0:T(8,128)(2,1)}, u32[]{:S(2)}) copy-start(bf16[1,1,512,512]{3,2,1,0:T(8,128)(2,1)} %param.8) | copy-start | bytes 1572868
  12.5 4.6 %copy-start.3 = (f32[1,1,512,128]{3,2,1,0:T(8,128)S(1)}, f32[1,1,512,128]{3,2,1,0:T(8,128)}, u32[]{:S(2)}) copy-start(f32[1,1,512,128]{3,2,1,0:T(8,128)} %param.7) | copy-start | bytes 786436
  14.7 0.7 copy-start.5
  15.4 0.7 copy-start.4
  119.7 15.4 %copy-start = (bf16[1,1,512,512]{3,2,1,0:T(8,128)(2,1)S(1)}, bf16[1,1,512,512]{3,2,1,0:T(8,128)(2,1)}, u32[]{:S(2)}) copy-start(bf16[1,1,512,512]{3,2,1,0:T(8,128)(2,1)} %param.9) | copy-start | bytes 1572868
  172.4 15.6 %copy-start.2 = (bf16[512,512]{1,0:T(8,128)(2,1)S(1)}, bf16[512,512]{1,0:T(8,128)(2,1)}, u32[]{:S(2)}) copy-start(bf16[512,512]{1,0:T(8,128)(2,1)} %shard_map.65.below) | copy-start | bytes 1572868

commit v15 on v11

--- a/solution.py
+++ b/solution.py
@@ -267,10 +267,10 @@
     )
     y0 = jnp.dot(up.astype(F32), base, precision=lax.Precision.HIGHEST)
 
-    slices = lax.all_to_all(sent, COL, 0, 0, tiled=True)
-    table, y0, base, up, low, below, slices = lax.optimization_barrier(
-        (table, y0, base, up, low, below, slices)
-    )
+    table, y0, base, up, low, below, sent = lax.optimization_barrier(
+        (table, y0, base, up, low, below, sent)
+    )
+    slices = a2a(sent, COL)
 
     def total(line, first, got, shape, start=0, stop=ncol):
         body = functools.partial(sum_kernel, line, first, start, stop)

time: 234 us -> 238 us (1.017)
  blocking collectives: 186 us -> 224 us
  waiting for transfers between devices: 22.7 us -> 0 us
  starting transfers between devices: 10.3 us -> 0 us
    all_to_all x13 -> x14, blocking collectives: 156 us -> 195 us  [a2a(): lax.all_to_all(array, axes, 0, 0, tiled=True)]
    all_to_all x1 -> x0, waiting for transfers between devices: 22.7 us -> none  [per_device(): slices = lax.all_to_all(sent, COL, 0, 0, tiled=True)]
    all_to_all x1 -> x0, starting transfers between devices: 10.3 us -> none  [per_device(): slices = lax.all_to_all(sent, COL, 0, 0, tiled=True)]
  transfers between devices with their start and end apart: 1 -> 0, of which waited for: 1 -> 0; matrix products, arithmetic and copies ran while one was open for 0% -> 0% of each run, Pallas kernels for 1% -> 0%
where the time goes in v15:
time: 238 us; the launch traced here: 236 us
  blocking collectives  224 us (94%)
  Pallas kernels  10.9 us (5%)
    all_to_all x14, blocking collectives, a2a(): lax.all_to_all(array, axes, 0, 0, tiled=True)  195 us
    all_gather x3, blocking collectives, whole(): return lax.all_gather(half, 'core', tiled=True).reshape(width, nrhs)  14.4 us
    all_gather x2, blocking collectives, spread_halves(): both = lax.all_gather(a2a(copied, BESIDE), 'core', tiled=True)  9.44 us
    pallas_call x15, Pallas kernels, call(): pl.pallas_call(body, out_shape=shape, in_specs=[SM] * scalars + [VM] * (l...  6.6 us
    all_gather x1, blocking collectives, per_device(): got = lax.all_gather(got, 'core')  5.25 us

profile of v15, /device:TPU:1, one launch (start us, length us, event | category | flops | bytes accessed | tf_op | source)
XLA Modules:
  0.0 236.3 jit_solution(7460422814432648820)
XLA Ops:
  0.0 2.1 shard_map.65.below
  2.1 2.3 shard_map.66
  4.4 0.6 copy-done.5
  5.2 0.6 fusion.y0
  5.9 1.0 shard_map.64.table
  7.0 37.9 %all_to_all.70.slices = f32[16,32,512]{2,1,0:T(8,128)S(1)} all-to-all(f32[16,32,512]{2,1,0:T(8,128)S(1)} %copy-done.6), channel_id=1, replica_groups=mesh['xh'=2,'xl'=2,'z'=8,'y'=8,'core'=2] {'y','core'}, dimensions={0} | all-to-all | bytes 2097152 | tf_op jit(solution)/shard_map/all_to_all | solution.py:228
  44.9 0.4 shard_map.67
  45.4 19.8 %all_to_all.71.got = f32[16,32,128]{2,1,0:T(8,128)S(1)} all-to-all(f32[16,32,128]{2,1,0:T(8,128)S(1)} %get-tuple-element.27), channel_id=1, replica_groups=mesh['xh'=2,'xl'=2,'z'=8,'y'=8,'core'=2] {'xl','z'}, dimensions={0} | all-to-all | bytes 524288 | tf_op jit(solution)/shard_map/all_to_all | solution.py:228
  65.2 12.9 %all_to_all.72 = f32[16,32,128]{2,1,0:T(8,128)S(1)} all-to-all(f32[16,32,128]{2,1,0:T(8,128)S(1)} %shard_map.68), channel_id=1, replica_groups=mesh['xh'=2,'xl'=2,'z'=8,'y'=8,'core'=2] {'xh','y'}, dimensions={0} | all-to-all | bytes 524288 | tf_op jit(solution)/shard_map/all_to_all | solution.py:228
  78.1 5.1 %all_gather.21 = f32[16,32,128]{2,1,0:T(8,128)S(1)} all-gather(f32[8,32,128]{2,1,0:T(8,128)S(1)} %slice.8), channel_id=1, replica_groups=mesh['xh'=2,'xl'=2,'z'=8,'y'=8,'core'=2] {'core'}, dimensions={0}, use_global_device_ids=true | all-gather | bytes 393216 | tf_op jit(solution)/shard_map/all_gather | solution.py:280
  83.2 0.7 shard_map.69
  83.8 11.6 %all_to_all.73.got = f32[16,16,128]{2,1,0:T(8,128)S(1)} all-to-all(f32[16,16,128]{2,1,0:T(8,128)S(1)} %get-tuple-element.31), channel_id=1, replica_groups=mesh['xh'=2,'xl'=2,'z'=8,'y'=8,'core'=2] {'xl','z'}, dimensions={0} | all-to-all | bytes 262144 | tf_op jit(solution)/shard_map/all_to_all | solution.py:228
  95.5 11.7 %all_to_all.74 = f32[16,16,128]{2,1,0:T(8,128)S(1)} all-to-all(f32[16,16,128]{2,1,0:T(8,128)S(1)} %shard_map.70), channel_id=1, replica_groups=mesh['xh'=2,'xl'=2,'z'=8,'y'=8,'core'=2] {'xl','y'}, dimensions={0} | all-to-all | bytes 262144 | tf_op jit(solution)/shard_map/all_to_all | solution.py:228
  107.2 5.1 %all_gather.22 = f32[32,16,128]{2,1,0:T(8,128)S(1)} all-gather(f32[16,16,128]{2,1,0:T(8,128)S(1)} %all_to_all.74), channel_id=1, replica_groups=mesh['xh'=2,'xl'=2,'z'=8,'y'=8,'core'=2] {'core'}, dimensions={0}, use_global_device_ids=true | all-gather | bytes 393216 | tf_op jit(solution)/shard_map/all_gather | solution.py:286
  112.3 0.7 shard_map.71
  113.0 10.4 %all_to_all.75.got = f32[8,32,128]{2,1,0:T(8,128)S(1)} all-to-all(f32[8,32,128]{2,1,0:T(8,128)S(1)} %get-tuple-element.33), channel_id=1, replica_groups=mesh['xh'=2,'xl'=2,'z'=8,'y'=8,'core'=2] {'z'}, dimensions={0} | all-to-all | bytes 262144 | tf_op jit(solution)/shard_map/all_to_all | solution.py:228
  123.4 10.8 %all_to_all.76 = f32[8,32,128]{2,1,0:T(8,128)S(1)} all-to-all(f32[8,32,128]{2,1,0:T(8,128)S(1)} %shard_map.72), channel_id=1, replica_groups=mesh['xh'=2,'xl'=2,'z'=8,'y'=8,'core'=2] {'y'}, dimensions={0} | all-to-all | bytes 262144 | tf_op jit(solution)/shard_map/all_to_all | solution.py:228
  134.1 4.9 %all_gather.23 = f32[16,32,128]{2,1,0:T(8,128)S(1)} all-gather(f32[8,32,128]{2,1,0:T(8,128)S(1)} %all_to_all.76), channel_id=1, replica_groups=mesh['xh'=2,'xl'=2,'z'=8,'y'=8,'core'=2] {'core'}, dimensions={0}, use_global_device_ids=true | all-gather | bytes 393216 | tf_op jit(solution)/shard_map/all_gather | solution.py:280
  139.1 1.0 shard_map.73
  140.1 10.8 %all_to_all.77.got = f32[8,32,128]{2,1,0:T(8,128)S(1)} all-to-all(f32[8,32,128]{2,1,0:T(8,128)S(1)} %get-tuple-element.36), channel_id=1, replica_groups=mesh['xh'=2,'xl'=2,'z'=8,'y'=8,'core'=2] {'z'}, dimensions={0} | all-to-all | bytes 262144 | tf_op jit(solution)/shard_map/all_to_all | solution.py:228
  150.9 10.3 %all_to_all.78 = f32[8,32,128]{2,1,0:T(8,128)S(1)} all-to-all(f32[8,32,128]{2,1,0:T(8,128)S(1)} %shard_map.74), channel_id=1, replica_groups=mesh['xh'=2,'xl'=2,'z'=8,'y'=8,'core'=2] {'y'}, dimensions={0} | all-to-all | bytes 262144 | tf_op jit(solution)/shard_map/all_to_all | solution.py:228
  161.3 4.3 %all_gather.24 = f32[16,32,128]{2,1,0:T(8,128)S(1)} all-gather(f32[8,32,128]{2,1,0:T(8,128)S(1)} %all_to_all.78), channel_id=1, replica_groups=mesh['xh'=2,'xl'=2,'z'=8,'y'=8,'core'=2] {'core'}, dimensions={0}, use_global_device_ids=true | all-gather | bytes 393216 | tf_op jit(solution)/shard_map/all_gather | solution.py:280
  165.6 0.7 shard_map.75
  166.3 10.1 %all_to_all.79.got = f32[16,16,128]{2,1,0:T(8,128)S(1)} all-to-all(f32[16,16,128]{2,1,0:T(8,128)S(1)} %get-tuple-element.38), channel_id=1, replica_groups=mesh['xh'=2,'xl'=2,'z'=8,'y'=8,'core'=2] {'xl','z'}, dimensions={0} | all-to-all | bytes 262144 | tf_op jit(solution)/shard_map/all_to_all | solution.py:228
  176.4 10.1 %all_to_all.80 = f32[16,16,128]{2,1,0:T(8,128)S(1)} all-to-all(f32[16,16,128]{2,1,0:T(8,128)S(1)} %shard_map.76), channel_id=1, replica_groups=mesh['xh'=2,'xl'=2,'z'=8,'y'=8,'core'=2] {'xl','y'}, dimensions={0} | all-to-all | bytes 262144 | tf_op jit(solution)/shard_map/all_to_all | solution.py:228
  186.5 4.3 %all_gather.25 = f32[32,16,128]{2,1,0:T(8,128)S(1)} all-gather(f32[16,16,128]{2,1,0:T(8,128)S(1)} %all_to_all.80), channel_id=1, replica_groups=mesh['xh'=2,'xl'=2,'z'=8,'y'=8,'core'=2] {'core'}, dimensions={0}, use_global_device_ids=true | all-gather | bytes 393216 | tf_op jit(solution)/shard_map/all_gather | solution.py:286
  190.8 0.8 shard_map.77
  191.6 12.5 %all_to_all.81.got = f32[16,32,128]{2,1,0:T(8,128)S(1)} all-to-all(f32[16,32,128]{2,1,0:T(8,128)S(1)} %get-tuple-element.41), channel_id=1, replica_groups=mesh['xh'=2,'xl'=2,'z'=8,'y'=8,'core'=2] {'xl','z'}, dimensions={0} | all-to-all | bytes 524288 | tf_op jit(solution)/shard_map/all_to_all | solution.py:228
  204.2 12.5 %all_to_all.82 = f32[16,32,128]{2,1,0:T(8,128)S(1)} all-to-all(f32[16,32,128]{2,1,0:T(8,128)S(1)} %shard_map.78), channel_id=1, replica_groups=mesh['xh'=2,'xl'=2,'z'=8,'y'=8,'core'=2] {'xh','y'}, dimensions={0} | all-to-all | bytes 524288 | tf_op jit(solution)/shard_map/all_to_all | solution.py:228
  216.7 5.3 %all-gather = f32[16,32,128]{2,1,0:T(8,128)S(1)} all-gather(f32[8,32,128]{2,1,0:T(8,128)S(1)} %slice.9), channel_id=2, replica_groups=mesh['xh'=2,'xl'=2,'z'=8,'y'=8,'core'=2] {'core'}, dimensions={0}, use_global_device_ids=true | all-gather | bytes 393216 | tf_op jit(solution)/shard_map/all_gather | solution.py:307
  221.9 13.2 %all_to_all.83 = f32[16,32,128]{2,1,0:T(8,128)S(1)} all-to-all(f32[16,32,128]{2,1,0:T(8,128)S(1)} %shard_map.79), channel_id=1, replica_groups=mesh['xh'=2,'xl'=2,'z'=8,'y'=8,'core'=2] {'xl','z'}, dimensions={0} | all-to-all | bytes 524288 | tf_op jit(solution)/shard_map/all_to_all | solution.py:228
  235.1 1.2 shard_map.80
  (24 shorter events, 0.5 us)
Async XLA Ops:
  2.1 3.1 %copy-start.1 = (bf16[1,1,512,512]{3,2,1,0:T(8,128)(2,1)S(1)}, bf16[1,1,512,512]{3,2,1,0:T(8,128)(2,1)}, u32[]{:S(2)}) copy-start(bf16[1,1,512,512]{3,2,1,0:T(8,128)(2,1)} %param.8) | copy-start | bytes 1572868
  2.1 3.1 %copy-start.3 = (f32[1,1,512,128]{3,2,1,0:T(8,128)S(1)}, f32[1,1,512,128]{3,2,1,0:T(8,128)}, u32[]{:S(2)}) copy-start(f32[1,1,512,128]{3,2,1,0:T(8,128)} %param.7) | copy-start | bytes 786436
  4.4 0.7 copy-start.5
  4.4 2.6 %copy-start.6 = (f32[16,32,512]{2,1,0:T(8,128)S(1)}, f32[16,32,512]{2,1,0:T(8,128)}, u32[]{:S(2)}) copy-start(f32[16,32,512]{2,1,0:T(8,128)} %shard_map.66) | copy-start | bytes 3145732
  5.2 0.7 copy-start.4
  123.3 15.7 %copy-start = (bf16[1,1,512,512]{3,2,1,0:T(8,128)(2,1)S(1)}, bf16[1,1,512,512]{3,2,1,0:T(8,128)(2,1)}, u32[]{:S(2)}) copy-start(bf16[1,1,512,512]{3,2,1,0:T(8,128)(2,1)} %param.9) | copy-start | bytes 1572868
  176.4 14.5 %copy-start.2 = (bf16[512,512]{1,0:T(8,128)(2,1)S(1)}, bf16[512,512]{1,0:T(8,128)(2,1)}, u32[]{:S(2)}) copy-start(bf16[512,512]{1,0:T(8,128)(2,1)} %shard_map.65.below) | copy-start | bytes 1572868
